TPU v7x, 128 devices: a whole 4x4x4 slice. The times are simulated.
128 devices in a mesh: row: 16 (over y_hi, x, core), ad: 8 (over z, y_lo).
Axes of the slice: x: 4, y: 4 (y_hi: 2, y_lo: 2; y = y_hi * 2 + y_lo), z: 4, core: 2. Of those that a mesh axis runs over, the one named last changes fastest.
Arguments:
- tokens: bfloat16 [2048, 8192], P('ad', 'row'), may hold values from -6 to 6
- token_adapter: int32 [2048], P('ad'), may hold values from 0 to 31, as said below
- base_weight: bfloat16 [8192, 16384], P(None, 'row'), may hold values from -1.5 to 1.5
- panel_down: bfloat16 [32, 8192, 64], P(None, ('row', 'ad')), may hold values from -0.5 to 0.5
- panel_up: bfloat16 [32, 64, 16384], P('ad', None, 'row'), may hold values from -0.8984375 to 0.8984375
- magnitude: float32 [32, 16384], P('ad', 'row'), may hold values from 0.5 to 2
Outputs:
- adapted: bfloat16 [2048, 16384], P('ad', 'row')
Inputs may be any that keep to these rules, and one draw needn't show every extreme that they name: `token_adapter`: the tokens of the g-th block of 256 tokens name adapters g * 4 to (g + 1) * 4 - 1, never falling within a block.
All inputs are finite; a program needn't handle non-finite values.
Results may differ from a plain program's by a relative error of at most 0.0028.
Values may be sent and summed in bfloat16 or wider, within the bound.
No kernel may reach another device: no remote copies, remote signals or barrier semaphores. Data moves between devices by JAX's collectives and lax.ppermute only.
A program may use at most 128 MiB of HBM per device.

v0:
```python
import math

import jax
import jax.numpy as jnp
from jax import lax
from jax.sharding import PartitionSpec as P


def on_device(tokens, token_adapter, base_weight, panel_down, panel_up, magnitude):
    tok_rows = tokens.shape[0]
    groups_here = panel_up.shape[0]
    rank_width = panel_up.shape[1]
    col_count = base_weight.shape[1]
    owned_panels = lax.all_to_all(panel_down, "ad", split_axis=0, concat_axis=1, tiled=True)
    first_adapter = lax.axis_index("ad") * groups_here
    local_ids = token_adapter - first_adapter
    slot_iota = lax.broadcasted_iota(jnp.int32, (tok_rows, groups_here), 1)
    pick_table = (local_ids[:, None] == slot_iota).astype(jnp.float32)
    spread = jnp.einsum("tk,akr->tar", tokens, owned_panels, preferred_element_type=jnp.float32)
    low_part = jnp.einsum("ta,tar->tr", pick_table, spread, precision=lax.Precision.HIGHEST)
    low_sum = lax.psum(low_part, "row")
    weight_rows = base_weight
    base_term = jnp.dot(
        lax.all_gather(tokens, "row", axis=1, tiled=True),
        weight_rows,
        preferred_element_type=jnp.float32,
    )
    empty_norms = jnp.zeros((groups_here, col_count), jnp.float32)
    running = empty_norms
    shard_piece = lax.all_gather(owned_panels, "row", axis=1, tiled=True)
    row_count = shard_piece.shape[1]
    block_rows = math.gcd(row_count, 512)
    for offset in range(0, row_count, block_rows):
        weight_rows = lax.dynamic_slice_in_dim(base_weight, offset, block_rows, 0).astype(
            jnp.float32
        )
        corrected = jnp.einsum(
            "akr,arf->akf",
            shard_piece[:, offset : offset + block_rows],
            panel_up,
            preferred_element_type=jnp.float32,
        )
        tile_vals = weight_rows[None, :, :] + corrected
        running = running + jnp.sum(tile_vals * tile_vals, axis=1)
    low_round = low_sum.astype(jnp.bfloat16)
    spread_low = (pick_table.astype(jnp.bfloat16)[:, :, None] * low_round[:, None, :]).reshape(
        tok_rows, groups_here * rank_width
    )
    delta_term = jnp.dot(
        spread_low,
        panel_up.reshape(groups_here * rank_width, col_count),
        preferred_element_type=jnp.float32,
    )
    scale_table = magnitude / jnp.sqrt(running + 1e-06)
    tok_scale = jnp.dot(pick_table, scale_table, precision=lax.Precision.HIGHEST)
    return (tok_scale * (base_term + delta_term)).astype(jnp.bfloat16)


def solution(mesh):
    placed = (
        P("ad", "row"),
        P("ad"),
        P(None, "row"),
        P(None, ("row", "ad"), None),
        P("ad", None, "row"),
        P("ad", "row"),
    )
    return jax.shard_map(
        on_device, mesh=mesh, in_specs=placed, out_specs=P("ad", "row"), check_vma=False
    )
```

profile of v0, /device:TPU:1, one launch (start us, length us, event | category | flops | bytes accessed | tf_op | source)
XLA Modules:
  0.0 162.4 jit_solution(736020516116679788)
XLA Ops:
  6.5 1.5 reshape.44
  8.0 12.9 %all_to_all.18 = bf16[8,2,8192]{2,1,0:T(2,128)(2,1)S(1)} all-to-all(bf16[8,2,8192]{2,1,0:T(2,128)(2,1)S(1)} %reshape.44), channel_id=1, replica_groups=mesh['row'=16,'ad'=8] {'ad'}, dimensions={0} | all-to-all | bytes 524288 | tf_op jit(solution)/shard_map/all_to_all | solution.py:14
  20.9 0.3 reshape.45
  21.3 0.3 copy.8
  21.6 1.0 all_to_all.16
  22.7 0.7 all-gather.5.cloned.1.call-update
  23.5 15.3 %slice_convert_fusion.14 = (f32[512,1024]{1,0:T(8,128)}, f32[512,1024]{1,0:T(8,128)}, f32[512,1024]{1,0:T(8,128)}, f32[512,1024]{1,0:T(8,128)}, f32[512,1024]{1,...) fusion(bf16[8192,1024]{1,0:T(8,128)(2,1)} %param.8), kind=kLoop, calls=%fused_computation.34 | loop fusion | flops 8388608 | bytes 50331648 | tf_op jit(solution)/shard_map/convert_element_type | solution.py:34
  38.8 0.3 fusion.45
  39.1 64.6 %psum.7 = bf16[256,64]{0,1:T(8,128)(2,1)S(1)} all-reduce(f32[256,64]{0,1:T(8,128)S(1)} %multiply_reduce_fusion.16), channel_id=1, replica_groups=mesh['row'=16,'ad'=8] {'row'}, use_global_device_ids=true, to_apply=%region_16.0 | all-reduce | flops 16384 | bytes 98304 | tf_op jit(solution)/shard_map/psum | solution.py:21
  103.7 1.3 convolution_bitcast_fusion
  105.0 3.1 %multiply_reduce_fusion = f32[4,1024]{1,0:T(4,128)S(1)} fusion(f32[512,1024]{1,0:T(8,128)} %get-tuple-element.20, bf16[4,64,1024]{2,1,0:T(8,128)(2,1)S(1)} %copy-done, bf16[4,8192,64]{1,2,0:T(8,128)(2,1)} %all-gather.3.cloned.1.call-done), kind=kOutput, calls=%fused_computation | convolution fusion | flops 274722816 | bytes 2899968 | tf_op jit(solution)/shard_map/akr,arf->akf/dot_general | solution.py:37
  108.2 0.4 copy-done.19
  108.6 1.4 multiply_reduce_fusion.1
  109.9 1.4 multiply_reduce_fusion.10
  111.5 1.4 multiply_reduce_fusion.11
  112.9 1.3 multiply_reduce_fusion.12
  114.5 1.4 multiply_reduce_fusion.13
  115.8 0.3 copy-done.10
  116.1 1.3 multiply_reduce_fusion.14
  117.6 1.4 multiply_reduce_fusion.15
  119.1 1.3 multiply_reduce_fusion.2
  120.6 1.6 multiply_reduce_fusion.3
  122.2 1.3 multiply_reduce_fusion.4
  123.5 0.2 copy-done.5
  123.7 1.3 multiply_reduce_fusion.5
  125.2 1.3 multiply_reduce_fusion.6
  126.7 1.4 multiply_reduce_fusion.7
  128.2 1.3 multiply_reduce_fusion.8
  129.5 1.4 multiply_reduce_fusion.9
  130.9 0.6 fusion.21
  131.6 11.5 %all-gather.5.cloned.1.call-done = bf16[256,8192]{1,0:T(8,128)(2,1)} async-done(((bf16[256,512]{1,0:T(8,128)(2,1)}), bf16[256,8192]{1,0:T(8,128)(2,1)}) %all-gather.5.cloned.1.call-update) | async-done | bytes 4194320 | tf_op jit(solution)/shard_map/all_gather | solution.py:24
  143.1 12.5 %fusion.1 = bf16[256,1024]{1,0:T(8,128)(2,1)} fusion(f32[256,1024]{1,0:T(8,128)S(1)} %fusion.21, f32[256,1024]{1,0:T(8,128)} %convolution_bitcast_fusion, bf16[256,8192]{1,0:T(8,128)(2,1)} %all-gather.5.cloned.1.call-done, bf16[8192,1024]{1,0:T(8,128)(2,1)} %param.8), kind=kOutput, calls=%fused_computation.19 | convolution fusion | flops 4295753728 | bytes 23592960 | tf_op jit(solution)/shard_map/dot_general | solution.py:23
  (44 shorter events, 1.3 us)
Async XLA Ops:
  6.5 97.2 %copy-start = (bf16[4,64,1024]{2,1,0:T(8,128)(2,1)S(1)}, bf16[4,64,1024]{2,1,0:T(8,128)(2,1)}, u32[]{:S(2)}) copy-start(bf16[4,64,1024]{2,1,0:T(8,128)(2,1)} %param.10) | copy-start | bytes 1572868
  6.5 16.9 %copy-start.18 = (s32[256]{0:T(256)S(1)}, s32[256]{0:T(256)}, u32[]{:S(2)}) copy-start(s32[256]{0:T(256)} %param.7) | copy-start | bytes 3076
  6.5 98.5 %all-gather.3.cloned.1.call-start = ((), (), s32[]{:S(2)}) async-start(), calls=%async_computation.1 | async-start | bytes 4456448 | tf_op jit(solution)/shard_map/all_gather | solution.py:30
  22.7 120.4 %all-gather.5.cloned.1.call-start = ((), (), s32[]{:S(2)}) async-start(), calls=%async_computation.2 | async-start | bytes 4456448 | tf_op jit(solution)/shard_map/all_gather | solution.py:24
  23.4 15.3 %copy-start.1 = (bf16[4,512,64]{1,2,0:T(8,128)(2,1)S(1)}, bf16[4,512,64]{1,2,0:T(8,128)(2,1)}, u32[]{:S(2)}) copy-start(bf16[4,512,64]{1,2,0:T(8,128)(2,1)} %all_to_all.16) | copy-start | bytes 786436
  23.5 15.3 %copy-start.16 = (bf16[256,512]{1,0:T(8,128)(2,1)S(1)}, bf16[256,512]{1,0:T(8,128)(2,1)}, u32[]{:S(2)}) copy-start(bf16[256,512]{1,0:T(8,128)(2,1)} %param.6) | copy-start | bytes 786436
  105.0 3.1 %copy-start.15 = (f32[512,1024]{1,0:T(8,128)S(1)}, f32[512,1024]{1,0:T(8,128)}, u32[]{:S(2)}) copy-start(f32[512,1024]{1,0:T(8,128)} %get-tuple-element.6) | copy-start | bytes 6291460
  105.0 3.5 %copy-start.19 = (bf16[4,8192,64]{1,2,0:T(8,128)(2,1)S(1)}, bf16[4,8192,64]{1,2,0:T(8,128)(2,1)}, u32[]{:S(2)}) copy-start(bf16[4,8192,64]{1,2,0:T(8,128)(2,1)} %all-gather.3.cloned.1.call-done) | copy-start | bytes 12582916
  108.2 1.8 %copy-start.14 = (f32[512,1024]{1,0:T(8,128)S(1)}, f32[512,1024]{1,0:T(8,128)}, u32[]{:S(2)}) copy-start(f32[512,1024]{1,0:T(8,128)} %get-tuple-element.15) | copy-start | bytes 6291460
  109.9 1.6 copy-start.13
  111.3 1.6 %copy-start.12 = (f32[512,1024]{1,0:T(8,128)S(1)}, f32[512,1024]{1,0:T(8,128)}, u32[]{:S(2)}) copy-start(f32[512,1024]{1,0:T(8,128)} %get-tuple-element.17) | copy-start | bytes 6291460
  112.9 1.6 copy-start.11
  114.3 1.8 %copy-start.10 = (f32[512,1024]{1,0:T(8,128)S(1)}, f32[512,1024]{1,0:T(8,128)}, u32[]{:S(2)}) copy-start(f32[512,1024]{1,0:T(8,128)} %get-tuple-element.5) | copy-start | bytes 6291460
  115.8 1.7 %copy-start.9 = (f32[512,1024]{1,0:T(8,128)S(1)}, f32[512,1024]{1,0:T(8,128)}, u32[]{:S(2)}) copy-start(f32[512,1024]{1,0:T(8,128)} %get-tuple-element.19) | copy-start | bytes 6291460
  117.5 1.6 copy-start.8
  118.9 1.6 %copy-start.7 = (f32[512,1024]{1,0:T(8,128)S(1)}, f32[512,1024]{1,0:T(8,128)}, u32[]{:S(2)}) copy-start(f32[512,1024]{1,0:T(8,128)} %get-tuple-element.8) | copy-start | bytes 6291460
  120.4 1.7 %copy-start.6 = (f32[512,1024]{1,0:T(8,128)S(1)}, f32[512,1024]{1,0:T(8,128)}, u32[]{:S(2)}) copy-start(f32[512,1024]{1,0:T(8,128)} %get-tuple-element.9) | copy-start | bytes 6291460
  122.2 1.6 copy-start.5
  123.5 1.6 %copy-start.4 = (f32[512,1024]{1,0:T(8,128)S(1)}, f32[512,1024]{1,0:T(8,128)}, u32[]{:S(2)}) copy-start(f32[512,1024]{1,0:T(8,128)} %get-tuple-element.11) | copy-start | bytes 6291460
  125.1 1.6 copy-start.3
  126.5 1.6 %copy-start.2 = (f32[512,1024]{1,0:T(8,128)S(1)}, f32[512,1024]{1,0:T(8,128)}, u32[]{:S(2)}) copy-start(f32[512,1024]{1,0:T(8,128)} %get-tuple-element.13) | copy-start | bytes 6291460
  129.5 1.4 copy-start.17
Sparse Core Ops, SparseCore 0:
  22.8 59.9 all-gather.2
  85.1 57.9 all-gather.4
where the time goes:
time: 163 us; the launch traced here: 162 us
  blocking collectives  77.5 us (48%)
  matrix products  38.4 us (24%)
  other arithmetic  15.3 us (9%)
  between operations  13.7 us (8%)
  waiting for transfers between devices  12.2 us (7%)
  local copies, waits for them, and re-layouts  5.25 us (3%)
    psum x1, blocking collectives, on_device(): low_sum = lax.psum(low_part, 'row')  64.6 us
    dot_general x16, matrix products, on_device(): jnp.einsum('akr,arf->akf', shard_piece[:, offset:offset + block_rows], pa...  23.6 us
    convert_element_type x1, other arithmetic, on_device(): lax.dynamic_slice_in_dim(base_weight, offset, block_rows, 0)  15.3 us
    all_to_all x1, blocking collectives, on_device(): lax.all_to_all(panel_down, 'ad', split_axis=0, concat_axis=1, tiled=True)  12.9 us
    dot_general x1, matrix products, on_device(): jnp.dot(lax.all_gather(tokens, 'row', axis=1, tiled=True), weight_rows, p...  12.5 us
    all_gather x1, waiting for transfers between devices, on_device(): lax.all_gather(tokens, 'row', axis=1, tiled=True)  11.5 us
    unnamed x42, local copies, waits for them, and re-layouts  3.88 us
  transfers between devices with their start and end apart: 2, of which 1 were waited for; matrix products, arithmetic and copies ran while one was open for 25% of the time, Pallas kernels for 0%

commit v1 on v0

v1 whole, which is shorter than its diff:
```python
import jax
import jax.numpy as jnp
from jax import lax
from jax.experimental import pallas as pl
from jax.experimental.pallas import tpu as pltpu
from jax.sharding import PartitionSpec as P

F32, BF16 = jnp.float32, jnp.bfloat16
VM = pl.BlockSpec(memory_space=pltpu.VMEM)
SM = pl.BlockSpec(memory_space=pltpu.SMEM)
NT = (((1,), (1,)), ((), ()))
TN = 256
MIB = 1 << 20

ROWS = [(yh, x, c) for yh in range(2) for x in range(4) for c in range(2)]
ADS = [(z, yl) for z in range(4) for yl in range(2)]


def row_of(yh, x, c):
    return (yh * 4 + x) * 2 + c


RING = [(row_of(yh, x, c), row_of(yh, (x + 1 - 2 * c) % 4, c)) for yh, x, c in ROWS]
CORE = [(row_of(yh, x, c), row_of(yh, x, 1 - c)) for yh, x, c in ROWS]
PAIR = [(row_of(yh, x, c), row_of(1 - yh, x, c)) for yh, x, c in ROWS]
YLO = [(z * 2 + yl, z * 2 + 1 - yl) for z, yl in ADS]


def ring(a):
    return lax.ppermute(a, "row", RING)


def core(a):
    return lax.ppermute(a, "row", CORE)


def pair(a):
    return lax.ppermute(a, "row", PAIR)


def ylo(a):
    return lax.ppermute(a, "ad", YLO)


def zshift(a, step):
    return lax.ppermute(a, "ad", [(z * 2 + yl, (z + step) % 4 * 2 + yl) for z, yl in ADS])


def tie(a, *after):
    return lax.optimization_barrier((a,) + after)[0]


def cat(*parts):
    return jnp.concatenate(parts, 0)


def params(limit=8 * MIB):
    return pltpu.CompilerParams(vmem_limit_bytes=limit)


def pack_body(pos_ref, d_ref, mine_ref, send_ref):
    z, yl = pos_ref[0], pos_ref[1]
    for out_ref, lane in ((mine_ref, yl), (send_ref, 1 - yl)):
        for j in range(4):
            group = lax.rem(z + j, 4) * 2 + lane
            four = d_ref[pl.ds(group * 4, 4)]
            out_ref[j] = jnp.concatenate([four[a] for a in range(4)], axis=1)


def pack(pos, panel):
    d, r = panel.shape[1:]
    shape = jax.ShapeDtypeStruct((4, d, 4 * r), BF16)
    return pl.pallas_call(
        pack_body,
        out_shape=[shape, shape],
        in_specs=[SM, VM],
        out_specs=[VM, VM],
        name="pack",
        cost_estimate=pl.CostEstimate(flops=0, bytes_accessed=MIB, transcendentals=0),
        compiler_params=params(),
    )(pos, panel)


def join_body(pos_ref, a0, a1, a2, a3, out_ref, full):
    z, yl = pos_ref[0], pos_ref[1]
    d = a0.shape[1]
    for ref, back in ((a0, 0), (a1, 3), (a2, 2), (a3, 1)):
        src = lax.rem(z + back, 4) * 2
        full[pl.ds(pl.multiple_of((src + yl) * d, d), d), :] = ref[0]
        full[pl.ds(pl.multiple_of((src + 1 - yl) * d, d), d), :] = ref[1]
    out_ref[...] = full[...].T


def join(pos, *pieces):
    _, d, width = pieces[0].shape
    return pl.pallas_call(
        join_body,
        out_shape=jax.ShapeDtypeStruct((width, 8 * d), BF16),
        in_specs=[SM] + [VM] * 4,
        out_specs=VM,
        scratch_shapes=[pltpu.VMEM((8 * d, width), BF16)],
        name="join",
        cost_estimate=pl.CostEstimate(flops=0, bytes_accessed=MIB, transcendentals=0),
        compiler_params=params(),
    )(pos, *pieces)


def halves(refs, height):
    return [(ref, h) for ref in refs for h in range(ref.shape[0] // height)]


def rows_at(block, height):
    ref, h = block
    return ref[h * height : (h + 1) * height, :]


def token_step(name, ids, blocks, weight, state):
    count = len(blocks)
    height, depth = blocks[0].shape[0], blocks[0].shape[1]
    height = 256 if height > 256 else height
    cols = weight.shape[1]
    first = state is None

    def body(ids_ref, *refs):
        held = halves(refs[:count], height)
        w_ref = refs[count]
        base_in, sq_in = (None, None) if first else refs[count + 1 : count + 3]
        base_out, sq_out = refs[-2:]
        for lo in range(0, cols, TN):
            tile = slice(lo, lo + TN)
            total = None if first else base_in[:, tile]
            squares = None if first else sq_in[:, tile]
            for i, block in enumerate(held):
                start = pl.multiple_of(ids_ref[i] * depth, depth)
                w = w_ref[pl.ds(start, depth), tile]
                part = jnp.dot(rows_at(block, height), w, preferred_element_type=F32)
                total = part if total is None else total + part
                wide = w.astype(F32)
                sq = jnp.sum((wide * wide).reshape(depth // 8, 8, TN), axis=0)
                squares = sq if squares is None else squares + sq
            base_out[:, tile] = total
            sq_out[:, tile] = squares

    n = sum(b.shape[0] // height for b in blocks)
    return pl.pallas_call(
        body,
        out_shape=[
            jax.ShapeDtypeStruct((height, cols), F32),
            jax.ShapeDtypeStruct((8, cols), F32),
        ],
        in_specs=[SM] + [VM] * (count + 1 + (0 if first else 2)),
        out_specs=[VM, VM],
        input_output_aliases={} if first else {count + 2: 0, count + 3: 1},
        name=name,
        cost_estimate=pl.CostEstimate(
            flops=2 * n * height * depth * cols, bytes_accessed=n * MIB, transcendentals=0
        ),
        compiler_params=params(),
    )(ids, *blocks, weight, *([] if first else state))


def panel_step(name, ids, tokens, panels, weight, state):
    count = len(panels)
    depth = panels[0].shape[1]
    height = 256
    cols = weight.shape[1]
    first = state is None

    def body(ids_ref, *refs):
        tok = halves(refs[:count], height)
        pan = halves(refs[count : 2 * count], height)
        w_ref = refs[2 * count]
        cross_in, both_in = (None, None) if first else refs[2 * count + 1 : 2 * count + 3]
        cross_out, both_out = refs[-2:]
        for lo in range(0, cols, TN):
            tile = slice(lo, lo + TN)
            total = None if first else cross_in[:, tile]
            for i, block in enumerate(pan):
                start = pl.multiple_of(ids_ref[i] * depth, depth)
                w = w_ref[pl.ds(start, depth), tile]
                part = jnp.dot(rows_at(block, height), w, preferred_element_type=F32)
                total = part if total is None else total + part
            cross_out[:, tile] = total
        for j, left in enumerate((tok, pan)):
            band = slice(j * height, (j + 1) * height)
            total = None if first else both_in[band, :]
            for a, b in zip(left, pan):
                part = lax.dot_general(
                    rows_at(a, height), rows_at(b, height), NT, preferred_element_type=F32
                )
                total = part if total is None else total + part
            both_out[band, :] = total

    n = sum(b.shape[0] // height for b in panels)
    return pl.pallas_call(
        body,
        out_shape=[
            jax.ShapeDtypeStruct((height, cols), F32),
            jax.ShapeDtypeStruct((2 * height, height), F32),
        ],
        in_specs=[SM] + [VM] * (2 * count + 1 + (0 if first else 2)),
        out_specs=[VM, VM],
        input_output_aliases={} if first else {2 * count + 2: 0, 2 * count + 3: 1},
        name=name,
        cost_estimate=pl.CostEstimate(
            flops=2 * n * height * depth * (cols + 2 * height),
            bytes_accessed=n * MIB,
            transcendentals=0,
        ),
        compiler_params=params(),
    )(ids, *tokens, *panels, weight, *([] if first else state))


def finish_body(base_ref, sq_ref, cross_ref, both_ref, up_ref, mag_ref, id_ref, out_ref):
    adapters = mag_ref.shape[0]
    tokens, cols = base_ref.shape
    width = cross_ref.shape[0]
    rank = width // adapters
    own = id_ref[...]
    lane = lax.broadcasted_iota(jnp.int32, (tokens, width), 1) // rank
    own_wide = jnp.concatenate([own] * (width // 128), axis=1)
    low = jnp.where(lane == own_wide, both_ref[:tokens, :], 0.0).astype(BF16)
    line = lax.broadcasted_iota(jnp.int32, (width, width), 0) // rank
    side = lax.broadcasted_iota(jnp.int32, (width, width), 1) // rank
    gram = jnp.where(line == side, both_ref[tokens:, :], 0.0)
    gram_hi = gram.astype(BF16)
    gram_lo = (gram - gram_hi.astype(F32)).astype(BF16)
    left = jnp.concatenate([low, gram_hi, gram_lo], axis=0)
    own_tile = jnp.concatenate([own] * (TN // 128), axis=1)
    for lo in range(0, cols, TN):
        tile = slice(lo, lo + TN)
        up = up_ref[:, tile]
        prod = jnp.dot(left, up, preferred_element_type=F32)
        delta = prod[:tokens]
        bent = prod[tokens : tokens + width] + prod[tokens + width :]
        terms = up.astype(F32) * (2.0 * cross_ref[:, tile] + bent)
        weight_sq = jnp.sum(sq_ref[:, tile], axis=0, keepdims=True)
        scale = None
        for a in range(adapters):
            mine = jnp.sum(terms[a * rank : (a + 1) * rank], axis=0, keepdims=True)
            gain = mag_ref[a : a + 1, tile] / jnp.sqrt(weight_sq + mine + 1e-6)
            wide = jnp.broadcast_to(gain, (tokens, TN))
            scale = wide if scale is None else jnp.where(own_tile == a, wide, scale)
        out_ref[:, tile] = (scale * (base_ref[:, tile] + delta)).astype(BF16)


def finish(base, sq, cross, both, up, mag, ids):
    tokens, cols = base.shape
    return pl.pallas_call(
        finish_body,
        out_shape=jax.ShapeDtypeStruct((tokens, cols), BF16),
        in_specs=[VM] * 7,
        out_specs=VM,
        name="finish",
        compiler_params=params(16 * MIB),
    )(base, sq, cross, both, up, mag, ids)


def on_device(tokens, token_adapter, base_weight, panel_down, panel_up, magnitude):
    adapters, rank, cols = panel_up.shape
    row = lax.axis_index("row").astype(jnp.int32)
    ad = lax.axis_index("ad").astype(jnp.int32)
    c, x, yh = row % 2, row // 2 % 4, row // 8
    step = 1 - 2 * c

    def at(dy, dx, dc):
        return (((yh + dy) % 2) * 4 + (x + dx * step + 8) % 4) * 2 + (c + dc) % 2

    def ids(*places):
        return jnp.stack([at(*p) for p in places])

    own, behind, ahead, far = (0, 0), (0, -1), (0, 1), (0, 2)
    p_own, p_behind, p_ahead, p_far = (1, 0), (1, -1), (1, 1), (1, 2)
    straight = lambda p: ((*p, 0), (*p, 1))
    crossed = lambda p: ((*p, 1), (*p, 0))

    pos = jnp.stack([ad // 2, ad % 2])
    up = panel_up.reshape(adapters * rank, cols)
    local = jnp.broadcast_to((token_adapter - ad * adapters)[:, None], (tokens.shape[0], 128))

    t0 = tokens
    o1 = core(t0)
    mine, send = pack(pos, panel_down)
    got = ylo(send)
    t_pair = pair(t0)
    t_ring = ring(cat(t0, o1))
    got = tie(got, o1)
    z_own = jnp.stack([mine[0], got[0]])
    z1 = zshift(jnp.stack([mine[1], got[1]]), 1)
    z3 = zshift(jnp.stack([mine[3], got[3]]), 3)
    z2 = zshift(jnp.stack([mine[2], got[2]]), 2)
    t_pair_c = core(t_pair)
    t_far = ring(t_ring[:256])
    t_pair_ring = ring(cat(t_pair, t_pair_c))
    z_own, z1, z2, z3 = tie((z_own, z1, z2, z3), t_ring, t_pair)
    q = join(pos, z_own, z1, z2, z3)
    base = token_step("tok_a", ids(*straight(own)), [t0, o1], base_weight, None)
    t_ring_c = core(t_ring)

    d_pair = pair(q)
    po = core(q)
    d_ring_a = ring(tie(q, t_far))
    d_ring_b = ring(po)
    base = token_step("tok_b", ids(*straight(behind), *crossed(ahead)), [t_ring, t_ring_c], base_weight, base)
    t_far_c = core(t_far)
    t_far_pair = pair(t_far)
    t_pair_ring_c = core(t_pair_ring)
    base = token_step(
        "tok_c",
        ids(*straight(p_own), *straight(far)),
        [t_pair, t_pair_c, t_far, t_far_c],
        base_weight,
        base,
    )
    norm = panel_step("pan_a", ids(*straight(own)), [t0, o1], [q, po], base_weight, None)
    d_pair_c = core(d_pair)
    d_far = ring(d_ring_a)
    d_pair_ring = ring(tie(cat(d_pair, d_pair_c), d_ring_b))
    t_far_pair_c = core(t_far_pair)
    base = token_step(
        "tok_d",
        ids(*straight(p_behind), *crossed(p_ahead), *straight(p_far)),
        [t_pair_ring, t_pair_ring_c, t_far_pair, t_far_pair_c],
        base_weight,
        base,
    )
    d_ring_ac, d_ring_bc = core(d_ring_a), core(d_ring_b)
    norm = panel_step(
        "pan_b",
        ids(*straight(behind), (*ahead, 1), (*ahead, 0), *straight(p_own)),
        [t_ring[:256], t_ring[256:], t_ring_c[:256], t_ring_c[256:], t_pair, t_pair_c],
        [d_ring_a, d_ring_b, d_ring_ac, d_ring_bc, d_pair, d_pair_c],
        base_weight,
        norm,
    )
    d_far_c = core(d_far)
    d_far_pair = pair(d_far)
    norm = panel_step("pan_c", ids(*straight(far)), [t_far, t_far_c], [d_far, d_far_c], base_weight, norm)
    d_pair_ring_c = core(d_pair_ring)
    norm = panel_step(
        "pan_d",
        ids(*straight(p_behind), *crossed(p_ahead)),
        [t_pair_ring, t_pair_ring_c],
        [d_pair_ring, d_pair_ring_c],
        base_weight,
        norm,
    )
    d_far_pair_c = core(d_far_pair)
    norm = panel_step(
        "pan_e", ids(*straight(p_far)), [t_far_pair, t_far_pair_c], [d_far_pair, d_far_pair_c], base_weight, norm
    )
    return finish(*base, *norm, up, magnitude, local)


def solution(mesh):
    placed = (
        P("ad", "row"),
        P("ad"),
        P(None, "row"),
        P(None, ("row", "ad"), None),
        P("ad", None, "row"),
        P("ad", "row"),
    )
    return jax.shard_map(on_device, mesh=mesh, in_specs=placed, out_specs=P("ad", "row"), check_vma=False)
```

time: 163 us -> 91.3 us (0.56)
  blocking collectives: 77.5 us -> 0 us
  matrix products: 38.4 us -> 0 us
  starting transfers between devices: 0.04 us -> 34.2 us
  Pallas kernels: 0 us -> 24.1 us
  between operations: 13.7 us -> 0.36 us
  other arithmetic: 15.3 us -> 4.92 us
  waiting for transfers between devices: 12.2 us -> 17.8 us
  local copies, waits for them, and re-layouts: 5.25 us -> 9.57 us
    psum x1 -> x0, blocking collectives: 64.6 us -> none  [on_device(): low_sum = lax.psum(low_part, 'row')]
    dot_general x19 -> x0, matrix products: 38.1 us -> none  [the longest x16 23.6 us: on_device(): jnp.einsum('akr,arf->akf', shard_piece[:, offset:offset + block_rows], pa...]
    ppermute x0 -> x28, starting transfers between devices: none -> 34.2 us  [the longest x7 10.4 us: ring(): return lax.ppermute(a, 'row', RING)]
    pallas_call x0 -> x12, Pallas kernels: none -> 24.1 us  [the longest x5 12.7 us: panel_step(): pl.pallas_call(body, out_shape=[jax.ShapeDtypeStruct((height, cols), F32)...]
    ppermute x0 -> x28, waiting for transfers between devices: none -> 17.8 us  [the longest x1 6.76 us: ylo(): return lax.ppermute(a, 'ad', YLO)]
    convert_element_type x2 -> x0, other arithmetic: 15.3 us -> none  [the longest x1 15.3 us: on_device(): lax.dynamic_slice_in_dim(base_weight, offset, block_rows, 0)]
    all_to_all x1 -> x0, blocking collectives: 12.9 us -> none  [on_device(): lax.all_to_all(panel_down, 'ad', split_axis=0, concat_axis=1, tiled=True)]
    all_gather x2 -> x0, waiting for transfers between devices: 11.5 us -> none  [the longest x1 11.5 us: on_device(): lax.all_gather(tokens, 'row', axis=1, tiled=True)]
  transfers between devices with their start and end apart: 2 -> 28, of which waited for: 1 -> 7; matrix products, arithmetic and copies ran while one was open for 25% -> 6% of each run, Pallas kernels for 0% -> 23%
where the time goes in v1:
time: 91.3 us; the launch traced here: 91 us
  starting transfers between devices  34.2 us (37%)
  Pallas kernels  24.1 us (26%)
  waiting for transfers between devices  17.8 us (19%)
  local copies, waits for them, and re-layouts  9.57 us (10%)
  other arithmetic  4.92 us (5%)
    pallas_call x5, Pallas kernels, panel_step(): pl.pallas_call(body, out_shape=[jax.ShapeDtypeStruct((height, cols), F32)...  12.7 us
    ppermute x7, starting transfers between devices, ring(): return lax.ppermute(a, 'row', RING)  10.4 us
    ppermute x13, starting transfers between devices, core(): return lax.ppermute(a, 'row', CORE)  9.97 us
    unnamed x28, local copies, waits for them, and re-layouts  8.51 us
    pallas_call x4, Pallas kernels, token_step(): pl.pallas_call(body, out_shape=[jax.ShapeDtypeStruct((height, cols), F32)...  8.2 us
    ppermute x4, starting transfers between devices, pair(): return lax.ppermute(a, 'row', PAIR)  7.57 us
    ppermute x1, waiting for transfers between devices, ylo(): return lax.ppermute(a, 'ad', YLO)  6.76 us
    ppermute x3, starting transfers between devices, zshift(): lax.ppermute(a, 'ad', [(z * 2 + yl, (z + step) % 4 * 2 + yl) for z, yl in...  5.88 us
  transfers between devices with their start and end apart: 28, of which 7 were waited for; matrix products, arithmetic and copies ran while one was open for 6% of the time, Pallas kernels for 23%

profile of v1, /device:TPU:1, one launch (start us, length us, event | category | flops | bytes accessed | tf_op | source)
XLA Modules:
  0.0 91.0 jit_solution(2165383978972107264)
XLA Ops:
  0.0 1.4 %collective-permute-start.4 = (bf16[256,512]{1,0:T(8,128)(2,1)}, bf16[256,512]{1,0:T(8,128)(2,1)S(1)}, u32[]{:S(2)}, u32[]{:S(2)}) collective-permute-start(bf16[256,512]{1,0:T(8,128)(2,1)} %refs_0_.3), channel_id=1, source_target_pairs={{0,8},{8,0},{16,24},{24,16},{32,40},{40,32},{48,56},{56,48},{64,72... | collective-permute-start | bytes 786440 | tf_op jit(solution)/shard_map/ppermute | solution.py:34
  1.4 3.0 %collective-permute-start = (bf16[256,512]{1,0:T(8,128)(2,1)}, bf16[256,512]{1,0:T(8,128)(2,1)S(1)}, u32[]{:S(2)}, u32[]{:S(2)}) collective-permute-start(bf16[256,512]{1,0:T(8,128)(2,1)} %refs_0_.3), channel_id=1, source_target_pairs={{0,64},{8,72},{16,80},{24,88},{32,96},{40,104},{48,112},{56,120},{... | collective-permute-start | bytes 786440 | tf_op jit(solution)/shard_map/ppermute | solution.py:38
  7.5 6.8 %collective-permute-done.11 = bf16[4,64,256]{2,1,0:T(8,128)(2,1)S(1)} collective-permute-done((bf16[4,64,256]{2,1,0:T(8,128)(2,1)S(1)}, bf16[4,64,256]{2,1,0:T(8,128)(2,1)S(1)}, u32[]{:S(2)}, u32[]{:S(2)}) %collective-permute-start.11) | collective-permute-done | bytes 131104 | tf_op jit(solution)/shard_map/ppermute | solution.py:42
  15.3 2.5 %collective-permute-start.5 = (bf16[512,512]{1,0:T(8,128)(2,1)S(1)}, bf16[512,512]{1,0:T(8,128)(2,1)S(1)}, u32[]{:S(2)}, u32[]{:S(2)}) collective-permute-start(bf16[512,512]{1,0:T(8,128)(2,1)S(1)} %pad_maximum_fusion.1), channel_id=1, source_target_pairs={{0,16},{8,56},{16,32},{24,8},{32,48},{40,24},{48,0},{56,40},{64,80... | collective-permute-start | bytes 1572872 | tf_op jit(solution)/shard_map/ppermute | solution.py:30
  17.9 1.7 %collective-permute-start.12 = (bf16[2,64,256]{2,1,0:T(8,128)(2,1)S(1)}, bf16[2,64,256]{2,1,0:T(8,128)(2,1)S(1)}, u32[]{:S(2)}, u32[]{:S(2)}) collective-permute-start(bf16[2,64,256]{2,1,0:T(8,128)(2,1)S(1)} %pad_maximum_fusion.4), channel_id=1, source_target_pairs={{0,2},{1,3},{2,4},{3,5},{4,6},{5,7},{6,0},{7,1},{8,10},{9,11},{10,... | collective-permute-start | bytes 196616 | tf_op jit(solution)/shard_map/ppermute | solution.py:46
  19.7 3.4 %collective-permute-start.13 = (bf16[2,64,256]{2,1,0:T(8,128)(2,1)S(1)}, bf16[2,64,256]{2,1,0:T(8,128)(2,1)S(1)}, u32[]{:S(2)}, u32[]{:S(2)}) collective-permute-start(bf16[2,64,256]{2,1,0:T(8,128)(2,1)S(1)} %pad_maximum_fusion.5), channel_id=1, source_target_pairs={{0,4},{1,5},{2,6},{3,7},{4,0},{5,1},{6,2},{7,3},{8,12},{9,13},{10,... | collective-permute-start | bytes 196616 | tf_op jit(solution)/shard_map/ppermute | solution.py:46
  24.3 2.3 %collective-permute-done.13.a2 = bf16[2,64,256]{2,1,0:T(8,128)(2,1)S(1)} collective-permute-done((bf16[2,64,256]{2,1,0:T(8,128)(2,1)S(1)}, bf16[2,64,256]{2,1,0:T(8,128)(2,1)S(1)}, u32[]{:S(2)}, u32[]{:S(2)}) %collective-permute-start.13) | collective-permute-done | bytes 65568 | tf_op jit(solution)/shard_map/ppermute | solution.py:46
  27.4 1.5 %collective-permute-start.21 = (bf16[256,512]{1,0:T(8,128)(2,1)S(1)}, bf16[256,512]{1,0:T(8,128)(2,1)}, u32[]{:S(2)}, u32[]{:S(2)}) collective-permute-start(bf16[256,512]{1,0:T(8,128)(2,1)S(1)} %join.1.refs_2_), channel_id=1, source_target_pairs={{0,8},{8,0},{16,24},{24,16},{32,40},{40,32},{48,56},{56,48},{64,72... | collective-permute-start | bytes 786440 | tf_op jit(solution)/shard_map/ppermute | solution.py:34
  28.9 1.6 %collective-permute-start.19 = (bf16[256,512]{1,0:T(8,128)(2,1)S(1)}, bf16[256,512]{1,0:T(8,128)(2,1)S(1)}, u32[]{:S(2)}, u32[]{:S(2)}) collective-permute-start(bf16[256,512]{1,0:T(8,128)(2,1)S(1)} %join.1.refs_2_), channel_id=1, source_target_pairs={{0,64},{8,72},{16,80},{24,88},{32,96},{40,104},{48,112},{56,120},{... | collective-permute-start | bytes 786440 | tf_op jit(solution)/shard_map/ppermute | solution.py:38
  31.3 1.0 %collective-permute-start.2 = (bf16[512,512]{1,0:T(8,128)(2,1)}, bf16[512,512]{1,0:T(8,128)(2,1)S(1)}, u32[]{:S(2)}, u32[]{:S(2)}) collective-permute-start(bf16[512,512]{1,0:T(8,128)(2,1)} %pad_maximum_fusion), channel_id=1, source_target_pairs={{0,16},{8,56},{16,32},{24,8},{32,48},{40,24},{48,0},{56,40},{64,80... | collective-permute-start | bytes 1572872 | tf_op jit(solution)/shard_map/ppermute | solution.py:30
  33.1 1.3 %collective-permute-start.6 = (bf16[256,512]{1,0:T(8,128)(2,1)S(1)}, bf16[256,512]{1,0:T(8,128)(2,1)S(1)}, u32[]{:S(2)}, u32[]{:S(2)}) collective-permute-start(bf16[256,512]{1,0:T(8,128)(2,1)S(1)} %get-tuple-element.62.refs_0_), channel_id=1, source_target_pairs={{0,16},{8,56},{16,32},{24,8},{32,48},{40,24},{48,0},{56,40},{64,80... | collective-permute-start | bytes 786440 | tf_op jit(solution)/shard_map/ppermute | solution.py:30
  35.6 2.6 %collective-permute-done.19.refs_10_ = bf16[256,512]{1,0:T(8,128)(2,1)S(1)} collective-permute-done((bf16[256,512]{1,0:T(8,128)(2,1)S(1)}, bf16[256,512]{1,0:T(8,128)(2,1)S(1)}, u32[]{:S(2)}, u32[]{:S(2)}) %collective-permute-start.19) | collective-permute-done | bytes 262176 | tf_op jit(solution)/shard_map/ppermute | solution.py:38
  39.4 3.2 %collective-permute-done.6.refs_2_.refs_0_ = bf16[256,512]{1,0:T(8,128)(2,1)S(1)} collective-permute-done((bf16[256,512]{1,0:T(8,128)(2,1)S(1)}, bf16[256,512]{1,0:T(8,128)(2,1)S(1)}, u32[]{:S(2)}, u32[]{:S(2)}) %collective-permute-start.6) | collective-permute-done | bytes 262176 | tf_op jit(solution)/shard_map/ppermute | solution.py:30
  42.6 2.0 %collective-permute-start.15 = (bf16[256,512]{1,0:T(8,128)(2,1)S(1)}, bf16[256,512]{1,0:T(8,128)(2,1)}, u32[]{:S(2)}, u32[]{:S(2)}) collective-permute-start(bf16[256,512]{1,0:T(8,128)(2,1)S(1)} %join.1.refs_2_), channel_id=1, source_target_pairs={{0,16},{8,56},{16,32},{24,8},{32,48},{40,24},{48,0},{56,40},{64,80... | collective-permute-start | bytes 786440 | tf_op jit(solution)/shard_map/ppermute | solution.py:30
  45.5 2.4 %collective-permute-start.9 = (bf16[256,512]{1,0:T(8,128)(2,1)S(1)}, bf16[256,512]{1,0:T(8,128)(2,1)S(1)}, u32[]{:S(2)}, u32[]{:S(2)}) collective-permute-start(bf16[256,512]{1,0:T(8,128)(2,1)S(1)} %collective-permute-done.6.refs_2_.refs_0_), channel_id=1, source_target_pairs={{0,8},{8,0},{16,24},{24,16},{32,40},{40,32},{48,56},{56,48},{64,72... | collective-permute-start | bytes 786440 | tf_op jit(solution)/shard_map/ppermute | solution.py:34
  48.0 1.4 %collective-permute-start.7 = (bf16[256,512]{1,0:T(8,128)(2,1)S(1)}, bf16[256,512]{1,0:T(8,128)(2,1)S(1)}, u32[]{:S(2)}, u32[]{:S(2)}) collective-permute-start(bf16[256,512]{1,0:T(8,128)(2,1)S(1)} %collective-permute-done.6.refs_2_.refs_0_), channel_id=1, source_target_pairs={{0,64},{8,72},{16,80},{24,88},{32,96},{40,104},{48,112},{56,120},{... | collective-permute-start | bytes 786440 | tf_op jit(solution)/shard_map/ppermute | solution.py:38
  49.4 1.9 %pad_maximum_fusion.2 = bf16[512,512]{1,0:T(8,128)(2,1)} fusion(bf16[256,512]{1,0:T(8,128)(2,1)} %collective-permute-done.20.refs_11_, bf16[256,512]{1,0:T(8,128)(2,1)} %copy-done.2), kind=kLoop, calls=%fused_computation.2 | loop fusion | flops 1048576 | bytes 1048576 | tf_op jit(solution)/shard_map/concatenate | solution.py:54
  51.6 5.8 %copy-done = bf16[8192,1024]{1,0:T(8,128)(2,1)S(1)} copy-done((bf16[8192,1024]{1,0:T(8,128)(2,1)S(1)}, bf16[8192,1024]{1,0:T(8,128)(2,1)}, u32[]{:S(2)}) %copy-start) | copy-done | bytes 16777240
  58.3 1.3 %tok_a.1 = (f32[256,1024]{1,0:T(8,128)S(1)}, f32[8,1024]{1,0:T(8,128)S(1)}) custom-call(s32[2]{0:T(128)S(1)} %pad_add_fusion.2.ids_ref, bf16[256,512]{1,0:T(8,128)(2,1)S(1)} %copy-done.1, bf16[256,512]{1,0:T(8,128)(2,1)S(1)} %collective-permute-done.4.refs_1_, bf16[8192,1024]{1,0:T(8,128)(2,1)S(1)} %copy-done), custom_call_target="tpu_custom_call" | custom-call | flops 536870912 | bytes 2097152 | tf_op jit(solution)/shard_map/tok_a/pallas_call | solution.py:145
  59.6 2.5 %pan_a.1 = (f32[256,1024]{1,0:T(8,128)S(1)}, f32[512,256]{1,0:T(8,128)S(1)}) custom-call(s32[2]{0:T(128)S(1)} %pad_add_fusion.2.ids_ref, bf16[256,512]{1,0:T(8,128)(2,1)S(1)} %copy-done.1, bf16[256,512]{1,0:T(8,128)(2,1)S(1)} %collective-permute-done.4.refs_1_, bf16[256,512]{1,0:T(8,128)(2,1)S(1)} %join.1.refs_2_, ...), custom_call_target="tpu_custom_call" | custom-call | flops 805306368 | bytes 2097152 | tf_op jit(solution)/shard_map/pan_a/pallas_call | solution.py:195
  63.1 2.9 %collective-permute-start.16 = (bf16[256,512]{1,0:T(8,128)(2,1)}, bf16[256,512]{1,0:T(8,128)(2,1)S(1)}, u32[]{:S(2)}, u32[]{:S(2)}) collective-permute-start(bf16[256,512]{1,0:T(8,128)(2,1)} %collective-permute-done.15.refs_6_), channel_id=1, source_target_pairs={{0,16},{8,56},{16,32},{24,8},{32,48},{40,24},{48,0},{56,40},{64,80... | collective-permute-start | bytes 786440 | tf_op jit(solution)/shard_map/ppermute | solution.py:30
  66.1 2.1 %tok_b.1 = (f32[256,1024]{1,0:T(8,128)S(1)}, f32[8,1024]{1,0:T(8,128)S(1)}) custom-call(s32[4]{0:T(128)S(1)} %pad_add_fusion.1.ids_ref, bf16[512,512]{1,0:T(8,128)(2,1)S(1)} %collective-permute-done.5.refs_0_, bf16[512,512]{1,0:T(8,128)(2,1)S(1)} %collective-permute-done.10.refs_1_, ...), custom_call_target="tpu_custom_call", output_to_operand_aliasing={{0}: (4, {}), {1}: (5, {})} | custom-call | flops 1073741824 | bytes 4194304 | tf_op jit(solution)/shard_map/tok_b/pallas_call | solution.py:145
  68.3 1.3 %collective-permute-done.16.refs_2_ = bf16[256,512]{1,0:T(8,128)(2,1)S(1)} collective-permute-done((bf16[256,512]{1,0:T(8,128)(2,1)}, bf16[256,512]{1,0:T(8,128)(2,1)S(1)}, u32[]{:S(2)}, u32[]{:S(2)}) %collective-permute-start.16) | collective-permute-done | bytes 262176 | tf_op jit(solution)/shard_map/ppermute | solution.py:30
  69.6 1.6 %collective-permute-start.17 = (bf16[256,512]{1,0:T(8,128)(2,1)S(1)}, bf16[256,512]{1,0:T(8,128)(2,1)S(1)}, u32[]{:S(2)}, u32[]{:S(2)}) collective-permute-start(bf16[256,512]{1,0:T(8,128)(2,1)S(1)} %collective-permute-done.16.refs_2_), channel_id=1, source_target_pairs={{0,64},{8,72},{16,80},{24,88},{32,96},{40,104},{48,112},{56,120},{... | collective-permute-start | bytes 786440 | tf_op jit(solution)/shard_map/ppermute | solution.py:38
  71.2 1.7 %collective-permute-start.24 = (bf16[512,512]{1,0:T(8,128)(2,1)}, bf16[512,512]{1,0:T(8,128)(2,1)S(1)}, u32[]{:S(2)}, u32[]{:S(2)}) collective-permute-start(bf16[512,512]{1,0:T(8,128)(2,1)} %collective-permute-done.23.refs_2_), channel_id=1, source_target_pairs={{0,8},{8,0},{16,24},{24,16},{32,40},{40,32},{48,56},{56,48},{64,72... | collective-permute-start | bytes 1572872 | tf_op jit(solution)/shard_map/ppermute | solution.py:34
  72.9 2.1 %tok_c.1 = (f32[256,1024]{1,0:T(8,128)S(1)}, f32[8,1024]{1,0:T(8,128)S(1)}) custom-call(s32[4]{0:T(128)S(1)} %pad_add_fusion.ids_ref, bf16[256,512]{1,0:T(8,128)(2,1)S(1)} %collective-permute-done.refs_0_.refs_4_, bf16[256,512]{1,0:T(8,128)(2,1)S(1)} %collective-permute-done.1.refs_1_.refs_5_, ...), custom_call_target="tpu_custom_call", output_to_operand_aliasing={{0}: (6, {}), {1}: (7, {})} | custom-call | flops 1073741824 | bytes 4194304 | tf_op jit(solution)/shard_map/tok_c/pallas_call | solution.py:145
  75.1 3.8 %pan_b.1 = (f32[256,1024]{1,0:T(8,128)S(1)}, f32[512,256]{1,0:T(8,128)S(1)}) custom-call(s32[6]{0:T(128)S(1)} %stack.140.ids_ref, bf16[256,512]{1,0:T(8,128)(2,1)S(1)} %copy-done.6, bf16[256,512]{1,0:T(8,128)(2,1)S(1)} %copy-done.4, bf16[256,512]{1,0:T(8,128)(2,1)S(1)} %get-tuple-element.60.refs_2_, ...), custom_call_target="tpu_custom_call", output_to_operand_aliasing={{0}: (14, {}), {1}: (15, {})} | custom-call | flops 2415919104 | bytes 6291456 | tf_op jit(solution)/shard_map/pan_b/pallas_call | solution.py:195
  79.9 2.8 %tok_d.1 = (f32[256,1024]{1,0:T(8,128)S(1)}, f32[8,1024]{1,0:T(8,128)S(1)}) custom-call(s32[6]{0:T(128)S(1)} %stack.116.ids_ref, bf16[512,512]{1,0:T(8,128)(2,1)S(1)} %collective-permute-done.2.refs_0_, bf16[512,512]{1,0:T(8,128)(2,1)S(1)} %collective-permute-done.3.refs_1_, ...), custom_call_target="tpu_custom_call", output_to_operand_aliasing={{0}: (6, {}), {1}: (7, {})} | custom-call | flops 1610612736 | bytes 6291456 | tf_op jit(solution)/shard_map/tok_d/pallas_call | solution.py:145
  82.6 1.6 %pan_c.1 = (f32[256,1024]{1,0:T(8,128)S(1)}, f32[512,256]{1,0:T(8,128)S(1)}) custom-call(s32[2]{0:T(128)S(1)} %pad_add_fusion.6.ids_ref, bf16[256,512]{1,0:T(8,128)(2,1)S(1)} %collective-permute-done.6.refs_2_.refs_0_, bf16[256,512]{1,0:T(8,128)(2,1)S(1)} %collective-permute-done.9.refs_3_.refs_1_, ...), custom_call_target="tpu_custom_call", output_to_operand_aliasing={{0}: (6, {}), {1}: (7, {})} | custom-call | flops 805306368 | bytes 2097152 | tf_op jit(solution)/shard_map/pan_c/pallas_call | solution.py:195
  84.3 3.0 %pan_d.1 = (f32[256,1024]{1,0:T(8,128)S(1)}, f32[512,256]{1,0:T(8,128)S(1)}) custom-call(s32[4]{0:T(128)S(1)} %pad_add_fusion.5.ids_ref, bf16[512,512]{1,0:T(8,128)(2,1)S(1)} %collective-permute-done.2.refs_0_, bf16[512,512]{1,0:T(8,128)(2,1)S(1)} %collective-permute-done.3.refs_1_, ...), custom_call_target="tpu_custom_call", output_to_operand_aliasing={{0}: (6, {}), {1}: (7, {})} | custom-call | flops 1610612736 | bytes 4194304 | tf_op jit(solution)/shard_map/pan_d/pallas_call | solution.py:195
  87.3 1.6 %pan_e.1 = (f32[256,1024]{1,0:T(8,128)S(1)}, f32[512,256]{1,0:T(8,128)S(1)}) custom-call(s32[2]{0:T(128)S(1)} %pad_add_fusion.3.ids_ref, bf16[256,512]{1,0:T(8,128)(2,1)S(1)} %collective-permute-done.7.refs_2_.refs_0_, bf16[256,512]{1,0:T(8,128)(2,1)S(1)} %collective-permute-done.8.refs_3_.refs_1_, ...), custom_call_target="tpu_custom_call", output_to_operand_aliasing={{0}: (6, {}), {1}: (7, {})} | custom-call | flops 805306368 | bytes 2097152 | tf_op jit(solution)/shard_map/pan_e/pallas_call | solution.py:195
  89.1 1.9 %finish.1 = bf16[256,1024]{1,0:T(8,128)(2,1)} custom-call(f32[256,1024]{1,0:T(8,128)S(1)} %get-tuple-element.38.base_ref, f32[8,1024]{1,0:T(8,128)S(1)} %get-tuple-element.39.sq_ref, f32[256,1024]{1,0:T(8,128)S(1)} %get-tuple-element.57.cross_ref, f32[512,256]{1,0:T(8,128)S(1)} %get-tuple-element.58.both_ref, bf16[256,1024]{1,0:T(8,128)(2,1)S(1)} %bitcast.21, ...), custom_call_target="tpu_custom_call" | custom-call | tf_op jit(solution)/shard_map/finish/pallas_call | solution.py:249
  (87 shorter events, 14.5 us)
Async XLA Ops:
  0.0 14.3 %collective-permute-start.4 = (bf16[256,512]{1,0:T(8,128)(2,1)}, bf16[256,512]{1,0:T(8,128)(2,1)S(1)}, u32[]{:S(2)}, u32[]{:S(2)}) collective-permute-start(bf16[256,512]{1,0:T(8,128)(2,1)} %refs_0_.3), channel_id=1, source_target_pairs={{0,8},{8,0},{16,24},{24,16},{32,40},{40,32},{48,56},{56,48},{64,72... | collective-permute-start | bytes 786440 | tf_op jit(solution)/shard_map/ppermute | solution.py:34
  1.4 18.2 %collective-permute-start = (bf16[256,512]{1,0:T(8,128)(2,1)}, bf16[256,512]{1,0:T(8,128)(2,1)S(1)}, u32[]{:S(2)}, u32[]{:S(2)}) collective-permute-start(bf16[256,512]{1,0:T(8,128)(2,1)} %refs_0_.3), channel_id=1, source_target_pairs={{0,64},{8,72},{16,80},{24,88},{32,96},{40,104},{48,112},{56,120},{... | collective-permute-start | bytes 786440 | tf_op jit(solution)/shard_map/ppermute | solution.py:38
  6.2 8.1 %collective-permute-start.11 = (bf16[4,64,256]{2,1,0:T(8,128)(2,1)S(1)}, bf16[4,64,256]{2,1,0:T(8,128)(2,1)S(1)}, u32[]{:S(2)}, u32[]{:S(2)}) collective-permute-start(bf16[4,64,256]{2,1,0:T(8,128)(2,1)S(1)} %get-tuple-element.41), channel_id=1, source_target_pairs={{0,1},{1,0},{2,3},{3,2},{4,5},{5,4},{6,7},{7,6},{8,9},{9,8},{10,11... | collective-permute-start | bytes 393224 | tf_op jit(solution)/shard_map/ppermute | solution.py:42
  15.3 11.4 %collective-permute-start.5 = (bf16[512,512]{1,0:T(8,128)(2,1)S(1)}, bf16[512,512]{1,0:T(8,128)(2,1)S(1)}, u32[]{:S(2)}, u32[]{:S(2)}) collective-permute-start(bf16[512,512]{1,0:T(8,128)(2,1)S(1)} %pad_maximum_fusion.1), channel_id=1, source_target_pairs={{0,16},{8,56},{16,32},{24,8},{32,48},{40,24},{48,0},{56,40},{64,80... | collective-permute-start | bytes 1572872 | tf_op jit(solution)/shard_map/ppermute | solution.py:30
  17.9 6.5 %collective-permute-start.12 = (bf16[2,64,256]{2,1,0:T(8,128)(2,1)S(1)}, bf16[2,64,256]{2,1,0:T(8,128)(2,1)S(1)}, u32[]{:S(2)}, u32[]{:S(2)}) collective-permute-start(bf16[2,64,256]{2,1,0:T(8,128)(2,1)S(1)} %pad_maximum_fusion.4), channel_id=1, source_target_pairs={{0,2},{1,3},{2,4},{3,5},{4,6},{5,7},{6,0},{7,1},{8,10},{9,11},{10,... | collective-permute-start | bytes 196616 | tf_op jit(solution)/shard_map/ppermute | solution.py:46
  19.6 10.9 %collective-permute-start.1 = (bf16[256,512]{1,0:T(8,128)(2,1)S(1)}, bf16[256,512]{1,0:T(8,128)(2,1)S(1)}, u32[]{:S(2)}, u32[]{:S(2)}) collective-permute-start(bf16[256,512]{1,0:T(8,128)(2,1)S(1)} %collective-permute-done.refs_0_.refs_4_), channel_id=1, source_target_pairs={{0,8},{8,0},{16,24},{24,16},{32,40},{40,32},{48,56},{56,48},{64,72... | collective-permute-start | bytes 786440 | tf_op jit(solution)/shard_map/ppermute | solution.py:34
  19.7 7.0 %collective-permute-start.13 = (bf16[2,64,256]{2,1,0:T(8,128)(2,1)S(1)}, bf16[2,64,256]{2,1,0:T(8,128)(2,1)S(1)}, u32[]{:S(2)}, u32[]{:S(2)}) collective-permute-start(bf16[2,64,256]{2,1,0:T(8,128)(2,1)S(1)} %pad_maximum_fusion.5), channel_id=1, source_target_pairs={{0,4},{1,5},{2,6},{3,7},{4,0},{5,1},{6,2},{7,3},{8,12},{9,13},{10,... | collective-permute-start | bytes 196616 | tf_op jit(solution)/shard_map/ppermute | solution.py:46
  23.1 3.6 %collective-permute-start.14 = (bf16[2,64,256]{2,1,0:T(8,128)(2,1)S(1)}, bf16[2,64,256]{2,1,0:T(8,128)(2,1)S(1)}, u32[]{:S(2)}, u32[]{:S(2)}) collective-permute-start(bf16[2,64,256]{2,1,0:T(8,128)(2,1)S(1)} %pad_maximum_fusion.6), channel_id=1, source_target_pairs={{0,6},{1,7},{2,0},{3,1},{4,2},{5,3},{6,4},{7,5},{8,14},{9,15},{10,... | collective-permute-start | bytes 196616 | tf_op jit(solution)/shard_map/ppermute | solution.py:46
  27.4 7.7 %collective-permute-start.21 = (bf16[256,512]{1,0:T(8,128)(2,1)S(1)}, bf16[256,512]{1,0:T(8,128)(2,1)}, u32[]{:S(2)}, u32[]{:S(2)}) collective-permute-start(bf16[256,512]{1,0:T(8,128)(2,1)S(1)} %join.1.refs_2_), channel_id=1, source_target_pairs={{0,8},{8,0},{16,24},{24,16},{32,40},{40,32},{48,56},{56,48},{64,72... | collective-permute-start | bytes 786440 | tf_op jit(solution)/shard_map/ppermute | solution.py:34
  28.9 9.4 %collective-permute-start.19 = (bf16[256,512]{1,0:T(8,128)(2,1)S(1)}, bf16[256,512]{1,0:T(8,128)(2,1)S(1)}, u32[]{:S(2)}, u32[]{:S(2)}) collective-permute-start(bf16[256,512]{1,0:T(8,128)(2,1)S(1)} %join.1.refs_2_), channel_id=1, source_target_pairs={{0,64},{8,72},{16,80},{24,88},{32,96},{40,104},{48,112},{56,120},{... | collective-permute-start | bytes 786440 | tf_op jit(solution)/shard_map/ppermute | solution.py:38
  31.3 20.0 %collective-permute-start.2 = (bf16[512,512]{1,0:T(8,128)(2,1)}, bf16[512,512]{1,0:T(8,128)(2,1)S(1)}, u32[]{:S(2)}, u32[]{:S(2)}) collective-permute-start(bf16[512,512]{1,0:T(8,128)(2,1)} %pad_maximum_fusion), channel_id=1, source_target_pairs={{0,16},{8,56},{16,32},{24,8},{32,48},{40,24},{48,0},{56,40},{64,80... | collective-permute-start | bytes 1572872 | tf_op jit(solution)/shard_map/ppermute | solution.py:30
  33.1 9.6 %collective-permute-start.6 = (bf16[256,512]{1,0:T(8,128)(2,1)S(1)}, bf16[256,512]{1,0:T(8,128)(2,1)S(1)}, u32[]{:S(2)}, u32[]{:S(2)}) collective-permute-start(bf16[256,512]{1,0:T(8,128)(2,1)S(1)} %get-tuple-element.62.refs_0_), channel_id=1, source_target_pairs={{0,16},{8,56},{16,32},{24,8},{32,48},{40,24},{48,0},{56,40},{64,80... | collective-permute-start | bytes 786440 | tf_op jit(solution)/shard_map/ppermute | solution.py:30
  35.0 10.5 %collective-permute-start.22 = (bf16[256,512]{1,0:T(8,128)(2,1)}, bf16[256,512]{1,0:T(8,128)(2,1)}, u32[]{:S(2)}, u32[]{:S(2)}) collective-permute-start(bf16[256,512]{1,0:T(8,128)(2,1)} %collective-permute-done.21.refs_3_), channel_id=1, source_target_pairs={{0,16},{8,56},{16,32},{24,8},{32,48},{40,24},{48,0},{56,40},{64,80... | collective-permute-start | bytes 786440 | tf_op jit(solution)/shard_map/ppermute | solution.py:30
  38.2 9.7 %copy-start.2 = (bf16[256,512]{1,0:T(8,128)(2,1)}, bf16[256,512]{1,0:T(8,128)(2,1)S(1)}, u32[]{:S(2)}) copy-start(bf16[256,512]{1,0:T(8,128)(2,1)S(1)} %collective-permute-done.19.refs_10_) | copy-start | bytes 786436
  38.2 9.7 %collective-permute-start.20 = (bf16[256,512]{1,0:T(8,128)(2,1)S(1)}, bf16[256,512]{1,0:T(8,128)(2,1)}, u32[]{:S(2)}, u32[]{:S(2)}) collective-permute-start(bf16[256,512]{1,0:T(8,128)(2,1)S(1)} %collective-permute-done.19.refs_10_), channel_id=1, source_target_pairs={{0,8},{8,0},{16,24},{24,16},{32,40},{40,32},{48,56},{56,48},{64,72... | collective-permute-start | bytes 786440 | tf_op jit(solution)/shard_map/ppermute | solution.py:34
  39.2 23.3 %collective-permute-start.10 = (bf16[512,512]{1,0:T(8,128)(2,1)S(1)}, bf16[512,512]{1,0:T(8,128)(2,1)S(1)}, u32[]{:S(2)}, u32[]{:S(2)}) collective-permute-start(bf16[512,512]{1,0:T(8,128)(2,1)S(1)} %collective-permute-done.5.refs_0_), channel_id=1, source_target_pairs={{0,8},{8,0},{16,24},{24,16},{32,40},{40,32},{48,56},{56,48},{64,72... | collective-permute-start | bytes 1572872 | tf_op jit(solution)/shard_map/ppermute | solution.py:34
  42.6 19.5 %collective-permute-start.15 = (bf16[256,512]{1,0:T(8,128)(2,1)S(1)}, bf16[256,512]{1,0:T(8,128)(2,1)}, u32[]{:S(2)}, u32[]{:S(2)}) collective-permute-start(bf16[256,512]{1,0:T(8,128)(2,1)S(1)} %join.1.refs_2_), channel_id=1, source_target_pairs={{0,16},{8,56},{16,32},{24,8},{32,48},{40,24},{48,0},{56,40},{64,80... | collective-permute-start | bytes 786440 | tf_op jit(solution)/shard_map/ppermute | solution.py:30
  45.5 17.2 %collective-permute-start.9 = (bf16[256,512]{1,0:T(8,128)(2,1)S(1)}, bf16[256,512]{1,0:T(8,128)(2,1)S(1)}, u32[]{:S(2)}, u32[]{:S(2)}) collective-permute-start(bf16[256,512]{1,0:T(8,128)(2,1)S(1)} %collective-permute-done.6.refs_2_.refs_0_), channel_id=1, source_target_pairs={{0,8},{8,0},{16,24},{24,16},{32,40},{40,32},{48,56},{56,48},{64,72... | collective-permute-start | bytes 786440 | tf_op jit(solution)/shard_map/ppermute | solution.py:34
  48.0 15.1 %collective-permute-start.7 = (bf16[256,512]{1,0:T(8,128)(2,1)S(1)}, bf16[256,512]{1,0:T(8,128)(2,1)S(1)}, u32[]{:S(2)}, u32[]{:S(2)}) collective-permute-start(bf16[256,512]{1,0:T(8,128)(2,1)S(1)} %collective-permute-done.6.refs_2_.refs_0_), channel_id=1, source_target_pairs={{0,64},{8,72},{16,80},{24,88},{32,96},{40,104},{48,112},{56,120},{... | collective-permute-start | bytes 786440 | tf_op jit(solution)/shard_map/ppermute | solution.py:38
  51.3 19.9 %collective-permute-start.23 = (bf16[512,512]{1,0:T(8,128)(2,1)}, bf16[512,512]{1,0:T(8,128)(2,1)}, u32[]{:S(2)}, u32[]{:S(2)}) collective-permute-start(bf16[512,512]{1,0:T(8,128)(2,1)} %pad_maximum_fusion.2), channel_id=1, source_target_pairs={{0,16},{8,56},{16,32},{24,8},{32,48},{40,24},{48,0},{56,40},{64,80... | collective-permute-start | bytes 1572872 | tf_op jit(solution)/shard_map/ppermute | solution.py:30
  62.1 17.7 %collective-permute-start.3 = (bf16[512,512]{1,0:T(8,128)(2,1)S(1)}, bf16[512,512]{1,0:T(8,128)(2,1)S(1)}, u32[]{:S(2)}, u32[]{:S(2)}) collective-permute-start(bf16[512,512]{1,0:T(8,128)(2,1)S(1)} %collective-permute-done.2.refs_0_), channel_id=1, source_target_pairs={{0,8},{8,0},{16,24},{24,16},{32,40},{40,32},{48,56},{56,48},{64,72... | collective-permute-start | bytes 1572872 | tf_op jit(solution)/shard_map/ppermute | solution.py:34
  62.5 5.7 %collective-permute-start.27 = (bf16[256,512]{1,0:T(8,128)(2,1)}, bf16[256,512]{1,0:T(8,128)(2,1)S(1)}, u32[]{:S(2)}, u32[]{:S(2)}) collective-permute-start(bf16[256,512]{1,0:T(8,128)(2,1)} %collective-permute-done.22.refs_7_), channel_id=1, source_target_pairs={{0,8},{8,0},{16,24},{24,16},{32,40},{40,32},{48,56},{56,48},{64,72... | collective-permute-start | bytes 786440 | tf_op jit(solution)/shard_map/ppermute | solution.py:34
  62.7 12.3 %collective-permute-start.26 = (bf16[256,512]{1,0:T(8,128)(2,1)}, bf16[256,512]{1,0:T(8,128)(2,1)S(1)}, u32[]{:S(2)}, u32[]{:S(2)}) collective-permute-start(bf16[256,512]{1,0:T(8,128)(2,1)} %collective-permute-done.15.refs_6_), channel_id=1, source_target_pairs={{0,8},{8,0},{16,24},{24,16},{32,40},{40,32},{48,56},{56,48},{64,72... | collective-permute-start | bytes 786440 | tf_op jit(solution)/shard_map/ppermute | solution.py:34
  63.1 6.6 %collective-permute-start.16 = (bf16[256,512]{1,0:T(8,128)(2,1)}, bf16[256,512]{1,0:T(8,128)(2,1)S(1)}, u32[]{:S(2)}, u32[]{:S(2)}) collective-permute-start(bf16[256,512]{1,0:T(8,128)(2,1)} %collective-permute-done.15.refs_6_), channel_id=1, source_target_pairs={{0,16},{8,56},{16,32},{24,8},{32,48},{40,24},{48,0},{56,40},{64,80... | collective-permute-start | bytes 786440 | tf_op jit(solution)/shard_map/ppermute | solution.py:30
  66.1 9.0 %copy-start.3 = (bf16[256,512]{1,0:T(8,128)(2,1)S(1)}, bf16[256,512]{1,0:T(8,128)(2,1)}, u32[]{:S(2)}) copy-start(bf16[256,512]{1,0:T(8,128)(2,1)} %copy-done.2) | copy-start | bytes 786436
  66.1 9.0 %copy-start.4 = (bf16[256,512]{1,0:T(8,128)(2,1)S(1)}, bf16[256,512]{1,0:T(8,128)(2,1)}, u32[]{:S(2)}) copy-start(bf16[256,512]{1,0:T(8,128)(2,1)} %get-tuple-element.61.refs_1_) | copy-start | bytes 786436
  66.1 9.0 %copy-start.6 = (bf16[256,512]{1,0:T(8,128)(2,1)S(1)}, bf16[256,512]{1,0:T(8,128)(2,1)}, u32[]{:S(2)}) copy-start(bf16[256,512]{1,0:T(8,128)(2,1)} %copy-done.5) | copy-start | bytes 786436
  68.2 11.6 %collective-permute-start.8 = (bf16[256,512]{1,0:T(8,128)(2,1)S(1)}, bf16[256,512]{1,0:T(8,128)(2,1)S(1)}, u32[]{:S(2)}, u32[]{:S(2)}) collective-permute-start(bf16[256,512]{1,0:T(8,128)(2,1)S(1)} %collective-permute-done.7.refs_2_.refs_0_), channel_id=1, source_target_pairs={{0,8},{8,0},{16,24},{24,16},{32,40},{40,32},{48,56},{56,48},{64,72... | collective-permute-start | bytes 786440 | tf_op jit(solution)/shard_map/ppermute | solution.py:34
  69.6 9.4 %collective-permute-start.17 = (bf16[256,512]{1,0:T(8,128)(2,1)S(1)}, bf16[256,512]{1,0:T(8,128)(2,1)S(1)}, u32[]{:S(2)}, u32[]{:S(2)}) collective-permute-start(bf16[256,512]{1,0:T(8,128)(2,1)S(1)} %collective-permute-done.16.refs_2_), channel_id=1, source_target_pairs={{0,64},{8,72},{16,80},{24,88},{32,96},{40,104},{48,112},{56,120},{... | collective-permute-start | bytes 786440 | tf_op jit(solution)/shard_map/ppermute | solution.py:38
  71.2 13.1 %collective-permute-start.24 = (bf16[512,512]{1,0:T(8,128)(2,1)}, bf16[512,512]{1,0:T(8,128)(2,1)S(1)}, u32[]{:S(2)}, u32[]{:S(2)}) collective-permute-start(bf16[512,512]{1,0:T(8,128)(2,1)} %collective-permute-done.23.refs_2_), channel_id=1, source_target_pairs={{0,8},{8,0},{16,24},{24,16},{32,40},{40,32},{48,56},{56,48},{64,72... | collective-permute-start | bytes 1572872 | tf_op jit(solution)/shard_map/ppermute | solution.py:34
  75.0 7.6 %collective-permute-start.25 = (bf16[256,512]{1,0:T(8,128)(2,1)S(1)}, bf16[256,512]{1,0:T(8,128)(2,1)S(1)}, u32[]{:S(2)}, u32[]{:S(2)}) collective-permute-start(bf16[256,512]{1,0:T(8,128)(2,1)S(1)} %collective-permute-done.16.refs_2_), channel_id=1, source_target_pairs={{0,8},{8,0},{16,24},{24,16},{32,40},{40,32},{48,56},{56,48},{64,72... | collective-permute-start | bytes 786440 | tf_op jit(solution)/shard_map/ppermute | solution.py:34
  79.0 8.3 %collective-permute-start.18 = (bf16[256,512]{1,0:T(8,128)(2,1)S(1)}, bf16[256,512]{1,0:T(8,128)(2,1)S(1)}, u32[]{:S(2)}, u32[]{:S(2)}) collective-permute-start(bf16[256,512]{1,0:T(8,128)(2,1)S(1)} %collective-permute-done.17.refs_2_), channel_id=1, source_target_pairs={{0,8},{8,0},{16,24},{24,16},{32,40},{40,32},{48,56},{56,48},{64,72... | collective-permute-start | bytes 786440 | tf_op jit(solution)/shard_map/ppermute | solution.py:34
  (10 other events, 46.6 us)

commit v2 on v0

v2 whole, which is shorter than its diff:
```python
import jax
import jax.numpy as jnp
from jax import lax
from jax.experimental import pallas as pl
from jax.experimental.pallas import tpu as pltpu
from jax.sharding import PartitionSpec as P

F32, BF16 = jnp.float32, jnp.bfloat16
ANY = pl.BlockSpec(memory_space=pltpu.HBM)
VM = pl.BlockSpec(memory_space=pltpu.VMEM)
SM = pl.BlockSpec(memory_space=pltpu.SMEM)
NT = (((1,), (1,)), ((), ()))
TN = 512
MIB = 1 << 20

ROWS = [(yh, x, c) for yh in range(2) for x in range(4) for c in range(2)]
ADS = [(z, yl) for z in range(4) for yl in range(2)]


def row_of(yh, x, c):
    return (yh * 4 + x) * 2 + c


RING = [(row_of(yh, x, c), row_of(yh, (x + 1 - 2 * c) % 4, c)) for yh, x, c in ROWS]
CORE = [(row_of(yh, x, c), row_of(yh, x, 1 - c)) for yh, x, c in ROWS]
PAIR = [(row_of(yh, x, c), row_of(1 - yh, x, c)) for yh, x, c in ROWS]
YLO = [(z * 2 + yl, z * 2 + 1 - yl) for z, yl in ADS]


def ring(a):
    return lax.ppermute(a, "row", RING)


def core(a):
    return lax.ppermute(a, "row", CORE)


def pair(a):
    return lax.ppermute(a, "row", PAIR)


def ylo(a):
    return lax.ppermute(a, "ad", YLO)


def zshift(a, step):
    return lax.ppermute(a, "ad", [(z * 2 + yl, (z + step) % 4 * 2 + yl) for z, yl in ADS])


class Line:
    def __init__(self):
        self.done = ()

    def after(self, a):
        return lax.optimization_barrier((a, *self.done))[0] if self.done else a

    def send(self, how, a):
        return how(self.after(a))

    def got(self, *values):
        self.done += values

    def ran(self, value):
        self.done = (value,)


def cat(*parts):
    return jnp.concatenate(parts, 0)


def cost():
    return pl.CostEstimate(flops=1024, bytes_accessed=1024, transcendentals=0)


def call(body, name, inputs, specs, outs, scratch=(), aliases=None, limit=8 * MIB, out_specs=None):
    return pl.pallas_call(
        body,
        out_shape=outs,
        in_specs=specs,
        out_specs=out_specs or [VM] * len(outs),
        scratch_shapes=list(scratch),
        input_output_aliases=aliases or {},
        name=name,
        cost_estimate=cost(),
        compiler_params=pltpu.CompilerParams(vmem_limit_bytes=limit),
    )(*inputs)


def pack_body(pos_ref, d_ref, mine_ref, send_ref):
    z, yl = pos_ref[0], pos_ref[1]
    for out_ref, lane in ((mine_ref, yl), (send_ref, 1 - yl)):
        for j in range(4):
            group = lax.rem(z + j, 4) * 2 + lane
            four = d_ref[pl.ds(group * 4, 4)]
            out_ref[j] = jnp.concatenate([four[a] for a in range(4)], axis=1)


def pack(pos, panel):
    d, r = panel.shape[1:]
    shape = jax.ShapeDtypeStruct((4, d, 4 * r), BF16)
    return call(pack_body, "pack", (pos, panel), [SM, VM], [shape, shape])


def join_body(pos_ref, a0, a1, a2, a3, out_ref, full):
    z, yl = pos_ref[0], pos_ref[1]
    d = a0.shape[1]
    for ref, back in ((a0, 0), (a1, 3), (a2, 2), (a3, 1)):
        src = lax.rem(z + back, 4) * 2
        full[pl.ds(pl.multiple_of((src + yl) * d, d), d), :] = ref[0]
        full[pl.ds(pl.multiple_of((src + 1 - yl) * d, d), d), :] = ref[1]
    out_ref[...] = full[...].T


def join(pos, *pieces):
    _, d, width = pieces[0].shape
    outs = [jax.ShapeDtypeStruct((width, 8 * d), BF16)]
    scratch = [pltpu.VMEM((8 * d, width), BF16)]
    return call(join_body, "join", (pos, *pieces), [SM] + [VM] * 4, outs, scratch)[0]


OWN = ((0, 0, 0), (0, 0, 1))
BEHIND = ((0, -1, 0), (0, -1, 1))
AHEAD = ((0, 1, 1), (0, 1, 0))
FAR = ((0, 2, 0), (0, 2, 1))


def mirrored(places):
    return tuple((1 - dy, dx, dc) for dy, dx, dc in places)


def weight_row(pos_ref, place, depth):
    dy, dx, dc = place
    c, x, yh = pos_ref[2], pos_ref[3], pos_ref[4]
    side = lax.rem(x + dx * (1 - 2 * c) + 4, 4)
    block = (lax.rem(yh + dy, 2) * 4 + side) * 2 + lax.rem(c + dc, 2)
    return pl.multiple_of(block * depth, depth)


def view(ref, h):
    return ref[h * 256 : (h + 1) * 256, :]


class Operands:
    def __init__(self):
        self.arrays = []

    def add(self, block):
        array, h = block if isinstance(block, tuple) else (block, 0)
        for i, known in enumerate(self.arrays):
            if known is array:
                return i, h
        self.arrays.append(array)
        return len(self.arrays) - 1, h


def squared(w):
    wide = w.astype(F32)
    return jnp.sum((wide * wide).reshape(w.shape[0] // 8, 8, w.shape[1]), axis=0)


def plus(a, b):
    return b if a is None else a + b


def tiles(cols):
    return [slice(lo, lo + TN) for lo in range(0, cols, TN)]


def nt(a, b):
    return lax.dot_general(a, b, NT, preferred_element_type=F32)


def spread_and_gram(refs, pans, spread, gram):
    for _, (i, g), (k, h) in pans:
        d = view(refs[k], h)
        spread = plus(spread, nt(view(refs[i], g), d))
        gram = plus(gram, nt(d, d))
    return spread, gram


def accumulators(cols, with_base, with_norm):
    shapes = [(256, cols), (8, cols)] * with_base + [(256, cols), (512, 256)] * with_norm
    return [jax.ShapeDtypeStruct(shape, F32) for shape in shapes]


def first_step(pos, both, toks, weight):
    ops = Operands()
    both = [(p, ops.add(t), ops.add(d)) for p, t, d in both]
    toks = [(p, ops.add(t)) for p, t in toks]
    count = len(ops.arrays)
    rows, cols = weight.shape
    depth = ops.arrays[0].shape[1]
    order = [item[0] for item in both + toks]
    order += [p for p in OWN + BEHIND + AHEAD + FAR if p not in order]
    order += mirrored(OWN + BEHIND + AHEAD + FAR)

    def body(pos_ref, *refs):
        hbm = refs[count]
        w_ref, base_out, sq_out, cross_out, both_out, sems = refs[count + 1 :]
        starts, copies = [], []
        for i, p in enumerate(order):
            starts.append(weight_row(pos_ref, p, depth))
            at = pl.ds(starts[i], depth)
            copies.append(pltpu.make_async_copy(hbm.at[at, :], w_ref.at[at, :], sems.at[i]))
            copies[i].start()
        spread, gram = spread_and_gram(refs, both, None, None)
        both_out[:256, :], both_out[256:, :] = spread, gram
        for i, item in enumerate(both + toks):
            copies[i].wait()
            for tile in tiles(cols):
                w = w_ref[pl.ds(starts[i], depth), tile]
                left = jnp.concatenate([view(refs[a], h) for a, h in item[1:]], axis=0)
                part = jnp.dot(left, w, preferred_element_type=F32)
                base, sq = part[:256], squared(w)
                base_out[:, tile] = base if i == 0 else base_out[:, tile] + base
                sq_out[:, tile] = sq if i == 0 else sq_out[:, tile] + sq
                if i < len(both):
                    cross = part[256:]
                    cross_out[:, tile] = cross if i == 0 else cross_out[:, tile] + cross
        for i in range(len(both + toks), len(order)):
            copies[i].wait()

    return call(
        body,
        "first",
        (pos, *ops.arrays, weight),
        [SM] + [VM] * count + [ANY],
        [jax.ShapeDtypeStruct((rows, cols), BF16)] + accumulators(cols, True, True),
        [pltpu.SemaphoreType.DMA((len(order),))],
        limit=30 * MIB,
    )


def step(name, pos, toks, pans, weight, base, norm):
    ops = Operands()
    toks = [(p, ops.add(t)) for p, t in toks]
    pans = [(p, ops.add(t), ops.add(d)) for p, t, d in pans]
    count = len(ops.arrays)
    depth, cols = ops.arrays[0].shape[1], weight.shape[1]
    state = (list(base) if toks else []) + (list(norm) if pans else [])
    n = len(state)

    def body(pos_ref, *refs):
        w_ref = refs[count]
        ins, outs = refs[count + 1 : count + 1 + n], refs[count + 1 + n :]
        if pans:
            spread, gram = spread_and_gram(refs, pans, ins[-1][:256, :], ins[-1][256:, :])
            outs[-1][:256, :], outs[-1][256:, :] = spread, gram
        tok_rows = [weight_row(pos_ref, item[0], depth) for item in toks]
        pan_rows = [weight_row(pos_ref, item[0], depth) for item in pans]
        for tile in tiles(cols):
            if toks:
                total, sq = ins[0][:, tile], ins[1][:, tile]
                for row, (_, (a, h)) in zip(tok_rows, toks):
                    w = w_ref[pl.ds(row, depth), tile]
                    total = total + jnp.dot(view(refs[a], h), w, preferred_element_type=F32)
                    sq = sq + squared(w)
                outs[0][:, tile], outs[1][:, tile] = total, sq
            if pans:
                total = ins[-2][:, tile]
                for row, (_, _, (a, h)) in zip(pan_rows, pans):
                    w = w_ref[pl.ds(row, depth), tile]
                    total = total + jnp.dot(view(refs[a], h), w, preferred_element_type=F32)
                outs[-2][:, tile] = total

    new = call(
        body,
        name,
        (pos, *ops.arrays, weight, *state),
        [SM] + [VM] * (count + 1 + n),
        accumulators(cols, bool(toks), bool(pans)),
        aliases={count + 2 + i: i for i in range(n)},
    )
    return (new[:2] if toks else base), (new[-2:] if pans else norm)


def last_step(pos, both, pans, weight, base, norm, up, mag, ids):
    ops = Operands()
    both, pans = ([(p, ops.add(t), ops.add(d)) for p, t, d in work] for work in (both, pans))
    count = len(ops.arrays)
    depth, cols = ops.arrays[0].shape[1], weight.shape[1]
    adapters, width, tokens = mag.shape[0], up.shape[0], base[0].shape[0]
    rank = width // adapters

    def body(pos_ref, *refs):
        w_ref, base_ref, sq_ref, cross_ref, both_ref, up_ref, mag_ref, id_ref = refs[count : count + 8]
        out_ref, held, sems = refs[count + 8 :]
        spread, gram = spread_and_gram(refs, both + pans, both_ref[:tokens, :], both_ref[tokens:, :])
        both_rows = [weight_row(pos_ref, item[0], depth) for item in both]
        rows = [weight_row(pos_ref, item[0], depth) for item in pans]
        local = id_ref[...] - (pos_ref[0] * 2 + pos_ref[1]) * adapters
        own = jnp.broadcast_to(local, (128, tokens)).T
        lane = lax.broadcasted_iota(jnp.int32, (tokens, width), 1) // rank
        own_wide = jnp.concatenate([own] * (width // 128), axis=1)
        low = jnp.where(lane == own_wide, spread, 0.0).astype(BF16)
        line = lax.broadcasted_iota(jnp.int32, (width, width), 0) // rank
        side = lax.broadcasted_iota(jnp.int32, (width, width), 1) // rank
        gram = jnp.where(line == side, gram, 0.0)
        gram_hi = gram.astype(BF16)
        gram_lo = (gram - gram_hi.astype(F32)).astype(BF16)
        left = jnp.concatenate([low, gram_hi, gram_lo], axis=0)
        own_tile = jnp.concatenate([own] * (TN // 128), axis=1)
        copies = []
        for n, tile in enumerate(tiles(cols)):
            base, sq, cross = base_ref[:, tile], sq_ref[:, tile], cross_ref[:, tile]
            for row, item in zip(both_rows, both):
                w = w_ref[pl.ds(row, depth), tile]
                pair_of = jnp.concatenate([view(refs[a], h) for a, h in item[1:]], axis=0)
                part = jnp.dot(pair_of, w, preferred_element_type=F32)
                base, cross, sq = base + part[:tokens], cross + part[tokens:], sq + squared(w)
            for row, (_, _, (a, h)) in zip(rows, pans):
                w = w_ref[pl.ds(row, depth), tile]
                cross = cross + jnp.dot(view(refs[a], h), w, preferred_element_type=F32)
            up_tile = up_ref[:, tile]
            prod = jnp.dot(left, up_tile, preferred_element_type=F32)
            bent = prod[tokens : tokens + width] + prod[tokens + width :]
            terms = up_tile.astype(F32) * (2.0 * cross + bent)
            weight_sq = jnp.sum(sq, axis=0, keepdims=True)
            scale = None
            for a in range(adapters):
                mine = jnp.sum(terms[a * rank : (a + 1) * rank], axis=0, keepdims=True)
                gain = mag_ref[a : a + 1, tile] / jnp.sqrt(weight_sq + mine + 1e-6)
                wide = jnp.broadcast_to(gain, (tokens, TN))
                scale = wide if scale is None else jnp.where(own_tile == a, wide, scale)
            held[n] = (scale * (base + prod[:tokens])).astype(BF16)
            copies.append(pltpu.make_async_copy(held.at[n], out_ref.at[:, tile], sems.at[n]))
            copies[n].start()
        for copy in copies:
            copy.wait()

    inputs = (pos, *ops.arrays, weight, *base, *norm, up, mag, ids)
    outs = [jax.ShapeDtypeStruct((tokens, cols), BF16)]
    scratch = [pltpu.VMEM((cols // TN, tokens, TN), BF16), pltpu.SemaphoreType.DMA((cols // TN,))]
    return call(body, "last", inputs, [SM] + [VM] * (count + 8), outs, scratch, out_specs=[ANY])[0]


def on_device(tokens, token_adapter, base_weight, panel_down, panel_up, magnitude):
    adapters, rank, cols = panel_up.shape
    row = lax.axis_index("row").astype(jnp.int32)
    ad = lax.axis_index("ad").astype(jnp.int32)
    pos = jnp.stack([ad // 2, ad % 2, row % 2, row // 2 % 4, row // 8])
    up = panel_up.reshape(adapters * rank, cols)

    line = Line()
    line.ran(pos)
    tc = line.send(core, tokens)
    tr = line.send(ring, tokens)
    mine, away = pack(line.after(pos), panel_down)
    line.ran(away)
    line.got(tc)

    got = line.send(ylo, away)
    tr2 = line.send(ring, tc)
    tp = line.send(pair, tokens)
    t = line.send(core, tc)
    line.got(got, tr, t)

    z1 = line.send(lambda a: zshift(a, 1), jnp.stack([mine[1], got[1]]))
    z3 = line.send(lambda a: zshift(a, -1), jnp.stack([mine[3], got[3]]))
    z2 = line.send(lambda a: zshift(a, 2), jnp.stack([mine[2], got[2]]))
    line.got(z1, z3, z2, tr2, tp)
    d = join(line.after(pos), jnp.stack([mine[0], got[0]]), z1, z2, z3)
    line.ran(d)

    dr = line.send(ring, d)
    dc = line.send(core, d)
    dp = line.send(pair, d)
    tpc = line.send(core, tp)
    trc = line.send(core, cat(tr, tr2))
    line.got(dc, trc, tpc)
    dr2 = line.send(ring, dc)
    tf = line.send(ring, tr)
    tpr = line.send(ring, cat(tp, tpc))
    w, *sums = first_step(
        line.after(pos),
        list(zip(OWN, [t, tc], [d, dc])),
        list(zip(BEHIND + AHEAD, [tr, tr2, (trc, 0), (trc, 1)])),
        base_weight,
    )
    base, norm = sums[:2], sums[2:]
    line.ran(norm[1])
    line.got(dr, dr2, dp, tf)

    df = line.send(ring, dr)
    tfp = line.send(pair, tf)
    dpc = line.send(core, dp)
    drc = line.send(core, cat(dr, dr2))
    base, norm = step(
        "mid_a",
        line.after(pos),
        list(zip(mirrored(OWN), [tp, tpc])),
        list(zip(BEHIND, [tr, tr2], [dr, dr2])),
        w,
        base,
        norm,
    )
    line.ran(norm[1])
    line.got(df, dpc, drc, tpr, tfp)

    dpr = line.send(ring, cat(dp, dpc))
    dfp = line.send(pair, df)
    tprc = line.send(core, tpr)
    tfc = line.send(core, tf)
    tfpc = line.send(core, tfp)
    base, norm = step(
        "mid_b",
        line.after(pos),
        list(zip(mirrored(BEHIND), [(tpr, 0), (tpr, 1)])),
        list(zip(AHEAD + mirrored(OWN), [(trc, 0), (trc, 1), tp, tpc], [(drc, 0), (drc, 1), dp, dpc])),
        w,
        base,
        norm,
    )
    line.ran(norm[1])
    line.got(tprc, tfc, tfpc, dpr, dfp)

    dprc = line.send(core, dpr)
    dfpc = line.send(core, dfp)
    dfc = line.send(core, df)
    base, norm = step(
        "mid_c", line.after(pos), list(zip(FAR + mirrored(AHEAD), [tf, tfc, (tprc, 0), (tprc, 1)])), [], w, base, norm
    )
    line.ran(base[1])
    line.got(dfpc, dprc, dfc)
    ring_t = [(tpr, 0), (tpr, 1), (tprc, 0), (tprc, 1)]
    ring_d = [(dpr, 0), (dpr, 1), (dprc, 0), (dprc, 1)]
    return last_step(
        line.after(pos),
        list(zip(mirrored(FAR), [tfp, tfpc], [dfp, dfpc])),
        list(zip(FAR + mirrored(BEHIND + AHEAD), [tf, tfc] + ring_t, [df, dfc] + ring_d)),
        w,
        base,
        norm,
        up,
        magnitude,
        token_adapter[None, :],
    )


def solution(mesh):
    placed = (
        P("ad", "row"),
        P("ad"),
        P(None, "row"),
        P(None, ("row", "ad"), None),
        P("ad", None, "row"),
        P("ad", "row"),
    )
    return jax.shard_map(on_device, mesh=mesh, in_specs=placed, out_specs=P("ad", "row"), check_vma=False)
```

time: 163 us -> 70 us (0.43)
  blocking collectives: 77.5 us -> 0 us
  matrix products: 38.4 us -> 0 us
  starting transfers between devices: 0.04 us -> 30.6 us
  Pallas kernels: 0 us -> 21.5 us
  other arithmetic: 15.3 us -> 0.17 us
  between operations: 13.7 us -> 0.42 us
  local copies, waits for them, and re-layouts: 5.25 us -> 1.15 us
  waiting for transfers between devices: 12.2 us -> 16 us
    psum x1 -> x0, blocking collectives: 64.6 us -> none  [on_device(): low_sum = lax.psum(low_part, 'row')]
    dot_general x19 -> x0, matrix products: 38.1 us -> none  [the longest x16 23.6 us: on_device(): jnp.einsum('akr,arf->akf', shard_piece[:, offset:offset + block_rows], pa...]
    ppermute x0 -> x29, starting transfers between devices: none -> 30.6 us  [the longest x13 8.88 us: core(): return lax.ppermute(a, 'row', CORE)]
    pallas_call x0 -> x7, Pallas kernels: none -> 21.5 us  [call(): pl.pallas_call(body, out_shape=outs, in_specs=specs, out_specs=out_specs...]
    ppermute x0 -> x29, waiting for transfers between devices: none -> 16 us  [the longest x4 13.4 us: pair(): return lax.ppermute(a, 'row', PAIR)]
    convert_element_type x2 -> x0, other arithmetic: 15.3 us -> none  [the longest x1 15.3 us: on_device(): lax.dynamic_slice_in_dim(base_weight, offset, block_rows, 0)]
    all_to_all x1 -> x0, blocking collectives: 12.9 us -> none  [on_device(): lax.all_to_all(panel_down, 'ad', split_axis=0, concat_axis=1, tiled=True)]
    all_gather x2 -> x0, waiting for transfers between devices: 11.5 us -> none  [the longest x1 11.5 us: on_device(): lax.all_gather(tokens, 'row', axis=1, tiled=True)]
  transfers between devices with their start and end apart: 2 -> 29, of which waited for: 1 -> 7; matrix products, arithmetic and copies ran while one was open for 25% -> 0% of each run, Pallas kernels for 0% -> 21%
where the time goes in v2:
time: 70 us; the launch traced here: 69.9 us
  starting transfers between devices  30.6 us (44%)
  Pallas kernels  21.5 us (31%)
  waiting for transfers between devices  16 us (23%)
  local copies, waits for them, and re-layouts  1.15 us (2%)
    pallas_call x7, Pallas kernels, call(): pl.pallas_call(body, out_shape=outs, in_specs=specs, out_specs=out_specs...  21.5 us
    ppermute x4, waiting for transfers between devices, pair(): return lax.ppermute(a, 'row', PAIR)  13.4 us
    ppermute x13, starting transfers between devices, core(): return lax.ppermute(a, 'row', CORE)  8.88 us
    ppermute x8, starting transfers between devices, ring(): return lax.ppermute(a, 'row', RING)  8.79 us
    ppermute x4, starting transfers between devices, pair(): return lax.ppermute(a, 'row', PAIR)  6.43 us
    ppermute x3, starting transfers between devices, zshift(): lax.ppermute(a, 'ad', [(z * 2 + yl, (z + step) % 4 * 2 + yl) for z, yl in...  5.13 us
    ppermute x8, waiting for transfers between devices, ring(): return lax.ppermute(a, 'row', RING)  1.58 us
  transfers between devices with their start and end apart: 29, of which 7 were waited for; matrix products, arithmetic and copies ran while one was open for 0% of the time, Pallas kernels for 21%

profile of v2, /device:TPU:1, one launch (start us, length us, event | category | flops | bytes accessed | tf_op | source)
XLA Modules:
  0.0 69.9 jit_solution(10876911993350917142)
XLA Ops:
  0.1 1.4 %collective-permute-start = (bf16[256,512]{1,0:T(8,128)(2,1)}, bf16[256,512]{1,0:T(8,128)(2,1)S(1)}, u32[]{:S(2)}, u32[]{:S(2)}) collective-permute-start(bf16[256,512]{1,0:T(8,128)(2,1)} %param.6), channel_id=1, source_target_pairs={{0,8},{8,0},{16,24},{24,16},{32,40},{40,32},{48,56},{56,48},{64,72... | collective-permute-start | bytes 786440 | tf_op jit(solution)/shard_map/ppermute | solution.py:35
  1.5 2.6 %collective-permute-start.2 = (bf16[256,512]{1,0:T(8,128)(2,1)}, bf16[256,512]{1,0:T(8,128)(2,1)S(1)}, u32[]{:S(2)}, u32[]{:S(2)}) collective-permute-start(bf16[256,512]{1,0:T(8,128)(2,1)} %param.6), channel_id=1, source_target_pairs={{0,16},{8,56},{16,32},{24,8},{32,48},{40,24},{48,0},{56,40},{64,80... | collective-permute-start | bytes 786440 | tf_op jit(solution)/shard_map/ppermute | solution.py:31
  4.1 1.0 %copy-done.1 = bf16[32,64,64]{2,1,0:T(8,128)(2,1)S(1)} copy-done((bf16[32,64,64]{2,1,0:T(8,128)(2,1)S(1)}, bf16[32,64,64]{2,1,0:T(8,128)(2,1)}, u32[]{:S(2)}) %copy-start.1) | copy-done | bytes 262168
  5.1 0.7 pack.1
  5.8 1.4 %collective-permute-start.1 = (bf16[4,64,256]{2,1,0:T(8,128)(2,1)S(1)}, bf16[4,64,256]{2,1,0:T(8,128)(2,1)S(1)}, u32[]{:S(2)}, u32[]{:S(2)}) collective-permute-start(bf16[4,64,256]{2,1,0:T(8,128)(2,1)S(1)} %get-tuple-element.57), channel_id=1, source_target_pairs={{0,1},{1,0},{2,3},{3,2},{4,5},{5,4},{6,7},{7,6},{8,9},{9,8},{10,11... | collective-permute-start | bytes 393224 | tf_op jit(solution)/shard_map/ppermute | solution.py:43
  7.2 0.6 collective-permute-start.7
  8.1 2.6 %collective-permute-start.8 = (bf16[256,512]{1,0:T(8,128)(2,1)}, bf16[256,512]{1,0:T(8,128)(2,1)S(1)}, u32[]{:S(2)}, u32[]{:S(2)}) collective-permute-start(bf16[256,512]{1,0:T(8,128)(2,1)} %param.6), channel_id=1, source_target_pairs={{0,64},{8,72},{16,80},{24,88},{32,96},{40,104},{48,112},{56,120},{... | collective-permute-start | bytes 786440 | tf_op jit(solution)/shard_map/ppermute | solution.py:39
  10.9 1.7 %collective-permute-start.4 = (bf16[2,64,256]{2,1,0:T(8,128)(2,1)S(1)}, bf16[2,64,256]{2,1,0:T(8,128)(2,1)S(1)}, u32[]{:S(2)}, u32[]{:S(2)}) collective-permute-start(bf16[2,64,256]{2,1,0:T(8,128)(2,1)S(1)} %get-tuple-element.60), channel_id=1, source_target_pairs={{0,2},{1,3},{2,4},{3,5},{4,6},{5,7},{6,0},{7,1},{8,10},{9,11},{10,... | collective-permute-start | bytes 196616 | tf_op jit(solution)/shard_map/ppermute | solution.py:47
  12.6 2.2 %collective-permute-start.5 = (bf16[2,64,256]{2,1,0:T(8,128)(2,1)S(1)}, bf16[2,64,256]{2,1,0:T(8,128)(2,1)S(1)}, u32[]{:S(2)}, u32[]{:S(2)}) collective-permute-start(bf16[2,64,256]{2,1,0:T(8,128)(2,1)S(1)} %get-tuple-element.61), channel_id=1, source_target_pairs={{0,6},{1,7},{2,0},{3,1},{4,2},{5,3},{6,4},{7,5},{8,14},{9,15},{10,... | collective-permute-start | bytes 196616 | tf_op jit(solution)/shard_map/ppermute | solution.py:47
  14.8 1.2 %collective-permute-start.6 = (bf16[2,64,256]{2,1,0:T(8,128)(2,1)S(1)}, bf16[2,64,256]{2,1,0:T(8,128)(2,1)S(1)}, u32[]{:S(2)}, u32[]{:S(2)}) collective-permute-start(bf16[2,64,256]{2,1,0:T(8,128)(2,1)S(1)} %pad_maximum_fusion.6), channel_id=1, source_target_pairs={{0,4},{1,5},{2,6},{3,7},{4,0},{5,1},{6,2},{7,3},{8,12},{9,13},{10,... | collective-permute-start | bytes 196616 | tf_op jit(solution)/shard_map/ppermute | solution.py:47
  16.0 2.9 %collective-permute-done.8.refs_0_.refs_3_ = bf16[256,512]{1,0:T(8,128)(2,1)S(1)} collective-permute-done((bf16[256,512]{1,0:T(8,128)(2,1)}, bf16[256,512]{1,0:T(8,128)(2,1)S(1)}, u32[]{:S(2)}, u32[]{:S(2)}) %collective-permute-start.8) | collective-permute-done | bytes 262176 | tf_op jit(solution)/shard_map/ppermute | solution.py:39
  18.9 0.5 collective-permute-done.6.a2
  19.4 0.7 join.1.refs_1_
  20.1 2.0 %collective-permute-start.10 = (bf16[512,512]{1,0:T(8,128)(2,1)S(1)}, bf16[512,512]{1,0:T(8,128)(2,1)S(1)}, u32[]{:S(2)}, u32[]{:S(2)}) collective-permute-start(bf16[512,512]{1,0:T(8,128)(2,1)S(1)} %pad_maximum_fusion), channel_id=1, source_target_pairs={{0,8},{8,0},{16,24},{24,16},{32,40},{40,32},{48,56},{56,48},{64,72... | collective-permute-start | bytes 1572872 | tf_op jit(solution)/shard_map/ppermute | solution.py:35
  22.6 1.3 %collective-permute-start.12 = (bf16[256,512]{1,0:T(8,128)(2,1)S(1)}, bf16[256,512]{1,0:T(8,128)(2,1)S(1)}, u32[]{:S(2)}, u32[]{:S(2)}) collective-permute-start(bf16[256,512]{1,0:T(8,128)(2,1)S(1)} %join.1.refs_1_), channel_id=1, source_target_pairs={{0,16},{8,56},{16,32},{24,8},{32,48},{40,24},{48,0},{56,40},{64,80... | collective-permute-start | bytes 786440 | tf_op jit(solution)/shard_map/ppermute | solution.py:31
  24.3 1.3 %collective-permute-start.13 = (bf16[256,512]{1,0:T(8,128)(2,1)S(1)}, bf16[256,512]{1,0:T(8,128)(2,1)S(1)}, u32[]{:S(2)}, u32[]{:S(2)}) collective-permute-start(bf16[256,512]{1,0:T(8,128)(2,1)S(1)} %collective-permute-done.9.refs_3_), channel_id=1, source_target_pairs={{0,16},{8,56},{16,32},{24,8},{32,48},{40,24},{48,0},{56,40},{64,80... | collective-permute-start | bytes 786440 | tf_op jit(solution)/shard_map/ppermute | solution.py:31
  25.6 2.8 %collective-permute-start.14 = (bf16[256,512]{1,0:T(8,128)(2,1)S(1)}, bf16[256,512]{1,0:T(8,128)(2,1)S(1)}, u32[]{:S(2)}, u32[]{:S(2)}) collective-permute-start(bf16[256,512]{1,0:T(8,128)(2,1)S(1)} %join.1.refs_1_), channel_id=1, source_target_pairs={{0,64},{8,72},{16,80},{24,88},{32,96},{40,104},{48,112},{56,120},{... | collective-permute-start | bytes 786440 | tf_op jit(solution)/shard_map/ppermute | solution.py:39
  28.9 0.5 collective-permute-start.19
  29.4 6.7 %first.1 = (bf16[8192,1024]{1,0:T(8,128)(2,1)S(1)}, f32[256,1024]{1,0:T(8,128)S(1)}, f32[8,1024]{1,0:T(8,128)S(1)}, f32[256,1024]{1,0:T(8,128)S(1)}, f32[512,256]{1,0:T(8,128)S(1)}) custom-call(s32[5]{0:T(128)S(1)} %stack.35.pos_ref, bf16[256,512]{1,0:T(8,128)(2,1)S(1)} %collective-permute-done.3.refs_0_, bf16[256,512]{1,0:T(8,128)(2,1)S(1)} %join.1.refs_1_, ...), custom_call_target="tpu_custom_call" | custom-call | flops 1024 | bytes 1024 | tf_op jit(solution)/shard_map/first/pallas_call | solution.py:76
  36.1 1.6 %collective-permute-start.18 = (bf16[512,512]{1,0:T(8,128)(2,1)S(1)}, bf16[512,512]{1,0:T(8,128)(2,1)S(1)}, u32[]{:S(2)}, u32[]{:S(2)}) collective-permute-start(bf16[512,512]{1,0:T(8,128)(2,1)S(1)} %pad_maximum_fusion.1), channel_id=1, source_target_pairs={{0,8},{8,0},{16,24},{24,16},{32,40},{40,32},{48,56},{56,48},{64,72... | collective-permute-start | bytes 1572872 | tf_op jit(solution)/shard_map/ppermute | solution.py:35
  37.8 1.7 %collective-permute-start.16 = (bf16[256,512]{1,0:T(8,128)(2,1)S(1)}, bf16[256,512]{1,0:T(8,128)(2,1)S(1)}, u32[]{:S(2)}, u32[]{:S(2)}) collective-permute-start(bf16[256,512]{1,0:T(8,128)(2,1)S(1)} %collective-permute-done.12.refs_3_), channel_id=1, source_target_pairs={{0,16},{8,56},{16,32},{24,8},{32,48},{40,24},{48,0},{56,40},{64,80... | collective-permute-start | bytes 786440 | tf_op jit(solution)/shard_map/ppermute | solution.py:31
  39.5 2.2 %mid_a.1 = (f32[256,1024]{1,0:T(8,128)S(1)}, f32[8,1024]{1,0:T(8,128)S(1)}, f32[256,1024]{1,0:T(8,128)S(1)}, f32[512,256]{1,0:T(8,128)S(1)}) custom-call(s32[5]{0:T(128)S(1)} %stack.35.pos_ref, bf16[256,512]{1,0:T(8,128)(2,1)S(1)} %collective-permute-done.8.refs_0_.refs_3_, ...), custom_call_target="tpu_custom_call", output_to_operand_aliasing={{0}: (8, {}), {1}: (9, {}), {2}: (10, {}), {3}: (11, {})} | custom-call | flops 1024 | bytes 1024 | tf_op jit(solution)/shard_map/mid_a/pallas_call | solution.py:76
  41.8 1.6 %collective-permute-done.16.refs_5_ = bf16[256,512]{1,0:T(8,128)(2,1)S(1)} collective-permute-done((bf16[256,512]{1,0:T(8,128)(2,1)S(1)}, bf16[256,512]{1,0:T(8,128)(2,1)S(1)}, u32[]{:S(2)}, u32[]{:S(2)}) %collective-permute-start.16) | collective-permute-done | bytes 262176 | tf_op jit(solution)/shard_map/ppermute | solution.py:31
  43.3 5.2 %collective-permute-done.20.refs_0_ = bf16[256,512]{1,0:T(8,128)(2,1)S(1)} collective-permute-done((bf16[256,512]{1,0:T(8,128)(2,1)S(1)}, bf16[256,512]{1,0:T(8,128)(2,1)S(1)}, u32[]{:S(2)}, u32[]{:S(2)}) %collective-permute-start.20) | collective-permute-done | bytes 262176 | tf_op jit(solution)/shard_map/ppermute | solution.py:39
  48.5 1.2 %collective-permute-start.21 = (bf16[512,512]{1,0:T(8,128)(2,1)S(1)}, bf16[512,512]{1,0:T(8,128)(2,1)S(1)}, u32[]{:S(2)}, u32[]{:S(2)}) collective-permute-start(bf16[512,512]{1,0:T(8,128)(2,1)S(1)} %collective-permute-done.19.refs_0_.refs_8_), channel_id=1, source_target_pairs={{0,8},{8,0},{16,24},{24,16},{32,40},{40,32},{48,56},{56,48},{64,72... | collective-permute-start | bytes 1572872 | tf_op jit(solution)/shard_map/ppermute | solution.py:35
  50.1 0.5 collective-permute-start.23
  50.6 1.0 %collective-permute-start.25 = (bf16[256,512]{1,0:T(8,128)(2,1)S(1)}, bf16[256,512]{1,0:T(8,128)(2,1)S(1)}, u32[]{:S(2)}, u32[]{:S(2)}) collective-permute-start(bf16[256,512]{1,0:T(8,128)(2,1)S(1)} %collective-permute-done.16.refs_5_), channel_id=1, source_target_pairs={{0,64},{8,72},{16,80},{24,88},{32,96},{40,104},{48,112},{56,120},{... | collective-permute-start | bytes 786440 | tf_op jit(solution)/shard_map/ppermute | solution.py:39
  51.7 3.0 %mid_b.1 = (f32[256,1024]{1,0:T(8,128)S(1)}, f32[8,1024]{1,0:T(8,128)S(1)}, f32[256,1024]{1,0:T(8,128)S(1)}, f32[512,256]{1,0:T(8,128)S(1)}) custom-call(s32[5]{0:T(128)S(1)} %stack.35.pos_ref, bf16[512,512]{1,0:T(8,128)(2,1)S(1)} %collective-permute-done.19.refs_0_.refs_8_, ...), custom_call_target="tpu_custom_call", output_to_operand_aliasing={{0}: (9, {}), {1}: (10, {}), {2}: (11, {}), {3}: (12, {})} | custom-call | flops 1024 | bytes 1024 | tf_op jit(solution)/shard_map/mid_b/pallas_call | solution.py:76
  54.7 5.3 %collective-permute-done.25.refs_1_ = bf16[256,512]{1,0:T(8,128)(2,1)S(1)} collective-permute-done((bf16[256,512]{1,0:T(8,128)(2,1)S(1)}, bf16[256,512]{1,0:T(8,128)(2,1)S(1)}, u32[]{:S(2)}, u32[]{:S(2)}) %collective-permute-start.25) | collective-permute-done | bytes 262176 | tf_op jit(solution)/shard_map/ppermute | solution.py:39
  60.1 0.8 %collective-permute-start.27 = (bf16[512,512]{1,0:T(8,128)(2,1)S(1)}, bf16[512,512]{1,0:T(8,128)(2,1)S(1)}, u32[]{:S(2)}, u32[]{:S(2)}) collective-permute-start(bf16[512,512]{1,0:T(8,128)(2,1)S(1)} %collective-permute-done.24.refs_9_), channel_id=1, source_target_pairs={{0,8},{8,0},{16,24},{24,16},{32,40},{40,32},{48,56},{56,48},{64,72... | collective-permute-start | bytes 1572872 | tf_op jit(solution)/shard_map/ppermute | solution.py:35
  61.4 1.9 %mid_c.1 = (f32[256,1024]{1,0:T(8,128)S(1)}, f32[8,1024]{1,0:T(8,128)S(1)}) custom-call(s32[5]{0:T(128)S(1)} %stack.35.pos_ref, bf16[256,512]{1,0:T(8,128)(2,1)S(1)} %collective-permute-done.15.refs_0_.refs_4_, bf16[256,512]{1,0:T(8,128)(2,1)S(1)} %collective-permute-done.22.refs_1_.refs_6_, ...), custom_call_target="tpu_custom_call", output_to_operand_aliasing={{0}: (5, {}), {1}: (6, {})} | custom-call | flops 1024 | bytes 1024 | tf_op jit(solution)/shard_map/mid_c/pallas_call | solution.py:76
  63.4 6.3 %last.1 = bf16[256,1024]{1,0:T(8,128)(2,1)} custom-call(s32[5]{0:T(128)S(1)} %stack.35.pos_ref, bf16[256,512]{1,0:T(8,128)(2,1)S(1)} %collective-permute-done.20.refs_0_, bf16[256,512]{1,0:T(8,128)(2,1)S(1)} %collective-permute-done.25.refs_1_, bf16[256,512]{1,0:T(8,128)(2,1)S(1)} %collective-permute-done.23.refs_2_, ...), custom_call_target="tpu_custom_call" | custom-call | flops 1024 | bytes 1024 | tf_op jit(solution)/shard_map/last/pallas_call | solution.py:76
  (51 shorter events, 3.2 us)
Async XLA Ops:
  0.1 5.7 %collective-permute-start = (bf16[256,512]{1,0:T(8,128)(2,1)}, bf16[256,512]{1,0:T(8,128)(2,1)S(1)}, u32[]{:S(2)}, u32[]{:S(2)}) collective-permute-start(bf16[256,512]{1,0:T(8,128)(2,1)} %param.6), channel_id=1, source_target_pairs={{0,8},{8,0},{16,24},{24,16},{32,40},{40,32},{48,56},{56,48},{64,72... | collective-permute-start | bytes 786440 | tf_op jit(solution)/shard_map/ppermute | solution.py:35
  1.5 9.3 %collective-permute-start.2 = (bf16[256,512]{1,0:T(8,128)(2,1)}, bf16[256,512]{1,0:T(8,128)(2,1)S(1)}, u32[]{:S(2)}, u32[]{:S(2)}) collective-permute-start(bf16[256,512]{1,0:T(8,128)(2,1)} %param.6), channel_id=1, source_target_pairs={{0,16},{8,56},{16,32},{24,8},{32,48},{40,24},{48,0},{56,40},{64,80... | collective-permute-start | bytes 786440 | tf_op jit(solution)/shard_map/ppermute | solution.py:31
  5.8 5.0 %collective-permute-start.1 = (bf16[4,64,256]{2,1,0:T(8,128)(2,1)S(1)}, bf16[4,64,256]{2,1,0:T(8,128)(2,1)S(1)}, u32[]{:S(2)}, u32[]{:S(2)}) collective-permute-start(bf16[4,64,256]{2,1,0:T(8,128)(2,1)S(1)} %get-tuple-element.57), channel_id=1, source_target_pairs={{0,1},{1,0},{2,3},{3,2},{4,5},{5,4},{6,7},{7,6},{8,9},{9,8},{10,11... | collective-permute-start | bytes 393224 | tf_op jit(solution)/shard_map/ppermute | solution.py:43
  7.2 8.8 %collective-permute-start.7 = (bf16[256,512]{1,0:T(8,128)(2,1)S(1)}, bf16[256,512]{1,0:T(8,128)(2,1)S(1)}, u32[]{:S(2)}, u32[]{:S(2)}) collective-permute-start(bf16[256,512]{1,0:T(8,128)(2,1)S(1)} %collective-permute-done.refs_2_), channel_id=1, source_target_pairs={{0,16},{8,56},{16,32},{24,8},{32,48},{40,24},{48,0},{56,40},{64,80... | collective-permute-start | bytes 786440 | tf_op jit(solution)/shard_map/ppermute | solution.py:31
  7.8 3.0 %collective-permute-start.3 = (bf16[256,512]{1,0:T(8,128)(2,1)S(1)}, bf16[256,512]{1,0:T(8,128)(2,1)S(1)}, u32[]{:S(2)}, u32[]{:S(2)}) collective-permute-start(bf16[256,512]{1,0:T(8,128)(2,1)S(1)} %collective-permute-done.refs_2_), channel_id=1, source_target_pairs={{0,8},{8,0},{16,24},{24,16},{32,40},{40,32},{48,56},{56,48},{64,72... | collective-permute-start | bytes 786440 | tf_op jit(solution)/shard_map/ppermute | solution.py:35
  8.1 10.8 %collective-permute-start.8 = (bf16[256,512]{1,0:T(8,128)(2,1)}, bf16[256,512]{1,0:T(8,128)(2,1)S(1)}, u32[]{:S(2)}, u32[]{:S(2)}) collective-permute-start(bf16[256,512]{1,0:T(8,128)(2,1)} %param.6), channel_id=1, source_target_pairs={{0,64},{8,72},{16,80},{24,88},{32,96},{40,104},{48,112},{56,120},{... | collective-permute-start | bytes 786440 | tf_op jit(solution)/shard_map/ppermute | solution.py:39
  10.9 8.0 %collective-permute-start.4 = (bf16[2,64,256]{2,1,0:T(8,128)(2,1)S(1)}, bf16[2,64,256]{2,1,0:T(8,128)(2,1)S(1)}, u32[]{:S(2)}, u32[]{:S(2)}) collective-permute-start(bf16[2,64,256]{2,1,0:T(8,128)(2,1)S(1)} %get-tuple-element.60), channel_id=1, source_target_pairs={{0,2},{1,3},{2,4},{3,5},{4,6},{5,7},{6,0},{7,1},{8,10},{9,11},{10,... | collective-permute-start | bytes 196616 | tf_op jit(solution)/shard_map/ppermute | solution.py:47
  12.6 6.3 %collective-permute-start.5 = (bf16[2,64,256]{2,1,0:T(8,128)(2,1)S(1)}, bf16[2,64,256]{2,1,0:T(8,128)(2,1)S(1)}, u32[]{:S(2)}, u32[]{:S(2)}) collective-permute-start(bf16[2,64,256]{2,1,0:T(8,128)(2,1)S(1)} %get-tuple-element.61), channel_id=1, source_target_pairs={{0,6},{1,7},{2,0},{3,1},{4,2},{5,3},{6,4},{7,5},{8,14},{9,15},{10,... | collective-permute-start | bytes 196616 | tf_op jit(solution)/shard_map/ppermute | solution.py:47
  14.8 4.6 %collective-permute-start.6 = (bf16[2,64,256]{2,1,0:T(8,128)(2,1)S(1)}, bf16[2,64,256]{2,1,0:T(8,128)(2,1)S(1)}, u32[]{:S(2)}, u32[]{:S(2)}) collective-permute-start(bf16[2,64,256]{2,1,0:T(8,128)(2,1)S(1)} %pad_maximum_fusion.6), channel_id=1, source_target_pairs={{0,4},{1,5},{2,6},{3,7},{4,0},{5,1},{6,2},{7,3},{8,12},{9,13},{10,... | collective-permute-start | bytes 196616 | tf_op jit(solution)/shard_map/ppermute | solution.py:47
  20.1 4.3 %collective-permute-start.10 = (bf16[512,512]{1,0:T(8,128)(2,1)S(1)}, bf16[512,512]{1,0:T(8,128)(2,1)S(1)}, u32[]{:S(2)}, u32[]{:S(2)}) collective-permute-start(bf16[512,512]{1,0:T(8,128)(2,1)S(1)} %pad_maximum_fusion), channel_id=1, source_target_pairs={{0,8},{8,0},{16,24},{24,16},{32,40},{40,32},{48,56},{56,48},{64,72... | collective-permute-start | bytes 1572872 | tf_op jit(solution)/shard_map/ppermute | solution.py:35
  22.1 1.9 %collective-permute-start.9 = (bf16[256,512]{1,0:T(8,128)(2,1)S(1)}, bf16[256,512]{1,0:T(8,128)(2,1)S(1)}, u32[]{:S(2)}, u32[]{:S(2)}) collective-permute-start(bf16[256,512]{1,0:T(8,128)(2,1)S(1)} %join.1.refs_1_), channel_id=1, source_target_pairs={{0,8},{8,0},{16,24},{24,16},{32,40},{40,32},{48,56},{56,48},{64,72... | collective-permute-start | bytes 786440 | tf_op jit(solution)/shard_map/ppermute | solution.py:35
  22.1 2.2 %collective-permute-start.11 = (bf16[256,512]{1,0:T(8,128)(2,1)S(1)}, bf16[256,512]{1,0:T(8,128)(2,1)S(1)}, u32[]{:S(2)}, u32[]{:S(2)}) collective-permute-start(bf16[256,512]{1,0:T(8,128)(2,1)S(1)} %collective-permute-done.8.refs_0_.refs_3_), channel_id=1, source_target_pairs={{0,8},{8,0},{16,24},{24,16},{32,40},{40,32},{48,56},{56,48},{64,72... | collective-permute-start | bytes 786440 | tf_op jit(solution)/shard_map/ppermute | solution.py:35
  22.6 13.5 %collective-permute-start.12 = (bf16[256,512]{1,0:T(8,128)(2,1)S(1)}, bf16[256,512]{1,0:T(8,128)(2,1)S(1)}, u32[]{:S(2)}, u32[]{:S(2)}) collective-permute-start(bf16[256,512]{1,0:T(8,128)(2,1)S(1)} %join.1.refs_1_), channel_id=1, source_target_pairs={{0,16},{8,56},{16,32},{24,8},{32,48},{40,24},{48,0},{56,40},{64,80... | collective-permute-start | bytes 786440 | tf_op jit(solution)/shard_map/ppermute | solution.py:31
  24.3 11.7 %collective-permute-start.13 = (bf16[256,512]{1,0:T(8,128)(2,1)S(1)}, bf16[256,512]{1,0:T(8,128)(2,1)S(1)}, u32[]{:S(2)}, u32[]{:S(2)}) collective-permute-start(bf16[256,512]{1,0:T(8,128)(2,1)S(1)} %collective-permute-done.9.refs_3_), channel_id=1, source_target_pairs={{0,16},{8,56},{16,32},{24,8},{32,48},{40,24},{48,0},{56,40},{64,80... | collective-permute-start | bytes 786440 | tf_op jit(solution)/shard_map/ppermute | solution.py:31
  25.6 10.5 %collective-permute-start.14 = (bf16[256,512]{1,0:T(8,128)(2,1)S(1)}, bf16[256,512]{1,0:T(8,128)(2,1)S(1)}, u32[]{:S(2)}, u32[]{:S(2)}) collective-permute-start(bf16[256,512]{1,0:T(8,128)(2,1)S(1)} %join.1.refs_1_), channel_id=1, source_target_pairs={{0,64},{8,72},{16,80},{24,88},{32,96},{40,104},{48,112},{56,120},{... | collective-permute-start | bytes 786440 | tf_op jit(solution)/shard_map/ppermute | solution.py:39
  28.4 7.8 %collective-permute-start.15 = (bf16[256,512]{1,0:T(8,128)(2,1)S(1)}, bf16[256,512]{1,0:T(8,128)(2,1)S(1)}, u32[]{:S(2)}, u32[]{:S(2)}) collective-permute-start(bf16[256,512]{1,0:T(8,128)(2,1)S(1)} %collective-permute-done.2.refs_4_.refs_2_), channel_id=1, source_target_pairs={{0,16},{8,56},{16,32},{24,8},{32,48},{40,24},{48,0},{56,40},{64,80... | collective-permute-start | bytes 786440 | tf_op jit(solution)/shard_map/ppermute | solution.py:31
  28.9 12.9 %collective-permute-start.19 = (bf16[512,512]{1,0:T(8,128)(2,1)S(1)}, bf16[512,512]{1,0:T(8,128)(2,1)S(1)}, u32[]{:S(2)}, u32[]{:S(2)}) collective-permute-start(bf16[512,512]{1,0:T(8,128)(2,1)S(1)} %pad_maximum_fusion.2), channel_id=1, source_target_pairs={{0,16},{8,56},{16,32},{24,8},{32,48},{40,24},{48,0},{56,40},{64,80... | collective-permute-start | bytes 1572872 | tf_op jit(solution)/shard_map/ppermute | solution.py:31
  36.1 12.3 %collective-permute-start.18 = (bf16[512,512]{1,0:T(8,128)(2,1)S(1)}, bf16[512,512]{1,0:T(8,128)(2,1)S(1)}, u32[]{:S(2)}, u32[]{:S(2)}) collective-permute-start(bf16[512,512]{1,0:T(8,128)(2,1)S(1)} %pad_maximum_fusion.1), channel_id=1, source_target_pairs={{0,8},{8,0},{16,24},{24,16},{32,40},{40,32},{48,56},{56,48},{64,72... | collective-permute-start | bytes 1572872 | tf_op jit(solution)/shard_map/ppermute | solution.py:35
  37.7 4.0 %collective-permute-start.17 = (bf16[256,512]{1,0:T(8,128)(2,1)S(1)}, bf16[256,512]{1,0:T(8,128)(2,1)S(1)}, u32[]{:S(2)}, u32[]{:S(2)}) collective-permute-start(bf16[256,512]{1,0:T(8,128)(2,1)S(1)} %collective-permute-done.14.refs_4_), channel_id=1, source_target_pairs={{0,8},{8,0},{16,24},{24,16},{32,40},{40,32},{48,56},{56,48},{64,72... | collective-permute-start | bytes 786440 | tf_op jit(solution)/shard_map/ppermute | solution.py:35
  37.8 5.5 %collective-permute-start.16 = (bf16[256,512]{1,0:T(8,128)(2,1)S(1)}, bf16[256,512]{1,0:T(8,128)(2,1)S(1)}, u32[]{:S(2)}, u32[]{:S(2)}) collective-permute-start(bf16[256,512]{1,0:T(8,128)(2,1)S(1)} %collective-permute-done.12.refs_3_), channel_id=1, source_target_pairs={{0,16},{8,56},{16,32},{24,8},{32,48},{40,24},{48,0},{56,40},{64,80... | collective-permute-start | bytes 786440 | tf_op jit(solution)/shard_map/ppermute | solution.py:31
  39.5 9.0 %collective-permute-start.20 = (bf16[256,512]{1,0:T(8,128)(2,1)S(1)}, bf16[256,512]{1,0:T(8,128)(2,1)S(1)}, u32[]{:S(2)}, u32[]{:S(2)}) collective-permute-start(bf16[256,512]{1,0:T(8,128)(2,1)S(1)} %collective-permute-done.15.refs_0_.refs_4_), channel_id=1, source_target_pairs={{0,64},{8,72},{16,80},{24,88},{32,96},{40,104},{48,112},{56,120},{... | collective-permute-start | bytes 786440 | tf_op jit(solution)/shard_map/ppermute | solution.py:39
  48.5 11.6 %collective-permute-start.21 = (bf16[512,512]{1,0:T(8,128)(2,1)S(1)}, bf16[512,512]{1,0:T(8,128)(2,1)S(1)}, u32[]{:S(2)}, u32[]{:S(2)}) collective-permute-start(bf16[512,512]{1,0:T(8,128)(2,1)S(1)} %collective-permute-done.19.refs_0_.refs_8_), channel_id=1, source_target_pairs={{0,8},{8,0},{16,24},{24,16},{32,40},{40,32},{48,56},{56,48},{64,72... | collective-permute-start | bytes 1572872 | tf_op jit(solution)/shard_map/ppermute | solution.py:35
  49.7 10.4 %collective-permute-start.24 = (bf16[512,512]{1,0:T(8,128)(2,1)S(1)}, bf16[512,512]{1,0:T(8,128)(2,1)S(1)}, u32[]{:S(2)}, u32[]{:S(2)}) collective-permute-start(bf16[512,512]{1,0:T(8,128)(2,1)S(1)} %pad_maximum_fusion.3), channel_id=1, source_target_pairs={{0,16},{8,56},{16,32},{24,8},{32,48},{40,24},{48,0},{56,40},{64,80... | collective-permute-start | bytes 1572872 | tf_op jit(solution)/shard_map/ppermute | solution.py:31
  50.1 4.6 %collective-permute-start.22 = (bf16[256,512]{1,0:T(8,128)(2,1)S(1)}, bf16[256,512]{1,0:T(8,128)(2,1)S(1)}, u32[]{:S(2)}, u32[]{:S(2)}) collective-permute-start(bf16[256,512]{1,0:T(8,128)(2,1)S(1)} %collective-permute-done.15.refs_0_.refs_4_), channel_id=1, source_target_pairs={{0,8},{8,0},{16,24},{24,16},{32,40},{40,32},{48,56},{56,48},{64,72... | collective-permute-start | bytes 786440 | tf_op jit(solution)/shard_map/ppermute | solution.py:35
  50.1 4.6 %collective-permute-start.23 = (bf16[256,512]{1,0:T(8,128)(2,1)S(1)}, bf16[256,512]{1,0:T(8,128)(2,1)S(1)}, u32[]{:S(2)}, u32[]{:S(2)}) collective-permute-start(bf16[256,512]{1,0:T(8,128)(2,1)S(1)} %collective-permute-done.20.refs_0_), channel_id=1, source_target_pairs={{0,8},{8,0},{16,24},{24,16},{32,40},{40,32},{48,56},{56,48},{64,72... | collective-permute-start | bytes 786440 | tf_op jit(solution)/shard_map/ppermute | solution.py:35
  50.6 9.4 %collective-permute-start.25 = (bf16[256,512]{1,0:T(8,128)(2,1)S(1)}, bf16[256,512]{1,0:T(8,128)(2,1)S(1)}, u32[]{:S(2)}, u32[]{:S(2)}) collective-permute-start(bf16[256,512]{1,0:T(8,128)(2,1)S(1)} %collective-permute-done.16.refs_5_), channel_id=1, source_target_pairs={{0,64},{8,72},{16,80},{24,88},{32,96},{40,104},{48,112},{56,120},{... | collective-permute-start | bytes 786440 | tf_op jit(solution)/shard_map/ppermute | solution.py:39
  51.7 11.7 %copy-start = (bf16[4,64,1024]{2,1,0:T(8,128)(2,1)S(1)}, bf16[4,64,1024]{2,1,0:T(8,128)(2,1)}, u32[]{:S(2)}) copy-start(bf16[4,64,1024]{2,1,0:T(8,128)(2,1)} %param.10) | copy-start | bytes 1572868
  51.7 11.7 %copy-start.2 = (f32[4,1024]{1,0:T(4,128)S(1)}, f32[4,1024]{1,0:T(4,128)}, u32[]{:S(2)}) copy-start(f32[4,1024]{1,0:T(4,128)} %refs_18_.1) | copy-start | bytes 49156
  51.7 11.7 %copy-start.3 = (s32[256]{0:T(256)S(1)}, s32[256]{0:T(256)}, u32[]{:S(2)}) copy-start(s32[256]{0:T(256)} %param.7) | copy-start | bytes 3076
  60.1 3.3 %collective-permute-start.27 = (bf16[512,512]{1,0:T(8,128)(2,1)S(1)}, bf16[512,512]{1,0:T(8,128)(2,1)S(1)}, u32[]{:S(2)}, u32[]{:S(2)}) collective-permute-start(bf16[512,512]{1,0:T(8,128)(2,1)S(1)} %collective-permute-done.24.refs_9_), channel_id=1, source_target_pairs={{0,8},{8,0},{16,24},{24,16},{32,40},{40,32},{48,56},{56,48},{64,72... | collective-permute-start | bytes 1572872 | tf_op jit(solution)/shard_map/ppermute | solution.py:35
  60.9 2.5 %collective-permute-start.26 = (bf16[256,512]{1,0:T(8,128)(2,1)S(1)}, bf16[256,512]{1,0:T(8,128)(2,1)S(1)}, u32[]{:S(2)}, u32[]{:S(2)}) collective-permute-start(bf16[256,512]{1,0:T(8,128)(2,1)S(1)} %collective-permute-done.25.refs_1_), channel_id=1, source_target_pairs={{0,8},{8,0},{16,24},{24,16},{32,40},{40,32},{48,56},{56,48},{64,72... | collective-permute-start | bytes 786440 | tf_op jit(solution)/shard_map/ppermute | solution.py:35
  61.0 2.4 %collective-permute-start.28 = (bf16[256,512]{1,0:T(8,128)(2,1)S(1)}, bf16[256,512]{1,0:T(8,128)(2,1)S(1)}, u32[]{:S(2)}, u32[]{:S(2)}) collective-permute-start(bf16[256,512]{1,0:T(8,128)(2,1)S(1)} %collective-permute-done.16.refs_5_), channel_id=1, source_target_pairs={{0,8},{8,0},{16,24},{24,16},{32,40},{40,32},{48,56},{56,48},{64,72... | collective-permute-start | bytes 786440 | tf_op jit(solution)/shard_map/ppermute | solution.py:35
  (1 other events, 1.0 us)

commit v3 on v2

--- a/solution.py
+++ b/solution.py
@@ -358,18 +358,19 @@
     z1 = line.send(lambda a: zshift(a, 1), jnp.stack([mine[1], got[1]]))
     z3 = line.send(lambda a: zshift(a, -1), jnp.stack([mine[3], got[3]]))
     z2 = line.send(lambda a: zshift(a, 2), jnp.stack([mine[2], got[2]]))
-    line.got(z1, z3, z2, tr2, tp)
+    tf = line.send(ring, tr)
+    line.got(z1, z3, z2, tr2, tp, tf)
     d = join(line.after(pos), jnp.stack([mine[0], got[0]]), z1, z2, z3)
     line.ran(d)
 
     dr = line.send(ring, d)
     dc = line.send(core, d)
-    dp = line.send(pair, d)
     tpc = line.send(core, tp)
     trc = line.send(core, cat(tr, tr2))
     line.got(dc, trc, tpc)
     dr2 = line.send(ring, dc)
-    tf = line.send(ring, tr)
+    dp = line.send(pair, d)
+    df = line.send(ring, dr)
     tpr = line.send(ring, cat(tp, tpc))
     w, *sums = first_step(
         line.after(pos),
@@ -379,55 +380,46 @@
     )
     base, norm = sums[:2], sums[2:]
     line.ran(norm[1])
-    line.got(dr, dr2, dp, tf)
-
-    df = line.send(ring, dr)
-    tfp = line.send(pair, tf)
+    line.got(dr2, dp, df, tpr)
+
     dpc = line.send(core, dp)
     drc = line.send(core, cat(dr, dr2))
+    tprc = line.send(core, tpr)
+    tfc = line.send(core, tf)
+    dfp = line.send(pair, df)
+    dpr = line.send(ring, cat(dp, dpc))
+    tfp = line.send(ring, tpr[:256])
+    dfc = line.send(core, df)
+    ring_t = [(tpr, 0), (tpr, 1), (tprc, 0), (tprc, 1)]
     base, norm = step(
-        "mid_a",
+        "middle",
         line.after(pos),
-        list(zip(mirrored(OWN), [tp, tpc])),
-        list(zip(BEHIND, [tr, tr2], [dr, dr2])),
+        list(zip(FAR + mirrored(OWN + BEHIND + AHEAD), [tf, tfc, tp, tpc] + ring_t)),
+        list(
+            zip(
+                BEHIND + AHEAD + mirrored(OWN),
+                [tr, tr2, (trc, 0), (trc, 1), tp, tpc],
+                [dr, dr2, (drc, 0), (drc, 1), dp, dpc],
+            )
+        ),
         w,
         base,
         norm,
     )
     line.ran(norm[1])
-    line.got(df, dpc, drc, tpr, tfp)
-
-    dpr = line.send(ring, cat(dp, dpc))
-    dfp = line.send(pair, df)
-    tprc = line.send(core, tpr)
-    tfc = line.send(core, tf)
-    tfpc = line.send(core, tfp)
-    base, norm = step(
-        "mid_b",
-        line.after(pos),
-        list(zip(mirrored(BEHIND), [(tpr, 0), (tpr, 1)])),
-        list(zip(AHEAD + mirrored(OWN), [(trc, 0), (trc, 1), tp, tpc], [(drc, 0), (drc, 1), dp, dpc])),
-        w,
-        base,
-        norm,
-    )
-    line.ran(norm[1])
-    line.got(tprc, tfc, tfpc, dpr, dfp)
+    line.got(dfp, dpr, tfp, dfc)
 
     dprc = line.send(core, dpr)
     dfpc = line.send(core, dfp)
-    dfc = line.send(core, df)
-    base, norm = step(
-        "mid_c", line.after(pos), list(zip(FAR + mirrored(AHEAD), [tf, tfc, (tprc, 0), (tprc, 1)])), [], w, base, norm
-    )
-    line.ran(base[1])
-    line.got(dfpc, dprc, dfc)
-    ring_t = [(tpr, 0), (tpr, 1), (tprc, 0), (tprc, 1)]
+    tfpc = line.send(core, tfp)
+    base, norm = step("far", line.after(pos), [], list(zip(FAR, [tf, tfc], [df, dfc])), w, base, norm)
+    line.ran(norm[1])
+    line.got(dfpc, dprc, tfpc)
     ring_d = [(dpr, 0), (dpr, 1), (dprc, 0), (dprc, 1)]
     return last_step(
         line.after(pos),
         list(zip(mirrored(FAR), [tfp, tfpc], [dfp, dfpc])),
-        list(zip(FAR + mirrored(BEHIND + AHEAD), [tf, tfc] + ring_t, [df, dfc] + ring_d)),
+        list(zip(mirrored(BEHIND + AHEAD), ring_t, ring_d)),
         w,
         base,
         norm,

time: 70 us -> 65.7 us (0.939)
  waiting for transfers between devices: 16 us -> 6.88 us
  starting transfers between devices: 30.6 us -> 36.1 us
    ppermute x4 -> x3, waiting for transfers between devices: 13.4 us -> 1.46 us  [pair(): return lax.ppermute(a, 'row', PAIR)]
    ppermute x8 -> x9, starting transfers between devices: 8.79 us -> 13 us  [ring(): return lax.ppermute(a, 'row', RING)]
    ppermute x3, waiting for transfers between devices: 0.49 us -> 1.9 us  [zshift(): lax.ppermute(a, 'ad', [(z * 2 + yl, (z + step) % 4 * 2 + yl) for z, yl in...]
    ppermute x13, starting transfers between devices: 8.88 us -> 10.2 us  [core(): return lax.ppermute(a, 'row', CORE)]
    ppermute x8 -> x9, waiting for transfers between devices: 1.58 us -> 2.92 us  [ring(): return lax.ppermute(a, 'row', RING)]
    pallas_call x7 -> x6, Pallas kernels: 21.5 us -> 20.8 us  [call(): pl.pallas_call(body, out_shape=outs, in_specs=specs, out_specs=out_specs...]
    ppermute x4 -> x3, starting transfers between devices: 6.43 us -> 6.39 us  [pair(): return lax.ppermute(a, 'row', PAIR)]
  transfers between devices with their start and end apart: 29 -> 29, of which waited for: 7 -> 6; matrix products, arithmetic and copies ran while one was open for 0% -> 0% of each run, Pallas kernels for 21% -> 22%
where the time goes in v3:
time: 65.7 us; the launch traced here: 65.5 us
  starting transfers between devices  36.1 us (55%)
  Pallas kernels  20.8 us (32%)
  waiting for transfers between devices  6.88 us (10%)
  local copies, waits for them, and re-layouts  1.17 us (2%)
    pallas_call x6, Pallas kernels, call(): pl.pallas_call(body, out_shape=outs, in_specs=specs, out_specs=out_specs...  20.8 us
    ppermute x9, starting transfers between devices, ring(): return lax.ppermute(a, 'row', RING)  13 us
    ppermute x13, starting transfers between devices, core(): return lax.ppermute(a, 'row', CORE)  10.2 us
    ppermute x3, starting transfers between devices, pair(): return lax.ppermute(a, 'row', PAIR)  6.39 us
    ppermute x3, starting transfers between devices, zshift(): lax.ppermute(a, 'ad', [(z * 2 + yl, (z + step) % 4 * 2 + yl) for z, yl in...  5.13 us
    ppermute x9, waiting for transfers between devices, ring(): return lax.ppermute(a, 'row', RING)  2.92 us
    ppermute x3, waiting for transfers between devices, zshift(): lax.ppermute(a, 'ad', [(z * 2 + yl, (z + step) % 4 * 2 + yl) for z, yl in...  1.9 us
    ppermute x3, waiting for transfers between devices, pair(): return lax.ppermute(a, 'row', PAIR)  1.46 us
  transfers between devices with their start and end apart: 29, of which 6 were waited for; matrix products, arithmetic and copies ran while one was open for 0% of the time, Pallas kernels for 22%

profile of v3, /device:TPU:1, one launch (start us, length us, event | category | flops | bytes accessed | tf_op | source)
XLA Modules:
  0.0 65.5 jit_solution(955366872888327040)
XLA Ops:
  0.1 1.4 %collective-permute-start = (bf16[256,512]{1,0:T(8,128)(2,1)}, bf16[256,512]{1,0:T(8,128)(2,1)S(1)}, u32[]{:S(2)}, u32[]{:S(2)}) collective-permute-start(bf16[256,512]{1,0:T(8,128)(2,1)} %param.6), channel_id=1, source_target_pairs={{0,8},{8,0},{16,24},{24,16},{32,40},{40,32},{48,56},{56,48},{64,72... | collective-permute-start | bytes 786440 | tf_op jit(solution)/shard_map/ppermute | solution.py:35
  1.5 2.6 %collective-permute-start.2 = (bf16[256,512]{1,0:T(8,128)(2,1)}, bf16[256,512]{1,0:T(8,128)(2,1)S(1)}, u32[]{:S(2)}, u32[]{:S(2)}) collective-permute-start(bf16[256,512]{1,0:T(8,128)(2,1)} %param.6), channel_id=1, source_target_pairs={{0,16},{8,56},{16,32},{24,8},{32,48},{40,24},{48,0},{56,40},{64,80... | collective-permute-start | bytes 786440 | tf_op jit(solution)/shard_map/ppermute | solution.py:31
  4.1 1.0 %copy-done.1 = bf16[32,64,64]{2,1,0:T(8,128)(2,1)S(1)} copy-done((bf16[32,64,64]{2,1,0:T(8,128)(2,1)S(1)}, bf16[32,64,64]{2,1,0:T(8,128)(2,1)}, u32[]{:S(2)}) %copy-start.1) | copy-done | bytes 262168
  5.1 0.7 %pack.1 = (bf16[4,64,256]{2,1,0:T(8,128)(2,1)S(1)}, bf16[4,64,256]{2,1,0:T(8,128)(2,1)S(1)}) custom-call(s32[5]{0:T(128)S(1)} %stack.35.pos_ref, bf16[32,64,64]{2,1,0:T(8,128)(2,1)S(1)} %copy-done.1), custom_call_target="tpu_custom_call" | custom-call | flops 1024 | bytes 1024 | tf_op jit(solution)/shard_map/pack/pallas_call | solution.py:76
  5.8 1.4 %collective-permute-start.1 = (bf16[4,64,256]{2,1,0:T(8,128)(2,1)S(1)}, bf16[4,64,256]{2,1,0:T(8,128)(2,1)S(1)}, u32[]{:S(2)}, u32[]{:S(2)}) collective-permute-start(bf16[4,64,256]{2,1,0:T(8,128)(2,1)S(1)} %get-tuple-element.52), channel_id=1, source_target_pairs={{0,1},{1,0},{2,3},{3,2},{4,5},{5,4},{6,7},{7,6},{8,9},{9,8},{10,11... | collective-permute-start | bytes 393224 | tf_op jit(solution)/shard_map/ppermute | solution.py:43
  7.3 0.8 %collective-permute-start.7 = (bf16[256,512]{1,0:T(8,128)(2,1)S(1)}, bf16[256,512]{1,0:T(8,128)(2,1)S(1)}, u32[]{:S(2)}, u32[]{:S(2)}) collective-permute-start(bf16[256,512]{1,0:T(8,128)(2,1)S(1)} %collective-permute-done.refs_2_), channel_id=1, source_target_pairs={{0,16},{8,56},{16,32},{24,8},{32,48},{40,24},{48,0},{56,40},{64,80... | collective-permute-start | bytes 786440 | tf_op jit(solution)/shard_map/ppermute | solution.py:31
  8.1 2.6 %collective-permute-start.8 = (bf16[256,512]{1,0:T(8,128)(2,1)}, bf16[256,512]{1,0:T(8,128)(2,1)S(1)}, u32[]{:S(2)}, u32[]{:S(2)}) collective-permute-start(bf16[256,512]{1,0:T(8,128)(2,1)} %param.6), channel_id=1, source_target_pairs={{0,64},{8,72},{16,80},{24,88},{32,96},{40,104},{48,112},{56,120},{... | collective-permute-start | bytes 786440 | tf_op jit(solution)/shard_map/ppermute | solution.py:39
  10.8 1.3 %collective-permute-start.9 = (bf16[256,512]{1,0:T(8,128)(2,1)S(1)}, bf16[256,512]{1,0:T(8,128)(2,1)S(1)}, u32[]{:S(2)}, u32[]{:S(2)}) collective-permute-start(bf16[256,512]{1,0:T(8,128)(2,1)S(1)} %collective-permute-done.2.refs_4_.refs_6_), channel_id=1, source_target_pairs={{0,16},{8,56},{16,32},{24,8},{32,48},{40,24},{48,0},{56,40},{64,80... | collective-permute-start | bytes 786440 | tf_op jit(solution)/shard_map/ppermute | solution.py:31
  12.2 1.7 %collective-permute-start.4 = (bf16[2,64,256]{2,1,0:T(8,128)(2,1)S(1)}, bf16[2,64,256]{2,1,0:T(8,128)(2,1)S(1)}, u32[]{:S(2)}, u32[]{:S(2)}) collective-permute-start(bf16[2,64,256]{2,1,0:T(8,128)(2,1)S(1)} %get-tuple-element.55), channel_id=1, source_target_pairs={{0,2},{1,3},{2,4},{3,5},{4,6},{5,7},{6,0},{7,1},{8,10},{9,11},{10,... | collective-permute-start | bytes 196616 | tf_op jit(solution)/shard_map/ppermute | solution.py:47
  13.9 2.2 %collective-permute-start.5 = (bf16[2,64,256]{2,1,0:T(8,128)(2,1)S(1)}, bf16[2,64,256]{2,1,0:T(8,128)(2,1)S(1)}, u32[]{:S(2)}, u32[]{:S(2)}) collective-permute-start(bf16[2,64,256]{2,1,0:T(8,128)(2,1)S(1)} %get-tuple-element.56), channel_id=1, source_target_pairs={{0,6},{1,7},{2,0},{3,1},{4,2},{5,3},{6,4},{7,5},{8,14},{9,15},{10,... | collective-permute-start | bytes 196616 | tf_op jit(solution)/shard_map/ppermute | solution.py:47
  16.1 1.2 %collective-permute-start.6 = (bf16[2,64,256]{2,1,0:T(8,128)(2,1)S(1)}, bf16[2,64,256]{2,1,0:T(8,128)(2,1)S(1)}, u32[]{:S(2)}, u32[]{:S(2)}) collective-permute-start(bf16[2,64,256]{2,1,0:T(8,128)(2,1)S(1)} %pad_maximum_fusion.6), channel_id=1, source_target_pairs={{0,4},{1,5},{2,6},{3,7},{4,0},{5,1},{6,2},{7,3},{8,12},{9,13},{10,... | collective-permute-start | bytes 196616 | tf_op jit(solution)/shard_map/ppermute | solution.py:47
  17.3 1.5 %collective-permute-done.8.refs_2_ = bf16[256,512]{1,0:T(8,128)(2,1)S(1)} collective-permute-done((bf16[256,512]{1,0:T(8,128)(2,1)}, bf16[256,512]{1,0:T(8,128)(2,1)S(1)}, u32[]{:S(2)}, u32[]{:S(2)}) %collective-permute-start.8) | collective-permute-done | bytes 262176 | tf_op jit(solution)/shard_map/ppermute | solution.py:39
  18.8 1.9 %collective-permute-done.6.a2 = bf16[2,64,256]{2,1,0:T(8,128)(2,1)S(1)} collective-permute-done((bf16[2,64,256]{2,1,0:T(8,128)(2,1)S(1)}, bf16[2,64,256]{2,1,0:T(8,128)(2,1)S(1)}, u32[]{:S(2)}, u32[]{:S(2)}) %collective-permute-start.6) | collective-permute-done | bytes 65568 | tf_op jit(solution)/shard_map/ppermute | solution.py:47
  20.7 0.7 %join.1.refs_1_ = bf16[256,512]{1,0:T(8,128)(2,1)S(1)} custom-call(s32[5]{0:T(128)S(1)} %stack.35.pos_ref, bf16[2,64,256]{2,1,0:T(8,128)(2,1)S(1)} %pad_maximum_fusion.7.a0, bf16[2,64,256]{2,1,0:T(8,128)(2,1)S(1)} %collective-permute-done.4.a1, bf16[2,64,256]{2,1,0:T(8,128)(2,1)S(1)} %collective-permute-done.6.a2, ...), custom_call_target="tpu_custom_call" | custom-call | flops 1024 | bytes 1024 | tf_op jit(solution)/shard_map/join/pallas_call | solution.py:76
  21.4 1.8 %collective-permute-start.11 = (bf16[512,512]{1,0:T(8,128)(2,1)S(1)}, bf16[512,512]{1,0:T(8,128)(2,1)S(1)}, u32[]{:S(2)}, u32[]{:S(2)}) collective-permute-start(bf16[512,512]{1,0:T(8,128)(2,1)S(1)} %pad_maximum_fusion), channel_id=1, source_target_pairs={{0,8},{8,0},{16,24},{24,16},{32,40},{40,32},{48,56},{56,48},{64,72... | collective-permute-start | bytes 1572872 | tf_op jit(solution)/shard_map/ppermute | solution.py:35
  23.7 1.8 %collective-permute-start.15 = (bf16[256,512]{1,0:T(8,128)(2,1)S(1)}, bf16[256,512]{1,0:T(8,128)(2,1)S(1)}, u32[]{:S(2)}, u32[]{:S(2)}) collective-permute-start(bf16[256,512]{1,0:T(8,128)(2,1)S(1)} %join.1.refs_1_), channel_id=1, source_target_pairs={{0,16},{8,56},{16,32},{24,8},{32,48},{40,24},{48,0},{56,40},{64,80... | collective-permute-start | bytes 786440 | tf_op jit(solution)/shard_map/ppermute | solution.py:31
  25.5 1.7 %collective-permute-start.17 = (bf16[512,512]{1,0:T(8,128)(2,1)S(1)}, bf16[512,512]{1,0:T(8,128)(2,1)S(1)}, u32[]{:S(2)}, u32[]{:S(2)}) collective-permute-start(bf16[512,512]{1,0:T(8,128)(2,1)S(1)} %pad_maximum_fusion.1), channel_id=1, source_target_pairs={{0,16},{8,56},{16,32},{24,8},{32,48},{40,24},{48,0},{56,40},{64,80... | collective-permute-start | bytes 1572872 | tf_op jit(solution)/shard_map/ppermute | solution.py:31
  27.3 1.3 %collective-permute-start.13 = (bf16[256,512]{1,0:T(8,128)(2,1)S(1)}, bf16[256,512]{1,0:T(8,128)(2,1)S(1)}, u32[]{:S(2)}, u32[]{:S(2)}) collective-permute-start(bf16[256,512]{1,0:T(8,128)(2,1)S(1)} %collective-permute-done.10.refs_3_), channel_id=1, source_target_pairs={{0,16},{8,56},{16,32},{24,8},{32,48},{40,24},{48,0},{56,40},{64,80... | collective-permute-start | bytes 786440 | tf_op jit(solution)/shard_map/ppermute | solution.py:31
  28.6 1.8 %collective-permute-start.14 = (bf16[256,512]{1,0:T(8,128)(2,1)S(1)}, bf16[256,512]{1,0:T(8,128)(2,1)S(1)}, u32[]{:S(2)}, u32[]{:S(2)}) collective-permute-start(bf16[256,512]{1,0:T(8,128)(2,1)S(1)} %join.1.refs_1_), channel_id=1, source_target_pairs={{0,64},{8,72},{16,80},{24,88},{32,96},{40,104},{48,112},{56,120},{... | collective-permute-start | bytes 786440 | tf_op jit(solution)/shard_map/ppermute | solution.py:39
  30.4 1.5 %collective-permute-start.16 = (bf16[256,512]{1,0:T(8,128)(2,1)S(1)}, bf16[256,512]{1,0:T(8,128)(2,1)S(1)}, u32[]{:S(2)}, u32[]{:S(2)}) collective-permute-start(bf16[256,512]{1,0:T(8,128)(2,1)S(1)} %collective-permute-done.15.refs_7_), channel_id=1, source_target_pairs={{0,16},{8,56},{16,32},{24,8},{32,48},{40,24},{48,0},{56,40},{64,80... | collective-permute-start | bytes 786440 | tf_op jit(solution)/shard_map/ppermute | solution.py:31
  31.9 6.7 %first.1 = (bf16[8192,1024]{1,0:T(8,128)(2,1)S(1)}, f32[256,1024]{1,0:T(8,128)S(1)}, f32[8,1024]{1,0:T(8,128)S(1)}, f32[256,1024]{1,0:T(8,128)S(1)}, f32[512,256]{1,0:T(8,128)S(1)}) custom-call(s32[5]{0:T(128)S(1)} %stack.35.pos_ref, bf16[256,512]{1,0:T(8,128)(2,1)S(1)} %collective-permute-done.3.refs_0_, bf16[256,512]{1,0:T(8,128)(2,1)S(1)} %join.1.refs_1_, ...), custom_call_target="tpu_custom_call" | custom-call | flops 1024 | bytes 1024 | tf_op jit(solution)/shard_map/first/pallas_call | solution.py:76
  38.6 1.8 %collective-permute-done.16.refs_1_ = bf16[256,512]{1,0:T(8,128)(2,1)S(1)} collective-permute-done((bf16[256,512]{1,0:T(8,128)(2,1)S(1)}, bf16[256,512]{1,0:T(8,128)(2,1)S(1)}, u32[]{:S(2)}, u32[]{:S(2)}) %collective-permute-start.16) | collective-permute-done | bytes 262176 | tf_op jit(solution)/shard_map/ppermute | solution.py:31
  40.5 2.2 %collective-permute-start.21 = (bf16[256,512]{1,0:T(8,128)(2,1)S(1)}, bf16[256,512]{1,0:T(8,128)(2,1)S(1)}, u32[]{:S(2)}, u32[]{:S(2)}) collective-permute-start(bf16[256,512]{1,0:T(8,128)(2,1)S(1)} %collective-permute-done.14.refs_12_), channel_id=1, source_target_pairs={{0,8},{8,0},{16,24},{24,16},{32,40},{40,32},{48,56},{56,48},{64,72... | collective-permute-start | bytes 786440 | tf_op jit(solution)/shard_map/ppermute | solution.py:35
  42.7 0.6 collective-permute-start.18
  43.8 1.0 %collective-permute-start.23 = (bf16[512,512]{1,0:T(8,128)(2,1)S(1)}, bf16[512,512]{1,0:T(8,128)(2,1)S(1)}, u32[]{:S(2)}, u32[]{:S(2)}) collective-permute-start(bf16[512,512]{1,0:T(8,128)(2,1)S(1)} %pad_maximum_fusion.3), channel_id=1, source_target_pairs={{0,16},{8,56},{16,32},{24,8},{32,48},{40,24},{48,0},{56,40},{64,80... | collective-permute-start | bytes 1572872 | tf_op jit(solution)/shard_map/ppermute | solution.py:31
  44.8 1.0 %collective-permute-start.24 = (bf16[256,512]{1,0:T(8,128)(2,1)S(1)}, bf16[256,512]{1,0:T(8,128)(2,1)S(1)}, u32[]{:S(2)}, u32[]{:S(2)}) collective-permute-start(bf16[256,512]{1,0:T(8,128)(2,1)S(1)} %slice.40), channel_id=1, source_target_pairs={{0,16},{8,56},{16,32},{24,8},{32,48},{40,24},{48,0},{56,40},{64,80... | collective-permute-start | bytes 786440 | tf_op jit(solution)/shard_map/ppermute | solution.py:31
  45.9 1.9 %collective-permute-start.22 = (bf16[256,512]{1,0:T(8,128)(2,1)S(1)}, bf16[256,512]{1,0:T(8,128)(2,1)S(1)}, u32[]{:S(2)}, u32[]{:S(2)}) collective-permute-start(bf16[256,512]{1,0:T(8,128)(2,1)S(1)} %collective-permute-done.16.refs_1_), channel_id=1, source_target_pairs={{0,64},{8,72},{16,80},{24,88},{32,96},{40,104},{48,112},{56,120},{... | collective-permute-start | bytes 786440 | tf_op jit(solution)/shard_map/ppermute | solution.py:39
  48.3 5.7 %middle.1 = (f32[256,1024]{1,0:T(8,128)S(1)}, f32[8,1024]{1,0:T(8,128)S(1)}, f32[256,1024]{1,0:T(8,128)S(1)}, f32[512,256]{1,0:T(8,128)S(1)}) custom-call(s32[5]{0:T(128)S(1)} %stack.35.pos_ref, bf16[256,512]{1,0:T(8,128)(2,1)S(1)} %collective-permute-done.9.refs_0_, ...), custom_call_target="tpu_custom_call", output_to_operand_aliasing={{0}: (16, {}), {1}: (17, {}), {2}: (18, {}), {3}: (19, {})} | custom-call | flops 1024 | bytes 1024 | tf_op jit(solution)/shard_map/middle/pallas_call | solution.py:76
  54.0 1.1 %collective-permute-done.24.refs_0_ = bf16[256,512]{1,0:T(8,128)(2,1)S(1)} collective-permute-done((bf16[256,512]{1,0:T(8,128)(2,1)S(1)}, bf16[256,512]{1,0:T(8,128)(2,1)S(1)}, u32[]{:S(2)}, u32[]{:S(2)}) %collective-permute-start.24) | collective-permute-done | bytes 262176 | tf_op jit(solution)/shard_map/ppermute | solution.py:31
  55.1 2.5 %collective-permute-start.27 = (bf16[512,512]{1,0:T(8,128)(2,1)S(1)}, bf16[512,512]{1,0:T(8,128)(2,1)S(1)}, u32[]{:S(2)}, u32[]{:S(2)}) collective-permute-start(bf16[512,512]{1,0:T(8,128)(2,1)S(1)} %collective-permute-done.23.refs_5_), channel_id=1, source_target_pairs={{0,8},{8,0},{16,24},{24,16},{32,40},{40,32},{48,56},{56,48},{64,72... | collective-permute-start | bytes 1572872 | tf_op jit(solution)/shard_map/ppermute | solution.py:35
  58.1 1.6 %far.1 = (f32[256,1024]{1,0:T(8,128)S(1)}, f32[512,256]{1,0:T(8,128)S(1)}) custom-call(s32[5]{0:T(128)S(1)} %stack.35.pos_ref, bf16[256,512]{1,0:T(8,128)(2,1)S(1)} %collective-permute-done.9.refs_0_, bf16[256,512]{1,0:T(8,128)(2,1)S(1)} %collective-permute-done.16.refs_1_, ...), custom_call_target="tpu_custom_call", output_to_operand_aliasing={{0}: (6, {}), {1}: (7, {})} | custom-call | flops 1024 | bytes 1024 | tf_op jit(solution)/shard_map/far/pallas_call | solution.py:76
  59.9 5.5 %last.1 = bf16[256,1024]{1,0:T(8,128)(2,1)} custom-call(s32[5]{0:T(128)S(1)} %stack.35.pos_ref, bf16[256,512]{1,0:T(8,128)(2,1)S(1)} %collective-permute-done.24.refs_0_, bf16[256,512]{1,0:T(8,128)(2,1)S(1)} %collective-permute-done.22.refs_1_, bf16[256,512]{1,0:T(8,128)(2,1)S(1)} %collective-permute-done.28.refs_2_, ...), custom_call_target="tpu_custom_call" | custom-call | flops 1024 | bytes 1024 | tf_op jit(solution)/shard_map/last/pallas_call | solution.py:76
  (51 shorter events, 2.7 us)
Async XLA Ops:
  0.1 5.7 %collective-permute-start = (bf16[256,512]{1,0:T(8,128)(2,1)}, bf16[256,512]{1,0:T(8,128)(2,1)S(1)}, u32[]{:S(2)}, u32[]{:S(2)}) collective-permute-start(bf16[256,512]{1,0:T(8,128)(2,1)} %param.6), channel_id=1, source_target_pairs={{0,8},{8,0},{16,24},{24,16},{32,40},{40,32},{48,56},{56,48},{64,72... | collective-permute-start | bytes 786440 | tf_op jit(solution)/shard_map/ppermute | solution.py:35
  1.5 9.3 %collective-permute-start.2 = (bf16[256,512]{1,0:T(8,128)(2,1)}, bf16[256,512]{1,0:T(8,128)(2,1)S(1)}, u32[]{:S(2)}, u32[]{:S(2)}) collective-permute-start(bf16[256,512]{1,0:T(8,128)(2,1)} %param.6), channel_id=1, source_target_pairs={{0,16},{8,56},{16,32},{24,8},{32,48},{40,24},{48,0},{56,40},{64,80... | collective-permute-start | bytes 786440 | tf_op jit(solution)/shard_map/ppermute | solution.py:31
  5.8 5.0 %collective-permute-start.1 = (bf16[4,64,256]{2,1,0:T(8,128)(2,1)S(1)}, bf16[4,64,256]{2,1,0:T(8,128)(2,1)S(1)}, u32[]{:S(2)}, u32[]{:S(2)}) collective-permute-start(bf16[4,64,256]{2,1,0:T(8,128)(2,1)S(1)} %get-tuple-element.52), channel_id=1, source_target_pairs={{0,1},{1,0},{2,3},{3,2},{4,5},{5,4},{6,7},{7,6},{8,9},{9,8},{10,11... | collective-permute-start | bytes 393224 | tf_op jit(solution)/shard_map/ppermute | solution.py:43
  7.2 3.6 %collective-permute-start.3 = (bf16[256,512]{1,0:T(8,128)(2,1)S(1)}, bf16[256,512]{1,0:T(8,128)(2,1)S(1)}, u32[]{:S(2)}, u32[]{:S(2)}) collective-permute-start(bf16[256,512]{1,0:T(8,128)(2,1)S(1)} %collective-permute-done.refs_2_), channel_id=1, source_target_pairs={{0,8},{8,0},{16,24},{24,16},{32,40},{40,32},{48,56},{56,48},{64,72... | collective-permute-start | bytes 786440 | tf_op jit(solution)/shard_map/ppermute | solution.py:35
  7.3 8.8 %collective-permute-start.7 = (bf16[256,512]{1,0:T(8,128)(2,1)S(1)}, bf16[256,512]{1,0:T(8,128)(2,1)S(1)}, u32[]{:S(2)}, u32[]{:S(2)}) collective-permute-start(bf16[256,512]{1,0:T(8,128)(2,1)S(1)} %collective-permute-done.refs_2_), channel_id=1, source_target_pairs={{0,16},{8,56},{16,32},{24,8},{32,48},{40,24},{48,0},{56,40},{64,80... | collective-permute-start | bytes 786440 | tf_op jit(solution)/shard_map/ppermute | solution.py:31
  8.1 10.7 %collective-permute-start.8 = (bf16[256,512]{1,0:T(8,128)(2,1)}, bf16[256,512]{1,0:T(8,128)(2,1)S(1)}, u32[]{:S(2)}, u32[]{:S(2)}) collective-permute-start(bf16[256,512]{1,0:T(8,128)(2,1)} %param.6), channel_id=1, source_target_pairs={{0,64},{8,72},{16,80},{24,88},{32,96},{40,104},{48,112},{56,120},{... | collective-permute-start | bytes 786440 | tf_op jit(solution)/shard_map/ppermute | solution.py:39
  10.8 9.9 %collective-permute-start.9 = (bf16[256,512]{1,0:T(8,128)(2,1)S(1)}, bf16[256,512]{1,0:T(8,128)(2,1)S(1)}, u32[]{:S(2)}, u32[]{:S(2)}) collective-permute-start(bf16[256,512]{1,0:T(8,128)(2,1)S(1)} %collective-permute-done.2.refs_4_.refs_6_), channel_id=1, source_target_pairs={{0,16},{8,56},{16,32},{24,8},{32,48},{40,24},{48,0},{56,40},{64,80... | collective-permute-start | bytes 786440 | tf_op jit(solution)/shard_map/ppermute | solution.py:31
  12.2 6.6 %collective-permute-start.4 = (bf16[2,64,256]{2,1,0:T(8,128)(2,1)S(1)}, bf16[2,64,256]{2,1,0:T(8,128)(2,1)S(1)}, u32[]{:S(2)}, u32[]{:S(2)}) collective-permute-start(bf16[2,64,256]{2,1,0:T(8,128)(2,1)S(1)} %get-tuple-element.55), channel_id=1, source_target_pairs={{0,2},{1,3},{2,4},{3,5},{4,6},{5,7},{6,0},{7,1},{8,10},{9,11},{10,... | collective-permute-start | bytes 196616 | tf_op jit(solution)/shard_map/ppermute | solution.py:47
  13.9 4.9 %collective-permute-start.5 = (bf16[2,64,256]{2,1,0:T(8,128)(2,1)S(1)}, bf16[2,64,256]{2,1,0:T(8,128)(2,1)S(1)}, u32[]{:S(2)}, u32[]{:S(2)}) collective-permute-start(bf16[2,64,256]{2,1,0:T(8,128)(2,1)S(1)} %get-tuple-element.56), channel_id=1, source_target_pairs={{0,6},{1,7},{2,0},{3,1},{4,2},{5,3},{6,4},{7,5},{8,14},{9,15},{10,... | collective-permute-start | bytes 196616 | tf_op jit(solution)/shard_map/ppermute | solution.py:47
  16.1 4.6 %collective-permute-start.6 = (bf16[2,64,256]{2,1,0:T(8,128)(2,1)S(1)}, bf16[2,64,256]{2,1,0:T(8,128)(2,1)S(1)}, u32[]{:S(2)}, u32[]{:S(2)}) collective-permute-start(bf16[2,64,256]{2,1,0:T(8,128)(2,1)S(1)} %pad_maximum_fusion.6), channel_id=1, source_target_pairs={{0,4},{1,5},{2,6},{3,7},{4,0},{5,1},{6,2},{7,3},{8,12},{9,13},{10,... | collective-permute-start | bytes 196616 | tf_op jit(solution)/shard_map/ppermute | solution.py:47
  21.4 4.2 %collective-permute-start.11 = (bf16[512,512]{1,0:T(8,128)(2,1)S(1)}, bf16[512,512]{1,0:T(8,128)(2,1)S(1)}, u32[]{:S(2)}, u32[]{:S(2)}) collective-permute-start(bf16[512,512]{1,0:T(8,128)(2,1)S(1)} %pad_maximum_fusion), channel_id=1, source_target_pairs={{0,8},{8,0},{16,24},{24,16},{32,40},{40,32},{48,56},{56,48},{64,72... | collective-permute-start | bytes 1572872 | tf_op jit(solution)/shard_map/ppermute | solution.py:35
  23.2 2.3 %collective-permute-start.12 = (bf16[256,512]{1,0:T(8,128)(2,1)S(1)}, bf16[256,512]{1,0:T(8,128)(2,1)S(1)}, u32[]{:S(2)}, u32[]{:S(2)}) collective-permute-start(bf16[256,512]{1,0:T(8,128)(2,1)S(1)} %collective-permute-done.8.refs_2_), channel_id=1, source_target_pairs={{0,8},{8,0},{16,24},{24,16},{32,40},{40,32},{48,56},{56,48},{64,72... | collective-permute-start | bytes 786440 | tf_op jit(solution)/shard_map/ppermute | solution.py:35
  23.3 2.2 %collective-permute-start.10 = (bf16[256,512]{1,0:T(8,128)(2,1)S(1)}, bf16[256,512]{1,0:T(8,128)(2,1)S(1)}, u32[]{:S(2)}, u32[]{:S(2)}) collective-permute-start(bf16[256,512]{1,0:T(8,128)(2,1)S(1)} %join.1.refs_1_), channel_id=1, source_target_pairs={{0,8},{8,0},{16,24},{24,16},{32,40},{40,32},{48,56},{56,48},{64,72... | collective-permute-start | bytes 786440 | tf_op jit(solution)/shard_map/ppermute | solution.py:35
  23.7 6.7 %collective-permute-start.15 = (bf16[256,512]{1,0:T(8,128)(2,1)S(1)}, bf16[256,512]{1,0:T(8,128)(2,1)S(1)}, u32[]{:S(2)}, u32[]{:S(2)}) collective-permute-start(bf16[256,512]{1,0:T(8,128)(2,1)S(1)} %join.1.refs_1_), channel_id=1, source_target_pairs={{0,16},{8,56},{16,32},{24,8},{32,48},{40,24},{48,0},{56,40},{64,80... | collective-permute-start | bytes 786440 | tf_op jit(solution)/shard_map/ppermute | solution.py:31
  25.5 14.9 %collective-permute-start.17 = (bf16[512,512]{1,0:T(8,128)(2,1)S(1)}, bf16[512,512]{1,0:T(8,128)(2,1)S(1)}, u32[]{:S(2)}, u32[]{:S(2)}) collective-permute-start(bf16[512,512]{1,0:T(8,128)(2,1)S(1)} %pad_maximum_fusion.1), channel_id=1, source_target_pairs={{0,16},{8,56},{16,32},{24,8},{32,48},{40,24},{48,0},{56,40},{64,80... | collective-permute-start | bytes 1572872 | tf_op jit(solution)/shard_map/ppermute | solution.py:31
  27.3 11.3 %collective-permute-start.13 = (bf16[256,512]{1,0:T(8,128)(2,1)S(1)}, bf16[256,512]{1,0:T(8,128)(2,1)S(1)}, u32[]{:S(2)}, u32[]{:S(2)}) collective-permute-start(bf16[256,512]{1,0:T(8,128)(2,1)S(1)} %collective-permute-done.10.refs_3_), channel_id=1, source_target_pairs={{0,16},{8,56},{16,32},{24,8},{32,48},{40,24},{48,0},{56,40},{64,80... | collective-permute-start | bytes 786440 | tf_op jit(solution)/shard_map/ppermute | solution.py:31
  28.6 10.1 %collective-permute-start.14 = (bf16[256,512]{1,0:T(8,128)(2,1)S(1)}, bf16[256,512]{1,0:T(8,128)(2,1)S(1)}, u32[]{:S(2)}, u32[]{:S(2)}) collective-permute-start(bf16[256,512]{1,0:T(8,128)(2,1)S(1)} %join.1.refs_1_), channel_id=1, source_target_pairs={{0,64},{8,72},{16,80},{24,88},{32,96},{40,104},{48,112},{56,120},{... | collective-permute-start | bytes 786440 | tf_op jit(solution)/shard_map/ppermute | solution.py:39
  30.4 10.1 %collective-permute-start.16 = (bf16[256,512]{1,0:T(8,128)(2,1)S(1)}, bf16[256,512]{1,0:T(8,128)(2,1)S(1)}, u32[]{:S(2)}, u32[]{:S(2)}) collective-permute-start(bf16[256,512]{1,0:T(8,128)(2,1)S(1)} %collective-permute-done.15.refs_7_), channel_id=1, source_target_pairs={{0,16},{8,56},{16,32},{24,8},{32,48},{40,24},{48,0},{56,40},{64,80... | collective-permute-start | bytes 786440 | tf_op jit(solution)/shard_map/ppermute | solution.py:31
  40.5 3.3 %collective-permute-start.21 = (bf16[256,512]{1,0:T(8,128)(2,1)S(1)}, bf16[256,512]{1,0:T(8,128)(2,1)S(1)}, u32[]{:S(2)}, u32[]{:S(2)}) collective-permute-start(bf16[256,512]{1,0:T(8,128)(2,1)S(1)} %collective-permute-done.14.refs_12_), channel_id=1, source_target_pairs={{0,8},{8,0},{16,24},{24,16},{32,40},{40,32},{48,56},{56,48},{64,72... | collective-permute-start | bytes 786440 | tf_op jit(solution)/shard_map/ppermute | solution.py:35
  42.6 5.1 %collective-permute-start.19 = (bf16[512,512]{1,0:T(8,128)(2,1)S(1)}, bf16[512,512]{1,0:T(8,128)(2,1)S(1)}, u32[]{:S(2)}, u32[]{:S(2)}) collective-permute-start(bf16[512,512]{1,0:T(8,128)(2,1)S(1)} %collective-permute-done.17.refs_4_), channel_id=1, source_target_pairs={{0,8},{8,0},{16,24},{24,16},{32,40},{40,32},{48,56},{56,48},{64,72... | collective-permute-start | bytes 1572872 | tf_op jit(solution)/shard_map/ppermute | solution.py:35
  42.7 3.2 %collective-permute-start.18 = (bf16[256,512]{1,0:T(8,128)(2,1)S(1)}, bf16[256,512]{1,0:T(8,128)(2,1)S(1)}, u32[]{:S(2)}, u32[]{:S(2)}) collective-permute-start(bf16[256,512]{1,0:T(8,128)(2,1)S(1)} %collective-permute-done.9.refs_0_), channel_id=1, source_target_pairs={{0,8},{8,0},{16,24},{24,16},{32,40},{40,32},{48,56},{56,48},{64,72... | collective-permute-start | bytes 786440 | tf_op jit(solution)/shard_map/ppermute | solution.py:35
  43.3 5.0 %collective-permute-start.20 = (bf16[512,512]{1,0:T(8,128)(2,1)S(1)}, bf16[512,512]{1,0:T(8,128)(2,1)S(1)}, u32[]{:S(2)}, u32[]{:S(2)}) collective-permute-start(bf16[512,512]{1,0:T(8,128)(2,1)S(1)} %pad_maximum_fusion.2), channel_id=1, source_target_pairs={{0,8},{8,0},{16,24},{24,16},{32,40},{40,32},{48,56},{56,48},{64,72... | collective-permute-start | bytes 1572872 | tf_op jit(solution)/shard_map/ppermute | solution.py:35
  43.8 11.2 %collective-permute-start.23 = (bf16[512,512]{1,0:T(8,128)(2,1)S(1)}, bf16[512,512]{1,0:T(8,128)(2,1)S(1)}, u32[]{:S(2)}, u32[]{:S(2)}) collective-permute-start(bf16[512,512]{1,0:T(8,128)(2,1)S(1)} %pad_maximum_fusion.3), channel_id=1, source_target_pairs={{0,16},{8,56},{16,32},{24,8},{32,48},{40,24},{48,0},{56,40},{64,80... | collective-permute-start | bytes 1572872 | tf_op jit(solution)/shard_map/ppermute | solution.py:31
  44.8 10.2 %collective-permute-start.24 = (bf16[256,512]{1,0:T(8,128)(2,1)S(1)}, bf16[256,512]{1,0:T(8,128)(2,1)S(1)}, u32[]{:S(2)}, u32[]{:S(2)}) collective-permute-start(bf16[256,512]{1,0:T(8,128)(2,1)S(1)} %slice.40), channel_id=1, source_target_pairs={{0,16},{8,56},{16,32},{24,8},{32,48},{40,24},{48,0},{56,40},{64,80... | collective-permute-start | bytes 786440 | tf_op jit(solution)/shard_map/ppermute | solution.py:31
  45.9 9.2 %collective-permute-start.22 = (bf16[256,512]{1,0:T(8,128)(2,1)S(1)}, bf16[256,512]{1,0:T(8,128)(2,1)S(1)}, u32[]{:S(2)}, u32[]{:S(2)}) collective-permute-start(bf16[256,512]{1,0:T(8,128)(2,1)S(1)} %collective-permute-done.16.refs_1_), channel_id=1, source_target_pairs={{0,64},{8,72},{16,80},{24,88},{32,96},{40,104},{48,112},{56,120},{... | collective-permute-start | bytes 786440 | tf_op jit(solution)/shard_map/ppermute | solution.py:39
  47.8 7.3 %collective-permute-start.25 = (bf16[256,512]{1,0:T(8,128)(2,1)S(1)}, bf16[256,512]{1,0:T(8,128)(2,1)S(1)}, u32[]{:S(2)}, u32[]{:S(2)}) collective-permute-start(bf16[256,512]{1,0:T(8,128)(2,1)S(1)} %collective-permute-done.16.refs_1_), channel_id=1, source_target_pairs={{0,8},{8,0},{16,24},{24,16},{32,40},{40,32},{48,56},{56,48},{64,72... | collective-permute-start | bytes 786440 | tf_op jit(solution)/shard_map/ppermute | solution.py:35
  48.3 11.6 %copy-start = (bf16[4,64,1024]{2,1,0:T(8,128)(2,1)S(1)}, bf16[4,64,1024]{2,1,0:T(8,128)(2,1)}, u32[]{:S(2)}) copy-start(bf16[4,64,1024]{2,1,0:T(8,128)(2,1)} %param.10) | copy-start | bytes 1572868
  48.3 11.6 %copy-start.2 = (f32[4,1024]{1,0:T(4,128)S(1)}, f32[4,1024]{1,0:T(4,128)}, u32[]{:S(2)}) copy-start(f32[4,1024]{1,0:T(4,128)} %refs_14_.1) | copy-start | bytes 49156
  48.3 11.6 %copy-start.3 = (s32[256]{0:T(256)S(1)}, s32[256]{0:T(256)}, u32[]{:S(2)}) copy-start(s32[256]{0:T(256)} %param.7) | copy-start | bytes 3076
  55.1 4.8 %collective-permute-start.27 = (bf16[512,512]{1,0:T(8,128)(2,1)S(1)}, bf16[512,512]{1,0:T(8,128)(2,1)S(1)}, u32[]{:S(2)}, u32[]{:S(2)}) collective-permute-start(bf16[512,512]{1,0:T(8,128)(2,1)S(1)} %collective-permute-done.23.refs_5_), channel_id=1, source_target_pairs={{0,8},{8,0},{16,24},{24,16},{32,40},{40,32},{48,56},{56,48},{64,72... | collective-permute-start | bytes 1572872 | tf_op jit(solution)/shard_map/ppermute | solution.py:35
  57.6 2.1 %collective-permute-start.26 = (bf16[256,512]{1,0:T(8,128)(2,1)S(1)}, bf16[256,512]{1,0:T(8,128)(2,1)S(1)}, u32[]{:S(2)}, u32[]{:S(2)}) collective-permute-start(bf16[256,512]{1,0:T(8,128)(2,1)S(1)} %collective-permute-done.22.refs_1_), channel_id=1, source_target_pairs={{0,8},{8,0},{16,24},{24,16},{32,40},{40,32},{48,56},{56,48},{64,72... | collective-permute-start | bytes 786440 | tf_op jit(solution)/shard_map/ppermute | solution.py:35
  57.7 2.2 %collective-permute-start.28 = (bf16[256,512]{1,0:T(8,128)(2,1)S(1)}, bf16[256,512]{1,0:T(8,128)(2,1)S(1)}, u32[]{:S(2)}, u32[]{:S(2)}) collective-permute-start(bf16[256,512]{1,0:T(8,128)(2,1)S(1)} %collective-permute-done.24.refs_0_), channel_id=1, source_target_pairs={{0,8},{8,0},{16,24},{24,16},{32,40},{40,32},{48,56},{56,48},{64,72... | collective-permute-start | bytes 786440 | tf_op jit(solution)/shard_map/ppermute | solution.py:35
  (1 other events, 1.0 us)

commit v4 on v3

--- a/solution.py
+++ b/solution.py
@@ -397,9 +397,9 @@
         list(zip(FAR + mirrored(OWN + BEHIND + AHEAD), [tf, tfc, tp, tpc] + ring_t)),
         list(
             zip(
-                BEHIND + AHEAD + mirrored(OWN),
-                [tr, tr2, (trc, 0), (trc, 1), tp, tpc],
-                [dr, dr2, (drc, 0), (drc, 1), dp, dpc],
+                BEHIND + AHEAD + mirrored(OWN) + FAR[:1],
+                [tr, tr2, (trc, 0), (trc, 1), tp, tpc, tf],
+                [dr, dr2, (drc, 0), (drc, 1), dp, dpc, df],
             )
         ),
         w,
@@ -412,14 +412,21 @@
     dprc = line.send(core, dpr)
     dfpc = line.send(core, dfp)
     tfpc = line.send(core, tfp)
-    base, norm = step("far", line.after(pos), [], list(zip(FAR, [tf, tfc], [df, dfc])), w, base, norm)
+    base, norm = step(
+        "far",
+        line.after(pos),
+        [],
+        list(zip(FAR[1:] + mirrored(BEHIND), [tfc, *ring_t[:2]], [dfc, (dpr, 0), (dpr, 1)])),
+        w,
+        base,
+        norm,
+    )
     line.ran(norm[1])
     line.got(dfpc, dprc, tfpc)
-    ring_d = [(dpr, 0), (dpr, 1), (dprc, 0), (dprc, 1)]
     return last_step(
         line.after(pos),
         list(zip(mirrored(FAR), [tfp, tfpc], [dfp, dfpc])),
-        list(zip(mirrored(BEHIND + AHEAD), ring_t, ring_d)),
+        list(zip(mirrored(AHEAD), ring_t[2:], [(dprc, 0), (dprc, 1)])),
         w,
         base,
         norm,

time: 65.7 us -> 65.2 us (level)
  transfers between devices with their start and end apart: 29 -> 29, of which waited for: 6 -> 5; matrix products, arithmetic and copies ran while one was open for 0% -> 0% of each run, Pallas kernels for 22% -> 24%
where the time goes in v4:
time: 65.2 us; the launch traced here: 65 us
  starting transfers between devices  36.1 us (55%)
  Pallas kernels  20.8 us (32%)
  waiting for transfers between devices  6.33 us (10%)
  local copies, waits for them, and re-layouts  1.17 us (2%)
    pallas_call x6, Pallas kernels, call(): pl.pallas_call(body, out_shape=outs, in_specs=specs, out_specs=out_specs...  20.8 us
    ppermute x9, starting transfers between devices, ring(): return lax.ppermute(a, 'row', RING)  13 us
    ppermute x13, starting transfers between devices, core(): return lax.ppermute(a, 'row', CORE)  10.2 us
    ppermute x3, starting transfers between devices, pair(): return lax.ppermute(a, 'row', PAIR)  6.39 us
    ppermute x3, starting transfers between devices, zshift(): lax.ppermute(a, 'ad', [(z * 2 + yl, (z + step) % 4 * 2 + yl) for z, yl in...  5.13 us
    ppermute x9, waiting for transfers between devices, ring(): return lax.ppermute(a, 'row', RING)  2.5 us
    ppermute x3, waiting for transfers between devices, zshift(): lax.ppermute(a, 'ad', [(z * 2 + yl, (z + step) % 4 * 2 + yl) for z, yl in...  1.9 us
    ppermute x3, waiting for transfers between devices, pair(): return lax.ppermute(a, 'row', PAIR)  1.46 us
  transfers between devices with their start and end apart: 29, of which 5 were waited for; matrix products, arithmetic and copies ran while one was open for 0% of the time, Pallas kernels for 24%

profile of v4, /device:TPU:1, one launch (start us, length us, event | category | flops | bytes accessed | tf_op | source)
XLA Modules:
  0.0 65.0 jit_solution(17915884964331953321)
XLA Ops:
  0.1 1.4 %collective-permute-start = (bf16[256,512]{1,0:T(8,128)(2,1)}, bf16[256,512]{1,0:T(8,128)(2,1)S(1)}, u32[]{:S(2)}, u32[]{:S(2)}) collective-permute-start(bf16[256,512]{1,0:T(8,128)(2,1)} %param.6), channel_id=1, source_target_pairs={{0,8},{8,0},{16,24},{24,16},{32,40},{40,32},{48,56},{56,48},{64,72... | collective-permute-start | bytes 786440 | tf_op jit(solution)/shard_map/ppermute | solution.py:35
  1.5 2.6 %collective-permute-start.2 = (bf16[256,512]{1,0:T(8,128)(2,1)}, bf16[256,512]{1,0:T(8,128)(2,1)S(1)}, u32[]{:S(2)}, u32[]{:S(2)}) collective-permute-start(bf16[256,512]{1,0:T(8,128)(2,1)} %param.6), channel_id=1, source_target_pairs={{0,16},{8,56},{16,32},{24,8},{32,48},{40,24},{48,0},{56,40},{64,80... | collective-permute-start | bytes 786440 | tf_op jit(solution)/shard_map/ppermute | solution.py:31
  4.1 1.0 %copy-done.1 = bf16[32,64,64]{2,1,0:T(8,128)(2,1)S(1)} copy-done((bf16[32,64,64]{2,1,0:T(8,128)(2,1)S(1)}, bf16[32,64,64]{2,1,0:T(8,128)(2,1)}, u32[]{:S(2)}) %copy-start.1) | copy-done | bytes 262168
  5.1 0.7 %pack.1 = (bf16[4,64,256]{2,1,0:T(8,128)(2,1)S(1)}, bf16[4,64,256]{2,1,0:T(8,128)(2,1)S(1)}) custom-call(s32[5]{0:T(128)S(1)} %stack.35.pos_ref, bf16[32,64,64]{2,1,0:T(8,128)(2,1)S(1)} %copy-done.1), custom_call_target="tpu_custom_call" | custom-call | flops 1024 | bytes 1024 | tf_op jit(solution)/shard_map/pack/pallas_call | solution.py:76
  5.8 1.4 %collective-permute-start.1 = (bf16[4,64,256]{2,1,0:T(8,128)(2,1)S(1)}, bf16[4,64,256]{2,1,0:T(8,128)(2,1)S(1)}, u32[]{:S(2)}, u32[]{:S(2)}) collective-permute-start(bf16[4,64,256]{2,1,0:T(8,128)(2,1)S(1)} %get-tuple-element.52), channel_id=1, source_target_pairs={{0,1},{1,0},{2,3},{3,2},{4,5},{5,4},{6,7},{7,6},{8,9},{9,8},{10,11... | collective-permute-start | bytes 393224 | tf_op jit(solution)/shard_map/ppermute | solution.py:43
  7.3 0.8 %collective-permute-start.7 = (bf16[256,512]{1,0:T(8,128)(2,1)S(1)}, bf16[256,512]{1,0:T(8,128)(2,1)S(1)}, u32[]{:S(2)}, u32[]{:S(2)}) collective-permute-start(bf16[256,512]{1,0:T(8,128)(2,1)S(1)} %collective-permute-done.refs_2_), channel_id=1, source_target_pairs={{0,16},{8,56},{16,32},{24,8},{32,48},{40,24},{48,0},{56,40},{64,80... | collective-permute-start | bytes 786440 | tf_op jit(solution)/shard_map/ppermute | solution.py:31
  8.1 2.6 %collective-permute-start.8 = (bf16[256,512]{1,0:T(8,128)(2,1)}, bf16[256,512]{1,0:T(8,128)(2,1)S(1)}, u32[]{:S(2)}, u32[]{:S(2)}) collective-permute-start(bf16[256,512]{1,0:T(8,128)(2,1)} %param.6), channel_id=1, source_target_pairs={{0,64},{8,72},{16,80},{24,88},{32,96},{40,104},{48,112},{56,120},{... | collective-permute-start | bytes 786440 | tf_op jit(solution)/shard_map/ppermute | solution.py:39
  10.8 1.3 %collective-permute-start.9 = (bf16[256,512]{1,0:T(8,128)(2,1)S(1)}, bf16[256,512]{1,0:T(8,128)(2,1)S(1)}, u32[]{:S(2)}, u32[]{:S(2)}) collective-permute-start(bf16[256,512]{1,0:T(8,128)(2,1)S(1)} %collective-permute-done.2.refs_4_.refs_6_), channel_id=1, source_target_pairs={{0,16},{8,56},{16,32},{24,8},{32,48},{40,24},{48,0},{56,40},{64,80... | collective-permute-start | bytes 786440 | tf_op jit(solution)/shard_map/ppermute | solution.py:31
  12.2 1.7 %collective-permute-start.4 = (bf16[2,64,256]{2,1,0:T(8,128)(2,1)S(1)}, bf16[2,64,256]{2,1,0:T(8,128)(2,1)S(1)}, u32[]{:S(2)}, u32[]{:S(2)}) collective-permute-start(bf16[2,64,256]{2,1,0:T(8,128)(2,1)S(1)} %get-tuple-element.55), channel_id=1, source_target_pairs={{0,2},{1,3},{2,4},{3,5},{4,6},{5,7},{6,0},{7,1},{8,10},{9,11},{10,... | collective-permute-start | bytes 196616 | tf_op jit(solution)/shard_map/ppermute | solution.py:47
  13.9 2.2 %collective-permute-start.5 = (bf16[2,64,256]{2,1,0:T(8,128)(2,1)S(1)}, bf16[2,64,256]{2,1,0:T(8,128)(2,1)S(1)}, u32[]{:S(2)}, u32[]{:S(2)}) collective-permute-start(bf16[2,64,256]{2,1,0:T(8,128)(2,1)S(1)} %get-tuple-element.56), channel_id=1, source_target_pairs={{0,6},{1,7},{2,0},{3,1},{4,2},{5,3},{6,4},{7,5},{8,14},{9,15},{10,... | collective-permute-start | bytes 196616 | tf_op jit(solution)/shard_map/ppermute | solution.py:47
  16.1 1.2 %collective-permute-start.6 = (bf16[2,64,256]{2,1,0:T(8,128)(2,1)S(1)}, bf16[2,64,256]{2,1,0:T(8,128)(2,1)S(1)}, u32[]{:S(2)}, u32[]{:S(2)}) collective-permute-start(bf16[2,64,256]{2,1,0:T(8,128)(2,1)S(1)} %pad_maximum_fusion.6), channel_id=1, source_target_pairs={{0,4},{1,5},{2,6},{3,7},{4,0},{5,1},{6,2},{7,3},{8,12},{9,13},{10,... | collective-permute-start | bytes 196616 | tf_op jit(solution)/shard_map/ppermute | solution.py:47
  17.3 1.5 %collective-permute-done.8.refs_2_ = bf16[256,512]{1,0:T(8,128)(2,1)S(1)} collective-permute-done((bf16[256,512]{1,0:T(8,128)(2,1)}, bf16[256,512]{1,0:T(8,128)(2,1)S(1)}, u32[]{:S(2)}, u32[]{:S(2)}) %collective-permute-start.8) | collective-permute-done | bytes 262176 | tf_op jit(solution)/shard_map/ppermute | solution.py:39
  18.8 1.9 %collective-permute-done.6.a2 = bf16[2,64,256]{2,1,0:T(8,128)(2,1)S(1)} collective-permute-done((bf16[2,64,256]{2,1,0:T(8,128)(2,1)S(1)}, bf16[2,64,256]{2,1,0:T(8,128)(2,1)S(1)}, u32[]{:S(2)}, u32[]{:S(2)}) %collective-permute-start.6) | collective-permute-done | bytes 65568 | tf_op jit(solution)/shard_map/ppermute | solution.py:47
  20.7 0.7 %join.1.refs_1_ = bf16[256,512]{1,0:T(8,128)(2,1)S(1)} custom-call(s32[5]{0:T(128)S(1)} %stack.35.pos_ref, bf16[2,64,256]{2,1,0:T(8,128)(2,1)S(1)} %pad_maximum_fusion.7.a0, bf16[2,64,256]{2,1,0:T(8,128)(2,1)S(1)} %collective-permute-done.4.a1, bf16[2,64,256]{2,1,0:T(8,128)(2,1)S(1)} %collective-permute-done.6.a2, ...), custom_call_target="tpu_custom_call" | custom-call | flops 1024 | bytes 1024 | tf_op jit(solution)/shard_map/join/pallas_call | solution.py:76
  21.4 1.8 %collective-permute-start.11 = (bf16[512,512]{1,0:T(8,128)(2,1)S(1)}, bf16[512,512]{1,0:T(8,128)(2,1)S(1)}, u32[]{:S(2)}, u32[]{:S(2)}) collective-permute-start(bf16[512,512]{1,0:T(8,128)(2,1)S(1)} %pad_maximum_fusion), channel_id=1, source_target_pairs={{0,8},{8,0},{16,24},{24,16},{32,40},{40,32},{48,56},{56,48},{64,72... | collective-permute-start | bytes 1572872 | tf_op jit(solution)/shard_map/ppermute | solution.py:35
  23.7 1.8 %collective-permute-start.15 = (bf16[256,512]{1,0:T(8,128)(2,1)S(1)}, bf16[256,512]{1,0:T(8,128)(2,1)S(1)}, u32[]{:S(2)}, u32[]{:S(2)}) collective-permute-start(bf16[256,512]{1,0:T(8,128)(2,1)S(1)} %join.1.refs_1_), channel_id=1, source_target_pairs={{0,16},{8,56},{16,32},{24,8},{32,48},{40,24},{48,0},{56,40},{64,80... | collective-permute-start | bytes 786440 | tf_op jit(solution)/shard_map/ppermute | solution.py:31
  25.5 1.7 %collective-permute-start.17 = (bf16[512,512]{1,0:T(8,128)(2,1)S(1)}, bf16[512,512]{1,0:T(8,128)(2,1)S(1)}, u32[]{:S(2)}, u32[]{:S(2)}) collective-permute-start(bf16[512,512]{1,0:T(8,128)(2,1)S(1)} %pad_maximum_fusion.1), channel_id=1, source_target_pairs={{0,16},{8,56},{16,32},{24,8},{32,48},{40,24},{48,0},{56,40},{64,80... | collective-permute-start | bytes 1572872 | tf_op jit(solution)/shard_map/ppermute | solution.py:31
  27.3 1.3 %collective-permute-start.13 = (bf16[256,512]{1,0:T(8,128)(2,1)S(1)}, bf16[256,512]{1,0:T(8,128)(2,1)S(1)}, u32[]{:S(2)}, u32[]{:S(2)}) collective-permute-start(bf16[256,512]{1,0:T(8,128)(2,1)S(1)} %collective-permute-done.10.refs_3_), channel_id=1, source_target_pairs={{0,16},{8,56},{16,32},{24,8},{32,48},{40,24},{48,0},{56,40},{64,80... | collective-permute-start | bytes 786440 | tf_op jit(solution)/shard_map/ppermute | solution.py:31
  28.6 1.8 %collective-permute-start.14 = (bf16[256,512]{1,0:T(8,128)(2,1)S(1)}, bf16[256,512]{1,0:T(8,128)(2,1)S(1)}, u32[]{:S(2)}, u32[]{:S(2)}) collective-permute-start(bf16[256,512]{1,0:T(8,128)(2,1)S(1)} %join.1.refs_1_), channel_id=1, source_target_pairs={{0,64},{8,72},{16,80},{24,88},{32,96},{40,104},{48,112},{56,120},{... | collective-permute-start | bytes 786440 | tf_op jit(solution)/shard_map/ppermute | solution.py:39
  30.4 1.5 %collective-permute-start.16 = (bf16[256,512]{1,0:T(8,128)(2,1)S(1)}, bf16[256,512]{1,0:T(8,128)(2,1)S(1)}, u32[]{:S(2)}, u32[]{:S(2)}) collective-permute-start(bf16[256,512]{1,0:T(8,128)(2,1)S(1)} %collective-permute-done.15.refs_7_), channel_id=1, source_target_pairs={{0,16},{8,56},{16,32},{24,8},{32,48},{40,24},{48,0},{56,40},{64,80... | collective-permute-start | bytes 786440 | tf_op jit(solution)/shard_map/ppermute | solution.py:31
  31.9 6.7 %first.1 = (bf16[8192,1024]{1,0:T(8,128)(2,1)S(1)}, f32[256,1024]{1,0:T(8,128)S(1)}, f32[8,1024]{1,0:T(8,128)S(1)}, f32[256,1024]{1,0:T(8,128)S(1)}, f32[512,256]{1,0:T(8,128)S(1)}) custom-call(s32[5]{0:T(128)S(1)} %stack.35.pos_ref, bf16[256,512]{1,0:T(8,128)(2,1)S(1)} %collective-permute-done.3.refs_0_, bf16[256,512]{1,0:T(8,128)(2,1)S(1)} %join.1.refs_1_, ...), custom_call_target="tpu_custom_call" | custom-call | flops 1024 | bytes 1024 | tf_op jit(solution)/shard_map/first/pallas_call | solution.py:76
  38.6 1.8 %collective-permute-done.16.refs_14_ = bf16[256,512]{1,0:T(8,128)(2,1)S(1)} collective-permute-done((bf16[256,512]{1,0:T(8,128)(2,1)S(1)}, bf16[256,512]{1,0:T(8,128)(2,1)S(1)}, u32[]{:S(2)}, u32[]{:S(2)}) %collective-permute-start.16) | collective-permute-done | bytes 262176 | tf_op jit(solution)/shard_map/ppermute | solution.py:31
  40.5 2.2 %collective-permute-start.21 = (bf16[256,512]{1,0:T(8,128)(2,1)S(1)}, bf16[256,512]{1,0:T(8,128)(2,1)S(1)}, u32[]{:S(2)}, u32[]{:S(2)}) collective-permute-start(bf16[256,512]{1,0:T(8,128)(2,1)S(1)} %collective-permute-done.14.refs_12_), channel_id=1, source_target_pairs={{0,8},{8,0},{16,24},{24,16},{32,40},{40,32},{48,56},{56,48},{64,72... | collective-permute-start | bytes 786440 | tf_op jit(solution)/shard_map/ppermute | solution.py:35
  42.7 0.6 collective-permute-start.18
  43.8 1.0 %collective-permute-start.23 = (bf16[512,512]{1,0:T(8,128)(2,1)S(1)}, bf16[512,512]{1,0:T(8,128)(2,1)S(1)}, u32[]{:S(2)}, u32[]{:S(2)}) collective-permute-start(bf16[512,512]{1,0:T(8,128)(2,1)S(1)} %pad_maximum_fusion.3), channel_id=1, source_target_pairs={{0,16},{8,56},{16,32},{24,8},{32,48},{40,24},{48,0},{56,40},{64,80... | collective-permute-start | bytes 1572872 | tf_op jit(solution)/shard_map/ppermute | solution.py:31
  44.8 1.0 %collective-permute-start.24 = (bf16[256,512]{1,0:T(8,128)(2,1)S(1)}, bf16[256,512]{1,0:T(8,128)(2,1)S(1)}, u32[]{:S(2)}, u32[]{:S(2)}) collective-permute-start(bf16[256,512]{1,0:T(8,128)(2,1)S(1)} %slice.40), channel_id=1, source_target_pairs={{0,16},{8,56},{16,32},{24,8},{32,48},{40,24},{48,0},{56,40},{64,80... | collective-permute-start | bytes 786440 | tf_op jit(solution)/shard_map/ppermute | solution.py:31
  45.9 1.9 %collective-permute-start.22 = (bf16[256,512]{1,0:T(8,128)(2,1)S(1)}, bf16[256,512]{1,0:T(8,128)(2,1)S(1)}, u32[]{:S(2)}, u32[]{:S(2)}) collective-permute-start(bf16[256,512]{1,0:T(8,128)(2,1)S(1)} %collective-permute-done.16.refs_14_), channel_id=1, source_target_pairs={{0,64},{8,72},{16,80},{24,88},{32,96},{40,104},{48,112},{56,120},{... | collective-permute-start | bytes 786440 | tf_op jit(solution)/shard_map/ppermute | solution.py:39
  48.3 6.1 %middle.1 = (f32[256,1024]{1,0:T(8,128)S(1)}, f32[8,1024]{1,0:T(8,128)S(1)}, f32[256,1024]{1,0:T(8,128)S(1)}, f32[512,256]{1,0:T(8,128)S(1)}) custom-call(s32[5]{0:T(128)S(1)} %stack.35.pos_ref, bf16[256,512]{1,0:T(8,128)(2,1)S(1)} %collective-permute-done.9.refs_0_, ...), custom_call_target="tpu_custom_call", output_to_operand_aliasing={{0}: (17, {}), {1}: (18, {}), {2}: (19, {}), {3}: (20, {})} | custom-call | flops 1024 | bytes 1024 | tf_op jit(solution)/shard_map/middle/pallas_call | solution.py:76
  54.4 0.6 collective-permute-done.24.refs_0_
  55.1 2.5 %collective-permute-start.27 = (bf16[512,512]{1,0:T(8,128)(2,1)S(1)}, bf16[512,512]{1,0:T(8,128)(2,1)S(1)}, u32[]{:S(2)}, u32[]{:S(2)}) collective-permute-start(bf16[512,512]{1,0:T(8,128)(2,1)S(1)} %collective-permute-done.23.refs_3_), channel_id=1, source_target_pairs={{0,8},{8,0},{16,24},{24,16},{32,40},{40,32},{48,56},{56,48},{64,72... | collective-permute-start | bytes 1572872 | tf_op jit(solution)/shard_map/ppermute | solution.py:35
  58.1 2.0 %far.1 = (f32[256,1024]{1,0:T(8,128)S(1)}, f32[512,256]{1,0:T(8,128)S(1)}) custom-call(s32[5]{0:T(128)S(1)} %stack.35.pos_ref, bf16[256,512]{1,0:T(8,128)(2,1)S(1)} %collective-permute-done.18.refs_1_.refs_0_, bf16[256,512]{1,0:T(8,128)(2,1)S(1)} %collective-permute-done.25.refs_1_, ...), custom_call_target="tpu_custom_call", output_to_operand_aliasing={{0}: (6, {}), {1}: (7, {})} | custom-call | flops 1024 | bytes 1024 | tf_op jit(solution)/shard_map/far/pallas_call | solution.py:76
  60.2 4.7 %last.1 = bf16[256,1024]{1,0:T(8,128)(2,1)} custom-call(s32[5]{0:T(128)S(1)} %stack.35.pos_ref, bf16[256,512]{1,0:T(8,128)(2,1)S(1)} %collective-permute-done.24.refs_0_, bf16[256,512]{1,0:T(8,128)(2,1)S(1)} %collective-permute-done.22.refs_1_, bf16[256,512]{1,0:T(8,128)(2,1)S(1)} %collective-permute-done.28.refs_2_, ...), custom_call_target="tpu_custom_call" | custom-call | flops 1024 | bytes 1024 | tf_op jit(solution)/shard_map/last/pallas_call | solution.py:76
  (51 shorter events, 2.5 us)
Async XLA Ops:
  0.1 5.7 %collective-permute-start = (bf16[256,512]{1,0:T(8,128)(2,1)}, bf16[256,512]{1,0:T(8,128)(2,1)S(1)}, u32[]{:S(2)}, u32[]{:S(2)}) collective-permute-start(bf16[256,512]{1,0:T(8,128)(2,1)} %param.6), channel_id=1, source_target_pairs={{0,8},{8,0},{16,24},{24,16},{32,40},{40,32},{48,56},{56,48},{64,72... | collective-permute-start | bytes 786440 | tf_op jit(solution)/shard_map/ppermute | solution.py:35
  1.5 9.3 %collective-permute-start.2 = (bf16[256,512]{1,0:T(8,128)(2,1)}, bf16[256,512]{1,0:T(8,128)(2,1)S(1)}, u32[]{:S(2)}, u32[]{:S(2)}) collective-permute-start(bf16[256,512]{1,0:T(8,128)(2,1)} %param.6), channel_id=1, source_target_pairs={{0,16},{8,56},{16,32},{24,8},{32,48},{40,24},{48,0},{56,40},{64,80... | collective-permute-start | bytes 786440 | tf_op jit(solution)/shard_map/ppermute | solution.py:31
  5.8 5.0 %collective-permute-start.1 = (bf16[4,64,256]{2,1,0:T(8,128)(2,1)S(1)}, bf16[4,64,256]{2,1,0:T(8,128)(2,1)S(1)}, u32[]{:S(2)}, u32[]{:S(2)}) collective-permute-start(bf16[4,64,256]{2,1,0:T(8,128)(2,1)S(1)} %get-tuple-element.52), channel_id=1, source_target_pairs={{0,1},{1,0},{2,3},{3,2},{4,5},{5,4},{6,7},{7,6},{8,9},{9,8},{10,11... | collective-permute-start | bytes 393224 | tf_op jit(solution)/shard_map/ppermute | solution.py:43
  7.2 3.6 %collective-permute-start.3 = (bf16[256,512]{1,0:T(8,128)(2,1)S(1)}, bf16[256,512]{1,0:T(8,128)(2,1)S(1)}, u32[]{:S(2)}, u32[]{:S(2)}) collective-permute-start(bf16[256,512]{1,0:T(8,128)(2,1)S(1)} %collective-permute-done.refs_2_), channel_id=1, source_target_pairs={{0,8},{8,0},{16,24},{24,16},{32,40},{40,32},{48,56},{56,48},{64,72... | collective-permute-start | bytes 786440 | tf_op jit(solution)/shard_map/ppermute | solution.py:35
  7.3 8.8 %collective-permute-start.7 = (bf16[256,512]{1,0:T(8,128)(2,1)S(1)}, bf16[256,512]{1,0:T(8,128)(2,1)S(1)}, u32[]{:S(2)}, u32[]{:S(2)}) collective-permute-start(bf16[256,512]{1,0:T(8,128)(2,1)S(1)} %collective-permute-done.refs_2_), channel_id=1, source_target_pairs={{0,16},{8,56},{16,32},{24,8},{32,48},{40,24},{48,0},{56,40},{64,80... | collective-permute-start | bytes 786440 | tf_op jit(solution)/shard_map/ppermute | solution.py:31
  8.1 10.7 %collective-permute-start.8 = (bf16[256,512]{1,0:T(8,128)(2,1)}, bf16[256,512]{1,0:T(8,128)(2,1)S(1)}, u32[]{:S(2)}, u32[]{:S(2)}) collective-permute-start(bf16[256,512]{1,0:T(8,128)(2,1)} %param.6), channel_id=1, source_target_pairs={{0,64},{8,72},{16,80},{24,88},{32,96},{40,104},{48,112},{56,120},{... | collective-permute-start | bytes 786440 | tf_op jit(solution)/shard_map/ppermute | solution.py:39
  10.8 9.9 %collective-permute-start.9 = (bf16[256,512]{1,0:T(8,128)(2,1)S(1)}, bf16[256,512]{1,0:T(8,128)(2,1)S(1)}, u32[]{:S(2)}, u32[]{:S(2)}) collective-permute-start(bf16[256,512]{1,0:T(8,128)(2,1)S(1)} %collective-permute-done.2.refs_4_.refs_6_), channel_id=1, source_target_pairs={{0,16},{8,56},{16,32},{24,8},{32,48},{40,24},{48,0},{56,40},{64,80... | collective-permute-start | bytes 786440 | tf_op jit(solution)/shard_map/ppermute | solution.py:31
  12.2 6.6 %collective-permute-start.4 = (bf16[2,64,256]{2,1,0:T(8,128)(2,1)S(1)}, bf16[2,64,256]{2,1,0:T(8,128)(2,1)S(1)}, u32[]{:S(2)}, u32[]{:S(2)}) collective-permute-start(bf16[2,64,256]{2,1,0:T(8,128)(2,1)S(1)} %get-tuple-element.55), channel_id=1, source_target_pairs={{0,2},{1,3},{2,4},{3,5},{4,6},{5,7},{6,0},{7,1},{8,10},{9,11},{10,... | collective-permute-start | bytes 196616 | tf_op jit(solution)/shard_map/ppermute | solution.py:47
  13.9 4.9 %collective-permute-start.5 = (bf16[2,64,256]{2,1,0:T(8,128)(2,1)S(1)}, bf16[2,64,256]{2,1,0:T(8,128)(2,1)S(1)}, u32[]{:S(2)}, u32[]{:S(2)}) collective-permute-start(bf16[2,64,256]{2,1,0:T(8,128)(2,1)S(1)} %get-tuple-element.56), channel_id=1, source_target_pairs={{0,6},{1,7},{2,0},{3,1},{4,2},{5,3},{6,4},{7,5},{8,14},{9,15},{10,... | collective-permute-start | bytes 196616 | tf_op jit(solution)/shard_map/ppermute | solution.py:47
  16.1 4.6 %collective-permute-start.6 = (bf16[2,64,256]{2,1,0:T(8,128)(2,1)S(1)}, bf16[2,64,256]{2,1,0:T(8,128)(2,1)S(1)}, u32[]{:S(2)}, u32[]{:S(2)}) collective-permute-start(bf16[2,64,256]{2,1,0:T(8,128)(2,1)S(1)} %pad_maximum_fusion.6), channel_id=1, source_target_pairs={{0,4},{1,5},{2,6},{3,7},{4,0},{5,1},{6,2},{7,3},{8,12},{9,13},{10,... | collective-permute-start | bytes 196616 | tf_op jit(solution)/shard_map/ppermute | solution.py:47
  21.4 4.2 %collective-permute-start.11 = (bf16[512,512]{1,0:T(8,128)(2,1)S(1)}, bf16[512,512]{1,0:T(8,128)(2,1)S(1)}, u32[]{:S(2)}, u32[]{:S(2)}) collective-permute-start(bf16[512,512]{1,0:T(8,128)(2,1)S(1)} %pad_maximum_fusion), channel_id=1, source_target_pairs={{0,8},{8,0},{16,24},{24,16},{32,40},{40,32},{48,56},{56,48},{64,72... | collective-permute-start | bytes 1572872 | tf_op jit(solution)/shard_map/ppermute | solution.py:35
  23.2 2.3 %collective-permute-start.12 = (bf16[256,512]{1,0:T(8,128)(2,1)S(1)}, bf16[256,512]{1,0:T(8,128)(2,1)S(1)}, u32[]{:S(2)}, u32[]{:S(2)}) collective-permute-start(bf16[256,512]{1,0:T(8,128)(2,1)S(1)} %collective-permute-done.8.refs_2_), channel_id=1, source_target_pairs={{0,8},{8,0},{16,24},{24,16},{32,40},{40,32},{48,56},{56,48},{64,72... | collective-permute-start | bytes 786440 | tf_op jit(solution)/shard_map/ppermute | solution.py:35
  23.3 2.2 %collective-permute-start.10 = (bf16[256,512]{1,0:T(8,128)(2,1)S(1)}, bf16[256,512]{1,0:T(8,128)(2,1)S(1)}, u32[]{:S(2)}, u32[]{:S(2)}) collective-permute-start(bf16[256,512]{1,0:T(8,128)(2,1)S(1)} %join.1.refs_1_), channel_id=1, source_target_pairs={{0,8},{8,0},{16,24},{24,16},{32,40},{40,32},{48,56},{56,48},{64,72... | collective-permute-start | bytes 786440 | tf_op jit(solution)/shard_map/ppermute | solution.py:35
  23.7 6.7 %collective-permute-start.15 = (bf16[256,512]{1,0:T(8,128)(2,1)S(1)}, bf16[256,512]{1,0:T(8,128)(2,1)S(1)}, u32[]{:S(2)}, u32[]{:S(2)}) collective-permute-start(bf16[256,512]{1,0:T(8,128)(2,1)S(1)} %join.1.refs_1_), channel_id=1, source_target_pairs={{0,16},{8,56},{16,32},{24,8},{32,48},{40,24},{48,0},{56,40},{64,80... | collective-permute-start | bytes 786440 | tf_op jit(solution)/shard_map/ppermute | solution.py:31
  25.5 14.9 %collective-permute-start.17 = (bf16[512,512]{1,0:T(8,128)(2,1)S(1)}, bf16[512,512]{1,0:T(8,128)(2,1)S(1)}, u32[]{:S(2)}, u32[]{:S(2)}) collective-permute-start(bf16[512,512]{1,0:T(8,128)(2,1)S(1)} %pad_maximum_fusion.1), channel_id=1, source_target_pairs={{0,16},{8,56},{16,32},{24,8},{32,48},{40,24},{48,0},{56,40},{64,80... | collective-permute-start | bytes 1572872 | tf_op jit(solution)/shard_map/ppermute | solution.py:31
  27.3 11.3 %collective-permute-start.13 = (bf16[256,512]{1,0:T(8,128)(2,1)S(1)}, bf16[256,512]{1,0:T(8,128)(2,1)S(1)}, u32[]{:S(2)}, u32[]{:S(2)}) collective-permute-start(bf16[256,512]{1,0:T(8,128)(2,1)S(1)} %collective-permute-done.10.refs_3_), channel_id=1, source_target_pairs={{0,16},{8,56},{16,32},{24,8},{32,48},{40,24},{48,0},{56,40},{64,80... | collective-permute-start | bytes 786440 | tf_op jit(solution)/shard_map/ppermute | solution.py:31
  28.6 10.1 %collective-permute-start.14 = (bf16[256,512]{1,0:T(8,128)(2,1)S(1)}, bf16[256,512]{1,0:T(8,128)(2,1)S(1)}, u32[]{:S(2)}, u32[]{:S(2)}) collective-permute-start(bf16[256,512]{1,0:T(8,128)(2,1)S(1)} %join.1.refs_1_), channel_id=1, source_target_pairs={{0,64},{8,72},{16,80},{24,88},{32,96},{40,104},{48,112},{56,120},{... | collective-permute-start | bytes 786440 | tf_op jit(solution)/shard_map/ppermute | solution.py:39
  30.4 10.1 %collective-permute-start.16 = (bf16[256,512]{1,0:T(8,128)(2,1)S(1)}, bf16[256,512]{1,0:T(8,128)(2,1)S(1)}, u32[]{:S(2)}, u32[]{:S(2)}) collective-permute-start(bf16[256,512]{1,0:T(8,128)(2,1)S(1)} %collective-permute-done.15.refs_7_), channel_id=1, source_target_pairs={{0,16},{8,56},{16,32},{24,8},{32,48},{40,24},{48,0},{56,40},{64,80... | collective-permute-start | bytes 786440 | tf_op jit(solution)/shard_map/ppermute | solution.py:31
  40.5 3.3 %collective-permute-start.21 = (bf16[256,512]{1,0:T(8,128)(2,1)S(1)}, bf16[256,512]{1,0:T(8,128)(2,1)S(1)}, u32[]{:S(2)}, u32[]{:S(2)}) collective-permute-start(bf16[256,512]{1,0:T(8,128)(2,1)S(1)} %collective-permute-done.14.refs_12_), channel_id=1, source_target_pairs={{0,8},{8,0},{16,24},{24,16},{32,40},{40,32},{48,56},{56,48},{64,72... | collective-permute-start | bytes 786440 | tf_op jit(solution)/shard_map/ppermute | solution.py:35
  42.6 5.1 %collective-permute-start.19 = (bf16[512,512]{1,0:T(8,128)(2,1)S(1)}, bf16[512,512]{1,0:T(8,128)(2,1)S(1)}, u32[]{:S(2)}, u32[]{:S(2)}) collective-permute-start(bf16[512,512]{1,0:T(8,128)(2,1)S(1)} %collective-permute-done.17.refs_4_.refs_2_), channel_id=1, source_target_pairs={{0,8},{8,0},{16,24},{24,16},{32,40},{40,32},{48,56},{56,48},{64,72... | collective-permute-start | bytes 1572872 | tf_op jit(solution)/shard_map/ppermute | solution.py:35
  42.7 3.2 %collective-permute-start.18 = (bf16[256,512]{1,0:T(8,128)(2,1)S(1)}, bf16[256,512]{1,0:T(8,128)(2,1)S(1)}, u32[]{:S(2)}, u32[]{:S(2)}) collective-permute-start(bf16[256,512]{1,0:T(8,128)(2,1)S(1)} %collective-permute-done.9.refs_0_), channel_id=1, source_target_pairs={{0,8},{8,0},{16,24},{24,16},{32,40},{40,32},{48,56},{56,48},{64,72... | collective-permute-start | bytes 786440 | tf_op jit(solution)/shard_map/ppermute | solution.py:35
  43.3 5.0 %collective-permute-start.20 = (bf16[512,512]{1,0:T(8,128)(2,1)S(1)}, bf16[512,512]{1,0:T(8,128)(2,1)S(1)}, u32[]{:S(2)}, u32[]{:S(2)}) collective-permute-start(bf16[512,512]{1,0:T(8,128)(2,1)S(1)} %pad_maximum_fusion.2), channel_id=1, source_target_pairs={{0,8},{8,0},{16,24},{24,16},{32,40},{40,32},{48,56},{56,48},{64,72... | collective-permute-start | bytes 1572872 | tf_op jit(solution)/shard_map/ppermute | solution.py:35
  43.8 11.2 %collective-permute-start.23 = (bf16[512,512]{1,0:T(8,128)(2,1)S(1)}, bf16[512,512]{1,0:T(8,128)(2,1)S(1)}, u32[]{:S(2)}, u32[]{:S(2)}) collective-permute-start(bf16[512,512]{1,0:T(8,128)(2,1)S(1)} %pad_maximum_fusion.3), channel_id=1, source_target_pairs={{0,16},{8,56},{16,32},{24,8},{32,48},{40,24},{48,0},{56,40},{64,80... | collective-permute-start | bytes 1572872 | tf_op jit(solution)/shard_map/ppermute | solution.py:31
  44.8 10.2 %collective-permute-start.24 = (bf16[256,512]{1,0:T(8,128)(2,1)S(1)}, bf16[256,512]{1,0:T(8,128)(2,1)S(1)}, u32[]{:S(2)}, u32[]{:S(2)}) collective-permute-start(bf16[256,512]{1,0:T(8,128)(2,1)S(1)} %slice.40), channel_id=1, source_target_pairs={{0,16},{8,56},{16,32},{24,8},{32,48},{40,24},{48,0},{56,40},{64,80... | collective-permute-start | bytes 786440 | tf_op jit(solution)/shard_map/ppermute | solution.py:31
  45.9 9.2 %collective-permute-start.22 = (bf16[256,512]{1,0:T(8,128)(2,1)S(1)}, bf16[256,512]{1,0:T(8,128)(2,1)S(1)}, u32[]{:S(2)}, u32[]{:S(2)}) collective-permute-start(bf16[256,512]{1,0:T(8,128)(2,1)S(1)} %collective-permute-done.16.refs_14_), channel_id=1, source_target_pairs={{0,64},{8,72},{16,80},{24,88},{32,96},{40,104},{48,112},{56,120},{... | collective-permute-start | bytes 786440 | tf_op jit(solution)/shard_map/ppermute | solution.py:39
  47.8 7.3 %collective-permute-start.25 = (bf16[256,512]{1,0:T(8,128)(2,1)S(1)}, bf16[256,512]{1,0:T(8,128)(2,1)S(1)}, u32[]{:S(2)}, u32[]{:S(2)}) collective-permute-start(bf16[256,512]{1,0:T(8,128)(2,1)S(1)} %collective-permute-done.16.refs_14_), channel_id=1, source_target_pairs={{0,8},{8,0},{16,24},{24,16},{32,40},{40,32},{48,56},{56,48},{64,72... | collective-permute-start | bytes 786440 | tf_op jit(solution)/shard_map/ppermute | solution.py:35
  48.3 11.9 %copy-start = (bf16[4,64,1024]{2,1,0:T(8,128)(2,1)S(1)}, bf16[4,64,1024]{2,1,0:T(8,128)(2,1)}, u32[]{:S(2)}) copy-start(bf16[4,64,1024]{2,1,0:T(8,128)(2,1)} %param.10) | copy-start | bytes 1572868
  48.3 11.9 %copy-start.2 = (f32[4,1024]{1,0:T(4,128)S(1)}, f32[4,1024]{1,0:T(4,128)}, u32[]{:S(2)}) copy-start(f32[4,1024]{1,0:T(4,128)} %refs_12_.1) | copy-start | bytes 49156
  48.3 11.9 %copy-start.3 = (s32[256]{0:T(256)S(1)}, s32[256]{0:T(256)}, u32[]{:S(2)}) copy-start(s32[256]{0:T(256)} %param.7) | copy-start | bytes 3076
  55.1 5.1 %collective-permute-start.27 = (bf16[512,512]{1,0:T(8,128)(2,1)S(1)}, bf16[512,512]{1,0:T(8,128)(2,1)S(1)}, u32[]{:S(2)}, u32[]{:S(2)}) collective-permute-start(bf16[512,512]{1,0:T(8,128)(2,1)S(1)} %collective-permute-done.23.refs_3_), channel_id=1, source_target_pairs={{0,8},{8,0},{16,24},{24,16},{32,40},{40,32},{48,56},{56,48},{64,72... | collective-permute-start | bytes 1572872 | tf_op jit(solution)/shard_map/ppermute | solution.py:35
  57.6 2.5 %collective-permute-start.26 = (bf16[256,512]{1,0:T(8,128)(2,1)S(1)}, bf16[256,512]{1,0:T(8,128)(2,1)S(1)}, u32[]{:S(2)}, u32[]{:S(2)}) collective-permute-start(bf16[256,512]{1,0:T(8,128)(2,1)S(1)} %collective-permute-done.22.refs_1_), channel_id=1, source_target_pairs={{0,8},{8,0},{16,24},{24,16},{32,40},{40,32},{48,56},{56,48},{64,72... | collective-permute-start | bytes 786440 | tf_op jit(solution)/shard_map/ppermute | solution.py:35
  57.7 2.5 %collective-permute-start.28 = (bf16[256,512]{1,0:T(8,128)(2,1)S(1)}, bf16[256,512]{1,0:T(8,128)(2,1)S(1)}, u32[]{:S(2)}, u32[]{:S(2)}) collective-permute-start(bf16[256,512]{1,0:T(8,128)(2,1)S(1)} %collective-permute-done.24.refs_0_), channel_id=1, source_target_pairs={{0,8},{8,0},{16,24},{24,16},{32,40},{40,32},{48,56},{56,48},{64,72... | collective-permute-start | bytes 786440 | tf_op jit(solution)/shard_map/ppermute | solution.py:35
  (1 other events, 1.0 us)

commit v5 on v4

--- a/solution.py
+++ b/solution.py
@@ -281,6 +281,7 @@
     depth, cols = ops.arrays[0].shape[1], weight.shape[1]
     adapters, width, tokens = mag.shape[0], up.shape[0], base[0].shape[0]
     rank = width // adapters
+    parts = [*tiles(cols - TN), *(slice(lo, lo + TN // 2) for lo in range(cols - TN, cols, TN // 2))]
 
     def body(pos_ref, *refs):
         w_ref, base_ref, sq_ref, cross_ref, both_ref, up_ref, mag_ref, id_ref = refs[count : count + 8]
@@ -299,9 +300,10 @@
         gram_hi = gram.astype(BF16)
         gram_lo = (gram - gram_hi.astype(F32)).astype(BF16)
         left = jnp.concatenate([low, gram_hi, gram_lo], axis=0)
-        own_tile = jnp.concatenate([own] * (TN // 128), axis=1)
+        own_wide = jnp.concatenate([own] * (TN // 128), axis=1)
         copies = []
-        for n, tile in enumerate(tiles(cols)):
+        for n, tile in enumerate(parts):
+            span = tile.stop - tile.start
             base, sq, cross = base_ref[:, tile], sq_ref[:, tile], cross_ref[:, tile]
             for row, item in zip(both_rows, both):
                 w = w_ref[pl.ds(row, depth), tile]
@@ -320,17 +322,17 @@
             for a in range(adapters):
                 mine = jnp.sum(terms[a * rank : (a + 1) * rank], axis=0, keepdims=True)
                 gain = mag_ref[a : a + 1, tile] / jnp.sqrt(weight_sq + mine + 1e-6)
-                wide = jnp.broadcast_to(gain, (tokens, TN))
-                scale = wide if scale is None else jnp.where(own_tile == a, wide, scale)
-            held[n] = (scale * (base + prod[:tokens])).astype(BF16)
-            copies.append(pltpu.make_async_copy(held.at[n], out_ref.at[:, tile], sems.at[n]))
+                wide = jnp.broadcast_to(gain, (tokens, span))
+                scale = wide if scale is None else jnp.where(own_wide[:, :span] == a, wide, scale)
+            held[:, tile] = (scale * (base + prod[:tokens])).astype(BF16)
+            copies.append(pltpu.make_async_copy(held.at[:, tile], out_ref.at[:, tile], sems.at[n]))
             copies[n].start()
         for copy in copies:
             copy.wait()
 
     inputs = (pos, *ops.arrays, weight, *base, *norm, up, mag, ids)
     outs = [jax.ShapeDtypeStruct((tokens, cols), BF16)]
-    scratch = [pltpu.VMEM((cols // TN, tokens, TN), BF16), pltpu.SemaphoreType.DMA((cols // TN,))]
+    scratch = [pltpu.VMEM((tokens, cols), BF16), pltpu.SemaphoreType.DMA((len(parts),))]
     return call(body, "last", inputs, [SM] + [VM] * (count + 8), outs, scratch, out_specs=[ANY])[0]
 
 

time: 65.2 us -> 65.1 us (level)
  no operation moved by 1% of the time
where the time goes in v5:
time: 65.1 us; the launch traced here: 64.9 us
  starting transfers between devices  36.1 us (55%)
  Pallas kernels  20.7 us (32%)
  waiting for transfers between devices  6.33 us (10%)
  local copies, waits for them, and re-layouts  1.17 us (2%)
    pallas_call x6, Pallas kernels, call(): pl.pallas_call(body, out_shape=outs, in_specs=specs, out_specs=out_specs...  20.7 us
    ppermute x9, starting transfers between devices, ring(): return lax.ppermute(a, 'row', RING)  13 us
    ppermute x13, starting transfers between devices, core(): return lax.ppermute(a, 'row', CORE)  10.2 us
    ppermute x3, starting transfers between devices, pair(): return lax.ppermute(a, 'row', PAIR)  6.39 us
    ppermute x3, starting transfers between devices, zshift(): lax.ppermute(a, 'ad', [(z * 2 + yl, (z + step) % 4 * 2 + yl) for z, yl in...  5.13 us
    ppermute x9, waiting for transfers between devices, ring(): return lax.ppermute(a, 'row', RING)  2.5 us
    ppermute x3, waiting for transfers between devices, zshift(): lax.ppermute(a, 'ad', [(z * 2 + yl, (z + step) % 4 * 2 + yl) for z, yl in...  1.9 us
    ppermute x3, waiting for transfers between devices, pair(): return lax.ppermute(a, 'row', PAIR)  1.46 us
  transfers between devices with their start and end apart: 29, of which 5 were waited for; matrix products, arithmetic and copies ran while one was open for 0% of the time, Pallas kernels for 24%

profile of v5, /device:TPU:1, one launch (start us, length us, event | category | flops | bytes accessed | tf_op | source)
XLA Modules:
  0.0 64.9 jit_solution(10655632107666889002)
XLA Ops:
  0.1 1.4 %collective-permute-start = (bf16[256,512]{1,0:T(8,128)(2,1)}, bf16[256,512]{1,0:T(8,128)(2,1)S(1)}, u32[]{:S(2)}, u32[]{:S(2)}) collective-permute-start(bf16[256,512]{1,0:T(8,128)(2,1)} %param.6), channel_id=1, source_target_pairs={{0,8},{8,0},{16,24},{24,16},{32,40},{40,32},{48,56},{56,48},{64,72... | collective-permute-start | bytes 786440 | tf_op jit(solution)/shard_map/ppermute | solution.py:35
  1.5 2.6 %collective-permute-start.2 = (bf16[256,512]{1,0:T(8,128)(2,1)}, bf16[256,512]{1,0:T(8,128)(2,1)S(1)}, u32[]{:S(2)}, u32[]{:S(2)}) collective-permute-start(bf16[256,512]{1,0:T(8,128)(2,1)} %param.6), channel_id=1, source_target_pairs={{0,16},{8,56},{16,32},{24,8},{32,48},{40,24},{48,0},{56,40},{64,80... | collective-permute-start | bytes 786440 | tf_op jit(solution)/shard_map/ppermute | solution.py:31
  4.1 1.0 %copy-done.1 = bf16[32,64,64]{2,1,0:T(8,128)(2,1)S(1)} copy-done((bf16[32,64,64]{2,1,0:T(8,128)(2,1)S(1)}, bf16[32,64,64]{2,1,0:T(8,128)(2,1)}, u32[]{:S(2)}) %copy-start.1) | copy-done | bytes 262168
  5.1 0.7 %pack.1 = (bf16[4,64,256]{2,1,0:T(8,128)(2,1)S(1)}, bf16[4,64,256]{2,1,0:T(8,128)(2,1)S(1)}) custom-call(s32[5]{0:T(128)S(1)} %stack.35.pos_ref, bf16[32,64,64]{2,1,0:T(8,128)(2,1)S(1)} %copy-done.1), custom_call_target="tpu_custom_call" | custom-call | flops 1024 | bytes 1024 | tf_op jit(solution)/shard_map/pack/pallas_call | solution.py:76
  5.8 1.4 %collective-permute-start.1 = (bf16[4,64,256]{2,1,0:T(8,128)(2,1)S(1)}, bf16[4,64,256]{2,1,0:T(8,128)(2,1)S(1)}, u32[]{:S(2)}, u32[]{:S(2)}) collective-permute-start(bf16[4,64,256]{2,1,0:T(8,128)(2,1)S(1)} %get-tuple-element.52), channel_id=1, source_target_pairs={{0,1},{1,0},{2,3},{3,2},{4,5},{5,4},{6,7},{7,6},{8,9},{9,8},{10,11... | collective-permute-start | bytes 393224 | tf_op jit(solution)/shard_map/ppermute | solution.py:43
  7.3 0.8 %collective-permute-start.7 = (bf16[256,512]{1,0:T(8,128)(2,1)S(1)}, bf16[256,512]{1,0:T(8,128)(2,1)S(1)}, u32[]{:S(2)}, u32[]{:S(2)}) collective-permute-start(bf16[256,512]{1,0:T(8,128)(2,1)S(1)} %collective-permute-done.refs_2_), channel_id=1, source_target_pairs={{0,16},{8,56},{16,32},{24,8},{32,48},{40,24},{48,0},{56,40},{64,80... | collective-permute-start | bytes 786440 | tf_op jit(solution)/shard_map/ppermute | solution.py:31
  8.1 2.6 %collective-permute-start.8 = (bf16[256,512]{1,0:T(8,128)(2,1)}, bf16[256,512]{1,0:T(8,128)(2,1)S(1)}, u32[]{:S(2)}, u32[]{:S(2)}) collective-permute-start(bf16[256,512]{1,0:T(8,128)(2,1)} %param.6), channel_id=1, source_target_pairs={{0,64},{8,72},{16,80},{24,88},{32,96},{40,104},{48,112},{56,120},{... | collective-permute-start | bytes 786440 | tf_op jit(solution)/shard_map/ppermute | solution.py:39
  10.8 1.3 %collective-permute-start.9 = (bf16[256,512]{1,0:T(8,128)(2,1)S(1)}, bf16[256,512]{1,0:T(8,128)(2,1)S(1)}, u32[]{:S(2)}, u32[]{:S(2)}) collective-permute-start(bf16[256,512]{1,0:T(8,128)(2,1)S(1)} %collective-permute-done.2.refs_4_.refs_6_), channel_id=1, source_target_pairs={{0,16},{8,56},{16,32},{24,8},{32,48},{40,24},{48,0},{56,40},{64,80... | collective-permute-start | bytes 786440 | tf_op jit(solution)/shard_map/ppermute | solution.py:31
  12.2 1.7 %collective-permute-start.4 = (bf16[2,64,256]{2,1,0:T(8,128)(2,1)S(1)}, bf16[2,64,256]{2,1,0:T(8,128)(2,1)S(1)}, u32[]{:S(2)}, u32[]{:S(2)}) collective-permute-start(bf16[2,64,256]{2,1,0:T(8,128)(2,1)S(1)} %get-tuple-element.55), channel_id=1, source_target_pairs={{0,2},{1,3},{2,4},{3,5},{4,6},{5,7},{6,0},{7,1},{8,10},{9,11},{10,... | collective-permute-start | bytes 196616 | tf_op jit(solution)/shard_map/ppermute | solution.py:47
  13.9 2.2 %collective-permute-start.5 = (bf16[2,64,256]{2,1,0:T(8,128)(2,1)S(1)}, bf16[2,64,256]{2,1,0:T(8,128)(2,1)S(1)}, u32[]{:S(2)}, u32[]{:S(2)}) collective-permute-start(bf16[2,64,256]{2,1,0:T(8,128)(2,1)S(1)} %get-tuple-element.56), channel_id=1, source_target_pairs={{0,6},{1,7},{2,0},{3,1},{4,2},{5,3},{6,4},{7,5},{8,14},{9,15},{10,... | collective-permute-start | bytes 196616 | tf_op jit(solution)/shard_map/ppermute | solution.py:47
  16.1 1.2 %collective-permute-start.6 = (bf16[2,64,256]{2,1,0:T(8,128)(2,1)S(1)}, bf16[2,64,256]{2,1,0:T(8,128)(2,1)S(1)}, u32[]{:S(2)}, u32[]{:S(2)}) collective-permute-start(bf16[2,64,256]{2,1,0:T(8,128)(2,1)S(1)} %pad_maximum_fusion.6), channel_id=1, source_target_pairs={{0,4},{1,5},{2,6},{3,7},{4,0},{5,1},{6,2},{7,3},{8,12},{9,13},{10,... | collective-permute-start | bytes 196616 | tf_op jit(solution)/shard_map/ppermute | solution.py:47
  17.3 1.5 %collective-permute-done.8.refs_2_ = bf16[256,512]{1,0:T(8,128)(2,1)S(1)} collective-permute-done((bf16[256,512]{1,0:T(8,128)(2,1)}, bf16[256,512]{1,0:T(8,128)(2,1)S(1)}, u32[]{:S(2)}, u32[]{:S(2)}) %collective-permute-start.8) | collective-permute-done | bytes 262176 | tf_op jit(solution)/shard_map/ppermute | solution.py:39
  18.8 1.9 %collective-permute-done.6.a2 = bf16[2,64,256]{2,1,0:T(8,128)(2,1)S(1)} collective-permute-done((bf16[2,64,256]{2,1,0:T(8,128)(2,1)S(1)}, bf16[2,64,256]{2,1,0:T(8,128)(2,1)S(1)}, u32[]{:S(2)}, u32[]{:S(2)}) %collective-permute-start.6) | collective-permute-done | bytes 65568 | tf_op jit(solution)/shard_map/ppermute | solution.py:47
  20.7 0.7 %join.1.refs_1_ = bf16[256,512]{1,0:T(8,128)(2,1)S(1)} custom-call(s32[5]{0:T(128)S(1)} %stack.35.pos_ref, bf16[2,64,256]{2,1,0:T(8,128)(2,1)S(1)} %pad_maximum_fusion.7.a0, bf16[2,64,256]{2,1,0:T(8,128)(2,1)S(1)} %collective-permute-done.4.a1, bf16[2,64,256]{2,1,0:T(8,128)(2,1)S(1)} %collective-permute-done.6.a2, ...), custom_call_target="tpu_custom_call" | custom-call | flops 1024 | bytes 1024 | tf_op jit(solution)/shard_map/join/pallas_call | solution.py:76
  21.4 1.8 %collective-permute-start.11 = (bf16[512,512]{1,0:T(8,128)(2,1)S(1)}, bf16[512,512]{1,0:T(8,128)(2,1)S(1)}, u32[]{:S(2)}, u32[]{:S(2)}) collective-permute-start(bf16[512,512]{1,0:T(8,128)(2,1)S(1)} %pad_maximum_fusion), channel_id=1, source_target_pairs={{0,8},{8,0},{16,24},{24,16},{32,40},{40,32},{48,56},{56,48},{64,72... | collective-permute-start | bytes 1572872 | tf_op jit(solution)/shard_map/ppermute | solution.py:35
  23.7 1.8 %collective-permute-start.15 = (bf16[256,512]{1,0:T(8,128)(2,1)S(1)}, bf16[256,512]{1,0:T(8,128)(2,1)S(1)}, u32[]{:S(2)}, u32[]{:S(2)}) collective-permute-start(bf16[256,512]{1,0:T(8,128)(2,1)S(1)} %join.1.refs_1_), channel_id=1, source_target_pairs={{0,16},{8,56},{16,32},{24,8},{32,48},{40,24},{48,0},{56,40},{64,80... | collective-permute-start | bytes 786440 | tf_op jit(solution)/shard_map/ppermute | solution.py:31
  25.5 1.7 %collective-permute-start.17 = (bf16[512,512]{1,0:T(8,128)(2,1)S(1)}, bf16[512,512]{1,0:T(8,128)(2,1)S(1)}, u32[]{:S(2)}, u32[]{:S(2)}) collective-permute-start(bf16[512,512]{1,0:T(8,128)(2,1)S(1)} %pad_maximum_fusion.1), channel_id=1, source_target_pairs={{0,16},{8,56},{16,32},{24,8},{32,48},{40,24},{48,0},{56,40},{64,80... | collective-permute-start | bytes 1572872 | tf_op jit(solution)/shard_map/ppermute | solution.py:31
  27.3 1.3 %collective-permute-start.13 = (bf16[256,512]{1,0:T(8,128)(2,1)S(1)}, bf16[256,512]{1,0:T(8,128)(2,1)S(1)}, u32[]{:S(2)}, u32[]{:S(2)}) collective-permute-start(bf16[256,512]{1,0:T(8,128)(2,1)S(1)} %collective-permute-done.10.refs_3_), channel_id=1, source_target_pairs={{0,16},{8,56},{16,32},{24,8},{32,48},{40,24},{48,0},{56,40},{64,80... | collective-permute-start | bytes 786440 | tf_op jit(solution)/shard_map/ppermute | solution.py:31
  28.6 1.8 %collective-permute-start.14 = (bf16[256,512]{1,0:T(8,128)(2,1)S(1)}, bf16[256,512]{1,0:T(8,128)(2,1)S(1)}, u32[]{:S(2)}, u32[]{:S(2)}) collective-permute-start(bf16[256,512]{1,0:T(8,128)(2,1)S(1)} %join.1.refs_1_), channel_id=1, source_target_pairs={{0,64},{8,72},{16,80},{24,88},{32,96},{40,104},{48,112},{56,120},{... | collective-permute-start | bytes 786440 | tf_op jit(solution)/shard_map/ppermute | solution.py:39
  30.4 1.5 %collective-permute-start.16 = (bf16[256,512]{1,0:T(8,128)(2,1)S(1)}, bf16[256,512]{1,0:T(8,128)(2,1)S(1)}, u32[]{:S(2)}, u32[]{:S(2)}) collective-permute-start(bf16[256,512]{1,0:T(8,128)(2,1)S(1)} %collective-permute-done.15.refs_7_), channel_id=1, source_target_pairs={{0,16},{8,56},{16,32},{24,8},{32,48},{40,24},{48,0},{56,40},{64,80... | collective-permute-start | bytes 786440 | tf_op jit(solution)/shard_map/ppermute | solution.py:31
  31.9 6.7 %first.1 = (bf16[8192,1024]{1,0:T(8,128)(2,1)S(1)}, f32[256,1024]{1,0:T(8,128)S(1)}, f32[8,1024]{1,0:T(8,128)S(1)}, f32[256,1024]{1,0:T(8,128)S(1)}, f32[512,256]{1,0:T(8,128)S(1)}) custom-call(s32[5]{0:T(128)S(1)} %stack.35.pos_ref, bf16[256,512]{1,0:T(8,128)(2,1)S(1)} %collective-permute-done.3.refs_0_, bf16[256,512]{1,0:T(8,128)(2,1)S(1)} %join.1.refs_1_, ...), custom_call_target="tpu_custom_call" | custom-call | flops 1024 | bytes 1024 | tf_op jit(solution)/shard_map/first/pallas_call | solution.py:76
  38.6 1.8 %collective-permute-done.16.refs_14_ = bf16[256,512]{1,0:T(8,128)(2,1)S(1)} collective-permute-done((bf16[256,512]{1,0:T(8,128)(2,1)S(1)}, bf16[256,512]{1,0:T(8,128)(2,1)S(1)}, u32[]{:S(2)}, u32[]{:S(2)}) %collective-permute-start.16) | collective-permute-done | bytes 262176 | tf_op jit(solution)/shard_map/ppermute | solution.py:31
  40.5 2.2 %collective-permute-start.21 = (bf16[256,512]{1,0:T(8,128)(2,1)S(1)}, bf16[256,512]{1,0:T(8,128)(2,1)S(1)}, u32[]{:S(2)}, u32[]{:S(2)}) collective-permute-start(bf16[256,512]{1,0:T(8,128)(2,1)S(1)} %collective-permute-done.14.refs_12_), channel_id=1, source_target_pairs={{0,8},{8,0},{16,24},{24,16},{32,40},{40,32},{48,56},{56,48},{64,72... | collective-permute-start | bytes 786440 | tf_op jit(solution)/shard_map/ppermute | solution.py:35
  42.7 0.6 collective-permute-start.18
  43.8 1.0 %collective-permute-start.23 = (bf16[512,512]{1,0:T(8,128)(2,1)S(1)}, bf16[512,512]{1,0:T(8,128)(2,1)S(1)}, u32[]{:S(2)}, u32[]{:S(2)}) collective-permute-start(bf16[512,512]{1,0:T(8,128)(2,1)S(1)} %pad_maximum_fusion.3), channel_id=1, source_target_pairs={{0,16},{8,56},{16,32},{24,8},{32,48},{40,24},{48,0},{56,40},{64,80... | collective-permute-start | bytes 1572872 | tf_op jit(solution)/shard_map/ppermute | solution.py:31
  44.8 1.0 %collective-permute-start.24 = (bf16[256,512]{1,0:T(8,128)(2,1)S(1)}, bf16[256,512]{1,0:T(8,128)(2,1)S(1)}, u32[]{:S(2)}, u32[]{:S(2)}) collective-permute-start(bf16[256,512]{1,0:T(8,128)(2,1)S(1)} %slice.40), channel_id=1, source_target_pairs={{0,16},{8,56},{16,32},{24,8},{32,48},{40,24},{48,0},{56,40},{64,80... | collective-permute-start | bytes 786440 | tf_op jit(solution)/shard_map/ppermute | solution.py:31
  45.9 1.9 %collective-permute-start.22 = (bf16[256,512]{1,0:T(8,128)(2,1)S(1)}, bf16[256,512]{1,0:T(8,128)(2,1)S(1)}, u32[]{:S(2)}, u32[]{:S(2)}) collective-permute-start(bf16[256,512]{1,0:T(8,128)(2,1)S(1)} %collective-permute-done.16.refs_14_), channel_id=1, source_target_pairs={{0,64},{8,72},{16,80},{24,88},{32,96},{40,104},{48,112},{56,120},{... | collective-permute-start | bytes 786440 | tf_op jit(solution)/shard_map/ppermute | solution.py:39
  48.3 6.1 %middle.1 = (f32[256,1024]{1,0:T(8,128)S(1)}, f32[8,1024]{1,0:T(8,128)S(1)}, f32[256,1024]{1,0:T(8,128)S(1)}, f32[512,256]{1,0:T(8,128)S(1)}) custom-call(s32[5]{0:T(128)S(1)} %stack.35.pos_ref, bf16[256,512]{1,0:T(8,128)(2,1)S(1)} %collective-permute-done.9.refs_0_, ...), custom_call_target="tpu_custom_call", output_to_operand_aliasing={{0}: (17, {}), {1}: (18, {}), {2}: (19, {}), {3}: (20, {})} | custom-call | flops 1024 | bytes 1024 | tf_op jit(solution)/shard_map/middle/pallas_call | solution.py:76
  54.4 0.6 collective-permute-done.24.refs_0_
  55.1 2.5 %collective-permute-start.27 = (bf16[512,512]{1,0:T(8,128)(2,1)S(1)}, bf16[512,512]{1,0:T(8,128)(2,1)S(1)}, u32[]{:S(2)}, u32[]{:S(2)}) collective-permute-start(bf16[512,512]{1,0:T(8,128)(2,1)S(1)} %collective-permute-done.23.refs_3_), channel_id=1, source_target_pairs={{0,8},{8,0},{16,24},{24,16},{32,40},{40,32},{48,56},{56,48},{64,72... | collective-permute-start | bytes 1572872 | tf_op jit(solution)/shard_map/ppermute | solution.py:35
  58.1 2.0 %far.1 = (f32[256,1024]{1,0:T(8,128)S(1)}, f32[512,256]{1,0:T(8,128)S(1)}) custom-call(s32[5]{0:T(128)S(1)} %stack.35.pos_ref, bf16[256,512]{1,0:T(8,128)(2,1)S(1)} %collective-permute-done.18.refs_1_.refs_0_, bf16[256,512]{1,0:T(8,128)(2,1)S(1)} %collective-permute-done.25.refs_1_, ...), custom_call_target="tpu_custom_call", output_to_operand_aliasing={{0}: (6, {}), {1}: (7, {})} | custom-call | flops 1024 | bytes 1024 | tf_op jit(solution)/shard_map/far/pallas_call | solution.py:76
  60.2 4.6 %last.1 = bf16[256,1024]{1,0:T(8,128)(2,1)} custom-call(s32[5]{0:T(128)S(1)} %stack.35.pos_ref, bf16[256,512]{1,0:T(8,128)(2,1)S(1)} %collective-permute-done.24.refs_0_, bf16[256,512]{1,0:T(8,128)(2,1)S(1)} %collective-permute-done.22.refs_1_, bf16[256,512]{1,0:T(8,128)(2,1)S(1)} %collective-permute-done.28.refs_2_, ...), custom_call_target="tpu_custom_call" | custom-call | flops 1024 | bytes 1024 | tf_op jit(solution)/shard_map/last/pallas_call | solution.py:76
  (51 shorter events, 2.5 us)
Async XLA Ops:
  0.1 5.7 %collective-permute-start = (bf16[256,512]{1,0:T(8,128)(2,1)}, bf16[256,512]{1,0:T(8,128)(2,1)S(1)}, u32[]{:S(2)}, u32[]{:S(2)}) collective-permute-start(bf16[256,512]{1,0:T(8,128)(2,1)} %param.6), channel_id=1, source_target_pairs={{0,8},{8,0},{16,24},{24,16},{32,40},{40,32},{48,56},{56,48},{64,72... | collective-permute-start | bytes 786440 | tf_op jit(solution)/shard_map/ppermute | solution.py:35
  1.5 9.3 %collective-permute-start.2 = (bf16[256,512]{1,0:T(8,128)(2,1)}, bf16[256,512]{1,0:T(8,128)(2,1)S(1)}, u32[]{:S(2)}, u32[]{:S(2)}) collective-permute-start(bf16[256,512]{1,0:T(8,128)(2,1)} %param.6), channel_id=1, source_target_pairs={{0,16},{8,56},{16,32},{24,8},{32,48},{40,24},{48,0},{56,40},{64,80... | collective-permute-start | bytes 786440 | tf_op jit(solution)/shard_map/ppermute | solution.py:31
  5.8 5.0 %collective-permute-start.1 = (bf16[4,64,256]{2,1,0:T(8,128)(2,1)S(1)}, bf16[4,64,256]{2,1,0:T(8,128)(2,1)S(1)}, u32[]{:S(2)}, u32[]{:S(2)}) collective-permute-start(bf16[4,64,256]{2,1,0:T(8,128)(2,1)S(1)} %get-tuple-element.52), channel_id=1, source_target_pairs={{0,1},{1,0},{2,3},{3,2},{4,5},{5,4},{6,7},{7,6},{8,9},{9,8},{10,11... | collective-permute-start | bytes 393224 | tf_op jit(solution)/shard_map/ppermute | solution.py:43
  7.2 3.6 %collective-permute-start.3 = (bf16[256,512]{1,0:T(8,128)(2,1)S(1)}, bf16[256,512]{1,0:T(8,128)(2,1)S(1)}, u32[]{:S(2)}, u32[]{:S(2)}) collective-permute-start(bf16[256,512]{1,0:T(8,128)(2,1)S(1)} %collective-permute-done.refs_2_), channel_id=1, source_target_pairs={{0,8},{8,0},{16,24},{24,16},{32,40},{40,32},{48,56},{56,48},{64,72... | collective-permute-start | bytes 786440 | tf_op jit(solution)/shard_map/ppermute | solution.py:35
  7.3 8.8 %collective-permute-start.7 = (bf16[256,512]{1,0:T(8,128)(2,1)S(1)}, bf16[256,512]{1,0:T(8,128)(2,1)S(1)}, u32[]{:S(2)}, u32[]{:S(2)}) collective-permute-start(bf16[256,512]{1,0:T(8,128)(2,1)S(1)} %collective-permute-done.refs_2_), channel_id=1, source_target_pairs={{0,16},{8,56},{16,32},{24,8},{32,48},{40,24},{48,0},{56,40},{64,80... | collective-permute-start | bytes 786440 | tf_op jit(solution)/shard_map/ppermute | solution.py:31
  8.1 10.7 %collective-permute-start.8 = (bf16[256,512]{1,0:T(8,128)(2,1)}, bf16[256,512]{1,0:T(8,128)(2,1)S(1)}, u32[]{:S(2)}, u32[]{:S(2)}) collective-permute-start(bf16[256,512]{1,0:T(8,128)(2,1)} %param.6), channel_id=1, source_target_pairs={{0,64},{8,72},{16,80},{24,88},{32,96},{40,104},{48,112},{56,120},{... | collective-permute-start | bytes 786440 | tf_op jit(solution)/shard_map/ppermute | solution.py:39
  10.8 9.9 %collective-permute-start.9 = (bf16[256,512]{1,0:T(8,128)(2,1)S(1)}, bf16[256,512]{1,0:T(8,128)(2,1)S(1)}, u32[]{:S(2)}, u32[]{:S(2)}) collective-permute-start(bf16[256,512]{1,0:T(8,128)(2,1)S(1)} %collective-permute-done.2.refs_4_.refs_6_), channel_id=1, source_target_pairs={{0,16},{8,56},{16,32},{24,8},{32,48},{40,24},{48,0},{56,40},{64,80... | collective-permute-start | bytes 786440 | tf_op jit(solution)/shard_map/ppermute | solution.py:31
  12.2 6.6 %collective-permute-start.4 = (bf16[2,64,256]{2,1,0:T(8,128)(2,1)S(1)}, bf16[2,64,256]{2,1,0:T(8,128)(2,1)S(1)}, u32[]{:S(2)}, u32[]{:S(2)}) collective-permute-start(bf16[2,64,256]{2,1,0:T(8,128)(2,1)S(1)} %get-tuple-element.55), channel_id=1, source_target_pairs={{0,2},{1,3},{2,4},{3,5},{4,6},{5,7},{6,0},{7,1},{8,10},{9,11},{10,... | collective-permute-start | bytes 196616 | tf_op jit(solution)/shard_map/ppermute | solution.py:47
  13.9 4.9 %collective-permute-start.5 = (bf16[2,64,256]{2,1,0:T(8,128)(2,1)S(1)}, bf16[2,64,256]{2,1,0:T(8,128)(2,1)S(1)}, u32[]{:S(2)}, u32[]{:S(2)}) collective-permute-start(bf16[2,64,256]{2,1,0:T(8,128)(2,1)S(1)} %get-tuple-element.56), channel_id=1, source_target_pairs={{0,6},{1,7},{2,0},{3,1},{4,2},{5,3},{6,4},{7,5},{8,14},{9,15},{10,... | collective-permute-start | bytes 196616 | tf_op jit(solution)/shard_map/ppermute | solution.py:47
  16.1 4.6 %collective-permute-start.6 = (bf16[2,64,256]{2,1,0:T(8,128)(2,1)S(1)}, bf16[2,64,256]{2,1,0:T(8,128)(2,1)S(1)}, u32[]{:S(2)}, u32[]{:S(2)}) collective-permute-start(bf16[2,64,256]{2,1,0:T(8,128)(2,1)S(1)} %pad_maximum_fusion.6), channel_id=1, source_target_pairs={{0,4},{1,5},{2,6},{3,7},{4,0},{5,1},{6,2},{7,3},{8,12},{9,13},{10,... | collective-permute-start | bytes 196616 | tf_op jit(solution)/shard_map/ppermute | solution.py:47
  21.4 4.2 %collective-permute-start.11 = (bf16[512,512]{1,0:T(8,128)(2,1)S(1)}, bf16[512,512]{1,0:T(8,128)(2,1)S(1)}, u32[]{:S(2)}, u32[]{:S(2)}) collective-permute-start(bf16[512,512]{1,0:T(8,128)(2,1)S(1)} %pad_maximum_fusion), channel_id=1, source_target_pairs={{0,8},{8,0},{16,24},{24,16},{32,40},{40,32},{48,56},{56,48},{64,72... | collective-permute-start | bytes 1572872 | tf_op jit(solution)/shard_map/ppermute | solution.py:35
  23.2 2.3 %collective-permute-start.12 = (bf16[256,512]{1,0:T(8,128)(2,1)S(1)}, bf16[256,512]{1,0:T(8,128)(2,1)S(1)}, u32[]{:S(2)}, u32[]{:S(2)}) collective-permute-start(bf16[256,512]{1,0:T(8,128)(2,1)S(1)} %collective-permute-done.8.refs_2_), channel_id=1, source_target_pairs={{0,8},{8,0},{16,24},{24,16},{32,40},{40,32},{48,56},{56,48},{64,72... | collective-permute-start | bytes 786440 | tf_op jit(solution)/shard_map/ppermute | solution.py:35
  23.3 2.2 %collective-permute-start.10 = (bf16[256,512]{1,0:T(8,128)(2,1)S(1)}, bf16[256,512]{1,0:T(8,128)(2,1)S(1)}, u32[]{:S(2)}, u32[]{:S(2)}) collective-permute-start(bf16[256,512]{1,0:T(8,128)(2,1)S(1)} %join.1.refs_1_), channel_id=1, source_target_pairs={{0,8},{8,0},{16,24},{24,16},{32,40},{40,32},{48,56},{56,48},{64,72... | collective-permute-start | bytes 786440 | tf_op jit(solution)/shard_map/ppermute | solution.py:35
  23.7 6.7 %collective-permute-start.15 = (bf16[256,512]{1,0:T(8,128)(2,1)S(1)}, bf16[256,512]{1,0:T(8,128)(2,1)S(1)}, u32[]{:S(2)}, u32[]{:S(2)}) collective-permute-start(bf16[256,512]{1,0:T(8,128)(2,1)S(1)} %join.1.refs_1_), channel_id=1, source_target_pairs={{0,16},{8,56},{16,32},{24,8},{32,48},{40,24},{48,0},{56,40},{64,80... | collective-permute-start | bytes 786440 | tf_op jit(solution)/shard_map/ppermute | solution.py:31
  25.5 14.9 %collective-permute-start.17 = (bf16[512,512]{1,0:T(8,128)(2,1)S(1)}, bf16[512,512]{1,0:T(8,128)(2,1)S(1)}, u32[]{:S(2)}, u32[]{:S(2)}) collective-permute-start(bf16[512,512]{1,0:T(8,128)(2,1)S(1)} %pad_maximum_fusion.1), channel_id=1, source_target_pairs={{0,16},{8,56},{16,32},{24,8},{32,48},{40,24},{48,0},{56,40},{64,80... | collective-permute-start | bytes 1572872 | tf_op jit(solution)/shard_map/ppermute | solution.py:31
  27.3 11.3 %collective-permute-start.13 = (bf16[256,512]{1,0:T(8,128)(2,1)S(1)}, bf16[256,512]{1,0:T(8,128)(2,1)S(1)}, u32[]{:S(2)}, u32[]{:S(2)}) collective-permute-start(bf16[256,512]{1,0:T(8,128)(2,1)S(1)} %collective-permute-done.10.refs_3_), channel_id=1, source_target_pairs={{0,16},{8,56},{16,32},{24,8},{32,48},{40,24},{48,0},{56,40},{64,80... | collective-permute-start | bytes 786440 | tf_op jit(solution)/shard_map/ppermute | solution.py:31
  28.6 10.1 %collective-permute-start.14 = (bf16[256,512]{1,0:T(8,128)(2,1)S(1)}, bf16[256,512]{1,0:T(8,128)(2,1)S(1)}, u32[]{:S(2)}, u32[]{:S(2)}) collective-permute-start(bf16[256,512]{1,0:T(8,128)(2,1)S(1)} %join.1.refs_1_), channel_id=1, source_target_pairs={{0,64},{8,72},{16,80},{24,88},{32,96},{40,104},{48,112},{56,120},{... | collective-permute-start | bytes 786440 | tf_op jit(solution)/shard_map/ppermute | solution.py:39
  30.4 10.1 %collective-permute-start.16 = (bf16[256,512]{1,0:T(8,128)(2,1)S(1)}, bf16[256,512]{1,0:T(8,128)(2,1)S(1)}, u32[]{:S(2)}, u32[]{:S(2)}) collective-permute-start(bf16[256,512]{1,0:T(8,128)(2,1)S(1)} %collective-permute-done.15.refs_7_), channel_id=1, source_target_pairs={{0,16},{8,56},{16,32},{24,8},{32,48},{40,24},{48,0},{56,40},{64,80... | collective-permute-start | bytes 786440 | tf_op jit(solution)/shard_map/ppermute | solution.py:31
  40.5 3.3 %collective-permute-start.21 = (bf16[256,512]{1,0:T(8,128)(2,1)S(1)}, bf16[256,512]{1,0:T(8,128)(2,1)S(1)}, u32[]{:S(2)}, u32[]{:S(2)}) collective-permute-start(bf16[256,512]{1,0:T(8,128)(2,1)S(1)} %collective-permute-done.14.refs_12_), channel_id=1, source_target_pairs={{0,8},{8,0},{16,24},{24,16},{32,40},{40,32},{48,56},{56,48},{64,72... | collective-permute-start | bytes 786440 | tf_op jit(solution)/shard_map/ppermute | solution.py:35
  42.6 5.1 %collective-permute-start.19 = (bf16[512,512]{1,0:T(8,128)(2,1)S(1)}, bf16[512,512]{1,0:T(8,128)(2,1)S(1)}, u32[]{:S(2)}, u32[]{:S(2)}) collective-permute-start(bf16[512,512]{1,0:T(8,128)(2,1)S(1)} %collective-permute-done.17.refs_4_.refs_2_), channel_id=1, source_target_pairs={{0,8},{8,0},{16,24},{24,16},{32,40},{40,32},{48,56},{56,48},{64,72... | collective-permute-start | bytes 1572872 | tf_op jit(solution)/shard_map/ppermute | solution.py:35
  42.7 3.2 %collective-permute-start.18 = (bf16[256,512]{1,0:T(8,128)(2,1)S(1)}, bf16[256,512]{1,0:T(8,128)(2,1)S(1)}, u32[]{:S(2)}, u32[]{:S(2)}) collective-permute-start(bf16[256,512]{1,0:T(8,128)(2,1)S(1)} %collective-permute-done.9.refs_0_), channel_id=1, source_target_pairs={{0,8},{8,0},{16,24},{24,16},{32,40},{40,32},{48,56},{56,48},{64,72... | collective-permute-start | bytes 786440 | tf_op jit(solution)/shard_map/ppermute | solution.py:35
  43.3 5.0 %collective-permute-start.20 = (bf16[512,512]{1,0:T(8,128)(2,1)S(1)}, bf16[512,512]{1,0:T(8,128)(2,1)S(1)}, u32[]{:S(2)}, u32[]{:S(2)}) collective-permute-start(bf16[512,512]{1,0:T(8,128)(2,1)S(1)} %pad_maximum_fusion.2), channel_id=1, source_target_pairs={{0,8},{8,0},{16,24},{24,16},{32,40},{40,32},{48,56},{56,48},{64,72... | collective-permute-start | bytes 1572872 | tf_op jit(solution)/shard_map/ppermute | solution.py:35
  43.8 11.2 %collective-permute-start.23 = (bf16[512,512]{1,0:T(8,128)(2,1)S(1)}, bf16[512,512]{1,0:T(8,128)(2,1)S(1)}, u32[]{:S(2)}, u32[]{:S(2)}) collective-permute-start(bf16[512,512]{1,0:T(8,128)(2,1)S(1)} %pad_maximum_fusion.3), channel_id=1, source_target_pairs={{0,16},{8,56},{16,32},{24,8},{32,48},{40,24},{48,0},{56,40},{64,80... | collective-permute-start | bytes 1572872 | tf_op jit(solution)/shard_map/ppermute | solution.py:31
  44.8 10.2 %collective-permute-start.24 = (bf16[256,512]{1,0:T(8,128)(2,1)S(1)}, bf16[256,512]{1,0:T(8,128)(2,1)S(1)}, u32[]{:S(2)}, u32[]{:S(2)}) collective-permute-start(bf16[256,512]{1,0:T(8,128)(2,1)S(1)} %slice.40), channel_id=1, source_target_pairs={{0,16},{8,56},{16,32},{24,8},{32,48},{40,24},{48,0},{56,40},{64,80... | collective-permute-start | bytes 786440 | tf_op jit(solution)/shard_map/ppermute | solution.py:31
  45.9 9.2 %collective-permute-start.22 = (bf16[256,512]{1,0:T(8,128)(2,1)S(1)}, bf16[256,512]{1,0:T(8,128)(2,1)S(1)}, u32[]{:S(2)}, u32[]{:S(2)}) collective-permute-start(bf16[256,512]{1,0:T(8,128)(2,1)S(1)} %collective-permute-done.16.refs_14_), channel_id=1, source_target_pairs={{0,64},{8,72},{16,80},{24,88},{32,96},{40,104},{48,112},{56,120},{... | collective-permute-start | bytes 786440 | tf_op jit(solution)/shard_map/ppermute | solution.py:39
  47.8 7.3 %collective-permute-start.25 = (bf16[256,512]{1,0:T(8,128)(2,1)S(1)}, bf16[256,512]{1,0:T(8,128)(2,1)S(1)}, u32[]{:S(2)}, u32[]{:S(2)}) collective-permute-start(bf16[256,512]{1,0:T(8,128)(2,1)S(1)} %collective-permute-done.16.refs_14_), channel_id=1, source_target_pairs={{0,8},{8,0},{16,24},{24,16},{32,40},{40,32},{48,56},{56,48},{64,72... | collective-permute-start | bytes 786440 | tf_op jit(solution)/shard_map/ppermute | solution.py:35
  48.3 11.9 %copy-start = (bf16[4,64,1024]{2,1,0:T(8,128)(2,1)S(1)}, bf16[4,64,1024]{2,1,0:T(8,128)(2,1)}, u32[]{:S(2)}) copy-start(bf16[4,64,1024]{2,1,0:T(8,128)(2,1)} %param.10) | copy-start | bytes 1572868
  48.3 11.9 %copy-start.2 = (f32[4,1024]{1,0:T(4,128)S(1)}, f32[4,1024]{1,0:T(4,128)}, u32[]{:S(2)}) copy-start(f32[4,1024]{1,0:T(4,128)} %refs_12_.1) | copy-start | bytes 49156
  48.3 11.9 %copy-start.3 = (s32[256]{0:T(256)S(1)}, s32[256]{0:T(256)}, u32[]{:S(2)}) copy-start(s32[256]{0:T(256)} %param.7) | copy-start | bytes 3076
  55.1 5.1 %collective-permute-start.27 = (bf16[512,512]{1,0:T(8,128)(2,1)S(1)}, bf16[512,512]{1,0:T(8,128)(2,1)S(1)}, u32[]{:S(2)}, u32[]{:S(2)}) collective-permute-start(bf16[512,512]{1,0:T(8,128)(2,1)S(1)} %collective-permute-done.23.refs_3_), channel_id=1, source_target_pairs={{0,8},{8,0},{16,24},{24,16},{32,40},{40,32},{48,56},{56,48},{64,72... | collective-permute-start | bytes 1572872 | tf_op jit(solution)/shard_map/ppermute | solution.py:35
  57.6 2.5 %collective-permute-start.26 = (bf16[256,512]{1,0:T(8,128)(2,1)S(1)}, bf16[256,512]{1,0:T(8,128)(2,1)S(1)}, u32[]{:S(2)}, u32[]{:S(2)}) collective-permute-start(bf16[256,512]{1,0:T(8,128)(2,1)S(1)} %collective-permute-done.22.refs_1_), channel_id=1, source_target_pairs={{0,8},{8,0},{16,24},{24,16},{32,40},{40,32},{48,56},{56,48},{64,72... | collective-permute-start | bytes 786440 | tf_op jit(solution)/shard_map/ppermute | solution.py:35
  57.7 2.5 %collective-permute-start.28 = (bf16[256,512]{1,0:T(8,128)(2,1)S(1)}, bf16[256,512]{1,0:T(8,128)(2,1)S(1)}, u32[]{:S(2)}, u32[]{:S(2)}) collective-permute-start(bf16[256,512]{1,0:T(8,128)(2,1)S(1)} %collective-permute-done.24.refs_0_), channel_id=1, source_target_pairs={{0,8},{8,0},{16,24},{24,16},{32,40},{40,32},{48,56},{56,48},{64,72... | collective-permute-start | bytes 786440 | tf_op jit(solution)/shard_map/ppermute | solution.py:35
  (1 other events, 1.0 us)
